TPU v7x, 128 devices: a whole 4x4x4 slice. The times are simulated.
128 devices in a mesh: ctx: 8 (over x, core), tp: 16 (over y, z).
Axes of the slice: x: 4, y: 4, z: 4, core: 2. Of those that a mesh axis runs over, the one named last changes fastest.
Arguments:
- features_in: bfloat16 [1024, 8192], P('ctx', 'tp'), may hold values from -6 to 6
- w_featurizer: bfloat16 [16, 512, 3, 8192], P(None, 'ctx', None, 'tp'), may hold values from -0.0625 to 0.0625
- filter_taps: bfloat16 [16, 512, 1024], P('tp', 'ctx'), may hold values from -0.1875 to 0.1875
- query_proj: bfloat16 [1024, 8192], P('ctx', 'tp'), may hold values from -6 to 6
- key_proj: bfloat16 [1024, 8192], P('ctx', 'tp'), may hold values from -6 to 6
- value_proj: bfloat16 [1024, 8192], P('ctx', 'tp'), may hold values from -6 to 6
- grad_mixed: bfloat16 [1024, 8192], P('ctx', 'tp'), may hold values from -1.1953125 to 1.1953125
Outputs:
- grad_features: bfloat16 [1024, 8192], P('ctx', 'tp')
- grad_featurizer: bfloat16 [16, 512, 3, 8192], P(None, 'ctx', None, 'tp')
- grad_taps: bfloat16 [16, 512, 1024], P('tp', 'ctx')
All inputs are finite; a program needn't handle non-finite values.
Results may differ from a plain program's by a relative error of at most 0.018.
Values may be sent and summed in bfloat16 or wider, within the bound.
No kernel may reach another device: no remote copies, remote signals or barrier semaphores. Data moves between devices by JAX's collectives and lax.ppermute only.
A program may use at most 64 MiB of HBM per device.

v0:
```python
import math

import jax
import jax.numpy as jnp
from jax import lax
from jax.sharding import PartitionSpec as P


def dft_tables(seq_len):
    size_fft = 2 * seq_len
    rows_idx = lax.broadcasted_iota(jnp.int32, (seq_len, size_fft), 0)
    cols_idx = lax.broadcasted_iota(jnp.int32, (seq_len, size_fft), 1)
    phase = rows_idx * cols_idx % size_fft
    angle = phase.astype(jnp.float32) * (2.0 * math.pi / size_fft)
    return (jnp.cos(angle), jnp.sin(angle))


def forward_dft(signal, cosines, sines):
    real_part = jnp.dot(
        signal, cosines, precision=lax.Precision.HIGHEST, preferred_element_type=jnp.float32
    )
    imag_part = -jnp.dot(
        signal, sines, precision=lax.Precision.HIGHEST, preferred_element_type=jnp.float32
    )
    return (real_part, imag_part)


def inverse_dft(real_part, imag_part, cosines, sines):
    size_fft = cosines.shape[1]
    dims = (((1,), (1,)), ((), ()))
    first = lax.dot_general(
        real_part,
        cosines,
        dims,
        precision=lax.Precision.HIGHEST,
        preferred_element_type=jnp.float32,
    )
    second = lax.dot_general(
        imag_part, sines, dims, precision=lax.Precision.HIGHEST, preferred_element_type=jnp.float32
    )
    return (first - second) * (1.0 / size_fft)


def per_device(
    features_in, w_featurizer, filter_taps, query_proj, key_proj, value_proj, grad_mixed
):
    tokens_dev, width_dev = features_in.shape
    n_ctx = lax.axis_size("ctx")
    n_tp = lax.axis_size("tp")
    sub_width = width_dev // n_ctx
    weights = w_featurizer.reshape(-1, 3, w_featurizer.shape[3])
    query, keys, values, upstream = (
        lax.all_to_all(query_proj.T, "ctx", split_axis=0, concat_axis=1, tiled=True),
        lax.all_to_all(key_proj.T, "ctx", split_axis=0, concat_axis=1, tiled=True),
        lax.all_to_all(value_proj.T, "ctx", split_axis=0, concat_axis=1, tiled=True),
        lax.all_to_all(grad_mixed.T, "ctx", split_axis=0, concat_axis=1, tiled=True),
    )
    channels, seq_len = query.shape
    taps = filter_taps.reshape(channels, seq_len).astype(jnp.float32)
    keys_f = keys.astype(jnp.float32)
    values_f = values.astype(jnp.float32)
    upstream_f = upstream.astype(jnp.float32)
    product = (keys_f * values_f).astype(jnp.bfloat16)
    grad_conv = (upstream_f * query.astype(jnp.float32)).astype(jnp.bfloat16)
    cosines, sines = dft_tables(seq_len)
    prod_re, prod_im = forward_dft(product.astype(jnp.float32), cosines, sines)
    taps_re, taps_im = forward_dft(taps, cosines, sines)
    grad_re, grad_im = forward_dft(grad_conv.astype(jnp.float32), cosines, sines)
    conv_out = inverse_dft(
        prod_re * taps_re - prod_im * taps_im, prod_re * taps_im + prod_im * taps_re, cosines, sines
    )
    grad_prod = inverse_dft(
        grad_re * taps_re + grad_im * taps_im, grad_im * taps_re - grad_re * taps_im, cosines, sines
    )
    grad_taps = inverse_dft(
        grad_re * prod_re + grad_im * prod_im, grad_im * prod_re - grad_re * prod_im, cosines, sines
    )
    grad_query = (upstream_f * conv_out).astype(jnp.bfloat16)
    grad_key = (grad_prod * values_f).astype(jnp.bfloat16)
    grad_value = (grad_prod * keys_f).astype(jnp.bfloat16)
    local_grads = jnp.stack([grad_query, grad_key, grad_value], axis=0)
    gathered = lax.all_gather(local_grads, "ctx", axis=1, tiled=True)
    whole = lax.all_gather(features_in, "tp", axis=1, tiled=True)
    regrouped = (
        whole.reshape(tokens_dev, n_tp, n_ctx, sub_width)
        .transpose(0, 2, 1, 3)
        .reshape(tokens_dev, -1)
    )
    rows = lax.all_to_all(regrouped, "ctx", split_axis=1, concat_axis=0, tiled=True)
    grad_w = jnp.einsum("tf,bct->fbc", rows, gathered, preferred_element_type=jnp.float32).astype(
        jnp.bfloat16
    )
    partial_value = jnp.einsum(
        "fbc,bct->tf", weights, gathered, preferred_element_type=jnp.float32
    ).astype(jnp.bfloat16)
    moved = lax.all_to_all(partial_value, "ctx", split_axis=0, concat_axis=1, tiled=True)
    ordered = (
        moved.reshape(tokens_dev, n_ctx, n_tp, sub_width)
        .transpose(0, 2, 1, 3)
        .reshape(tokens_dev, -1)
    )
    grad_features = lax.psum_scatter(
        ordered.astype(jnp.float32).astype(jnp.bfloat16), "tp", scatter_dimension=1, tiled=True
    )
    return (
        grad_features,
        grad_w.reshape(w_featurizer.shape),
        grad_taps.astype(jnp.bfloat16).reshape(filter_taps.shape),
    )


def solution(mesh):
    return jax.shard_map(
        per_device,
        mesh=mesh,
        in_specs=(
            P("ctx", "tp"),
            P(None, "ctx", None, "tp"),
            P("tp", "ctx", None),
            P("ctx", "tp"),
            P("ctx", "tp"),
            P("ctx", "tp"),
            P("ctx", "tp"),
        ),
        out_specs=(P("ctx", "tp"), P(None, "ctx", None, "tp"), P("tp", "ctx", None)),
        check_vma=False,
    )
```

profile of v0, /device:TPU:1, one launch (start us, length us, event | category | flops | bytes accessed | tf_op | source)
XLA Modules:
  0.0 589.9 jit_solution(11558677745971134532)
XLA Ops:
  7.2 0.0 copy-start
  7.2 1.7 copy.17
  8.9 5.8 all-to-all-start
  14.7 0.0 copy-done
  14.7 35.3 %fusion.32 = f32[64,2048]{1,0:T(8,128)S(1)} fusion(bf16[1,64,1024]{2,1,0:T(8,128)(2,1)S(1)} %copy-done), kind=kOutput, calls=%fused_computation.25 | convolution fusion | flops 1639972864 | bytes 655360 | tf_op jit(solution)/shard_map/dot_general | solution.py:22
  49.9 0.0 copy-done.2
  50.0 0.0 copy-start.14
  50.0 0.8 copy.23
  50.8 0.0 all-to-all-done
  50.8 4.8 all-to-all-start.3
  55.6 35.0 %fusion.35 = f32[64,2048]{1,0:T(8,128)S(1)} fusion(bf16[1,64,1024]{2,1,0:T(8,128)(2,1)S(1)} %copy-done), kind=kOutput, calls=%fused_computation.26 | convolution fusion | flops 1639972864 | bytes 655360 | tf_op jit(solution)/shard_map/dot_general | solution.py:19
  90.6 0.0 copy-done.3
  90.6 0.0 copy-start.15
  90.6 0.8 copy.19
  91.4 0.0 copy-done.4
  91.4 0.8 copy.21
  92.2 0.0 all-to-all-done.3
  92.2 5.1 all-to-all-start.1
  97.3 35.3 %fusion.24 = f32[64,2048]{1,0:T(8,128)S(1)} fusion(bf16[64,1024]{1,0:T(8,128)(2,1)S(1)} %fusion.95), kind=kOutput, calls=%fused_computation.20 | convolution fusion | flops 1639972864 | bytes 655360 | tf_op jit(solution)/shard_map/dot_general | solution.py:22
  132.6 0.0 copy-start.6
  132.6 35.0 %fusion.12 = f32[64,2048]{1,0:T(8,128)S(1)} fusion(bf16[64,1024]{1,0:T(8,128)(2,1)S(1)} %fusion.95), kind=kOutput, calls=%fused_computation.14 | convolution fusion | flops 1639972864 | bytes 655360 | tf_op jit(solution)/shard_map/dot_general | solution.py:19
  167.6 0.0 copy-start.8
  167.6 0.0 all-to-all-done.1
  167.6 4.8 all-to-all-start.2
  172.5 0.5 all-gather.3.cloned.1.call-start
  173.0 38.4 %fusion.10 = f32[64,1024]{1,0:T(8,128)S(1)} fusion(f32[64,2048]{1,0:T(8,128)S(1)} %fusion.24, f32[64,2048]{1,0:T(8,128)S(1)} %fusion.32, f32[64,2048]{1,0:T(8,128)S(1)} %fusion.12, f32[64,2048]{1,0:T(8,128)S(1)} %fusion.35), kind=kOutput, calls=%fused_computation.13 | convolution fusion | flops 1640366080 | bytes 2359296 | tf_op jit(solution)/shard_map/dot_general | solution.py:31
  211.4 0.0 all-to-all-done.2
  211.4 0.0 copy-done.6
  211.4 0.0 copy-done.8
  211.5 38.9 %fusion.96 = (bf16[64,1024]{1,0:T(8,128)(2,1)S(1)}, bf16[1,64,1024]{2,1,0:T(8,128)(2,1)S(1)}, bf16[1,64,1024]{2,1,0:T(8,128)(2,1)S(1)}) fusion(f32[64,1024]{1,0:T(8,128)S(1)} %fusion.10, f32[64,2048]{1,0:T(8,128)S(1)} %fusion.12, f32[64,2048]{1,0:T(8,128)S(1)} %fusion.35, f32[64,2048]{1,0:T(8,128)S(1)} %fusion.24, f32[64,2048]{1,0:T(8,128)S(1)} %fusion.32, ...), kind=kOutput, calls=%fused_computation.67 | convolution fusion | flops 1641283584 | bytes 3014656 | tf_op jit(solution)/shard_map/dot_general | solution.py:38
  250.3 35.4 %fusion.30 = f32[64,2048]{1,0:T(8,128)S(1)} fusion(bf16[64,1024]{1,0:T(8,128)(2,1)S(1)} %get-tuple-element.9), kind=kOutput, calls=%fused_computation.23 | convolution fusion | flops 1639972864 | bytes 655360 | tf_op jit(solution)/shard_map/dot_general | solution.py:22
  285.8 0.0 copy-start.10
  285.8 35.0 %fusion.18 = f32[64,2048]{1,0:T(8,128)S(1)} fusion(bf16[64,1024]{1,0:T(8,128)(2,1)S(1)} %get-tuple-element.9), kind=kOutput, calls=%fused_computation.17 | convolution fusion | flops 1639972864 | bytes 655360 | tf_op jit(solution)/shard_map/dot_general | solution.py:19
  320.8 0.0 copy-done.14
  320.8 0.0 copy-done.15
  320.8 0.0 copy-start.12
  320.8 38.6 %fusion.14 = f32[64,1024]{1,0:T(8,128)S(1)} fusion(f32[64,2048]{1,0:T(8,128)S(1)} %fusion.30, f32[64,2048]{1,0:T(8,128)S(1)} %fusion.32, f32[64,2048]{1,0:T(8,128)S(1)} %fusion.18, f32[64,2048]{1,0:T(8,128)S(1)} %fusion.35), kind=kOutput, calls=%fused_computation.15 | convolution fusion | flops 1640366080 | bytes 2359296 | tf_op jit(solution)/shard_map/dot_general | solution.py:31
  359.5 0.0 copy-start.5
  359.5 0.0 copy-start.1
  359.5 39.9 %fusion.68 = bf16[1,64,1024]{2,1,0:T(8,128)(2,1)S(1)} fusion(f32[64,1024]{1,0:T(8,128)S(1)} %fusion.14, f32[64,2048]{1,0:T(8,128)} %copy-done.15, f32[64,2048]{1,0:T(8,128)S(1)} %fusion.18, f32[64,2048]{1,0:T(8,128)S(1)} %fusion.30, f32[64,2048]{1,0:T(8,128)} %copy-done.14, bf16[8,64,128]{2,1,0:T(8,128)(2,1)S(1)} %all-to-all-done), kind=kOutput, calls=%fused_computation.37 | convolution fusion | flops 1640955904 | bytes 2621440 | tf_op jit(solution)/shard_map/dot_general | solution.py:38
  399.4 0.8 pad_maximum_fusion
  400.2 0.0 all-gather.3.cloned.1.call-update
  400.2 0.0 all-gather.5.cloned.1.call-start
  400.3 0.8 copy.28
  401.0 0.0 all-gather.5.cloned.1.call-update
  401.1 0.0 reduce-scatter.2.cloned.1.call-start
  401.1 1.9 copy.25
  403.0 27.7 %all-gather.3.cloned.1.call-done = bf16[3,512,1024]{2,1,0:T(8,128)(2,1)} async-done(((bf16[3,64,1024]{2,1,0:T(8,128)(2,1)}), bf16[3,512,1024]{2,1,0:T(8,128)(2,1)}) %all-gather.3.cloned.1.call-update) | async-done | bytes 3145744 | tf_op jit(solution)/shard_map/all_gather | solution.py:82
  430.7 7.7 %bitcast_convert_fusion = bf16[1024,1024]{1,0:T(8,128)(2,1)} fusion(bf16[3,512,1024]{2,1,0:T(8,128)(2,1)} %all-gather.3.cloned.1.call-done, bf16[1024,3,512]{2,0,1:T(8,128)(2,1)} %bitcast.103), kind=kOutput, calls=%fused_computation.9 | convolution fusion | flops 3222274048 | bytes 8388608 | tf_op jit(solution)/shard_map/fbc,bct->tf/dot_general | solution.py:93
  438.4 3.0 copy.26
  441.4 29.6 %all_to_all.87 = bf16[8,128,1024]{1,2,0:T(8,128)(2,1)S(1)} all-to-all(bf16[8,128,1024]{1,2,0:T(8,128)(2,1)S(1)} %copy.26), channel_id=1, replica_groups=mesh['ctx'=8,'tp'=16] {'ctx'}, dimensions={0} | all-to-all | bytes 4194304 | tf_op jit(solution)/shard_map/all_to_all | solution.py:96
  471.0 1.5 copy.27
  472.5 0.0 reduce-scatter.2.cloned.1.call-update
  472.5 4.8 all-gather.5.cloned.1.call-done
  477.3 3.1 copy.29
  480.5 6.5 %all-to-all-start.5 = ((bf16[128,8,1024]{0,2,1:T(8,128)(2,1)}), bf16[128,8,1024]{0,2,1:T(8,128)(2,1)S(1)}, u32[]{:S(2)}, u32[]{:S(2)}) async-start(bf16[128,8,1024]{0,2,1:T(8,128)(2,1)} %bitcast.101), calls=%async_computation.6 | async-start | bytes 4194304 | tf_op jit(solution)/shard_map/all_to_all | solution.py:89
  487.1 39.4 %fusion.8 = f32[64,1024]{1,0:T(8,128)S(1)} fusion(f32[64,2048]{1,0:T(8,128)S(1)} %copy-done.7, f32[64,2048]{1,0:T(8,128)} %copy-done.10, f32[64,2048]{1,0:T(8,128)S(1)} %copy-done.9, f32[64,2048]{1,0:T(8,128)} %copy-done.12), kind=kOutput, calls=%fused_computation.12 | convolution fusion | flops 1640366080 | bytes 2359296 | tf_op jit(solution)/shard_map/dot_general | solution.py:31
  526.6 39.5 %fusion.65 = bf16[1,64,1024]{2,1,0:T(8,128)(2,1)} fusion(f32[64,1024]{1,0:T(8,128)S(1)} %fusion.8, f32[64,2048]{1,0:T(8,128)S(1)} %copy-done.9, f32[64,2048]{1,0:T(8,128)S(1)} %copy-done.13, f32[64,2048]{1,0:T(8,128)S(1)} %copy-done.7, f32[64,2048]{1,0:T(8,128)S(1)} %copy-done.11), kind=kOutput, calls=%fused_computation.36 | convolution fusion | flops 1640824832 | bytes 2490368 | tf_op jit(solution)/shard_map/dot_general | solution.py:38
  566.0 0.0 all-to-all-done.5
  566.0 2.7 copy.30
  568.8 7.6 %convert_bitcast_fusion = bf16[1024,3,512]{0,2,1:T(8,128)(2,1)} fusion(bf16[3,512,1024]{2,1,0:T(8,128)(2,1)} %all-gather.3.cloned.1.call-done, bf16[1024,1024,1]{1,0,2:T(8,128)(2,1)} %bitcast.105), kind=kOutput, calls=%fused_computation.24 | convolution fusion | flops 3222798336 | bytes 8388608 | tf_op jit(solution)/shard_map/tf,bct->fbc/dot_general | solution.py:90
  576.4 3.2 copy.31
  579.6 1.9 copy.33
  581.5 1.7 copy.32
  (17 shorter events, 0.1 us)
Async XLA Ops:
  7.2 7.5 %copy-start = (bf16[1,64,1024]{2,1,0:T(8,128)(2,1)S(1)}, bf16[1,64,1024]{2,1,0:T(8,128)(2,1)}, u32[]{:S(2)}) copy-start(bf16[1,64,1024]{2,1,0:T(8,128)(2,1)} %param.9) | copy-start | bytes 393220
  8.9 41.9 %all-to-all-start = ((bf16[8,64,128]{2,1,0:T(8,128)(2,1)}), bf16[8,64,128]{2,1,0:T(8,128)(2,1)S(1)}, u32[]{:S(2)}, u32[]{:S(2)}) async-start(bf16[8,64,128]{2,1,0:T(8,128)(2,1)} %bitcast.1), calls=%async_computation | async-start | bytes 262144 | tf_op jit(solution)/shard_map/all_to_all | solution.py:56
  14.7 35.3 %copy-start.2 = (bf16[128,512]{1,0:T(8,128)(2,1)S(1)}, bf16[128,512]{1,0:T(8,128)(2,1)}, u32[]{:S(2)}) copy-start(bf16[128,512]{1,0:T(8,128)(2,1)} %param.10) | copy-start | bytes 393220
  50.0 270.8 %copy-start.14 = (f32[64,2048]{1,0:T(8,128)}, f32[64,2048]{1,0:T(8,128)S(1)}, u32[]{:S(2)}) copy-start(f32[64,2048]{1,0:T(8,128)S(1)} %fusion.32) | copy-start | bytes 1572868
  50.8 41.4 %all-to-all-start.3 = ((bf16[8,64,128]{2,1,0:T(8,128)(2,1)}), bf16[8,64,128]{2,1,0:T(8,128)(2,1)S(1)}, u32[]{:S(2)}, u32[]{:S(2)}) async-start(bf16[8,64,128]{2,1,0:T(8,128)(2,1)} %bitcast.14), calls=%async_computation.3 | async-start | bytes 262144 | tf_op jit(solution)/shard_map/all_to_all | solution.py:53
  55.6 35.0 %copy-start.3 = (bf16[128,512]{1,0:T(8,128)(2,1)S(1)}, bf16[128,512]{1,0:T(8,128)(2,1)}, u32[]{:S(2)}) copy-start(bf16[128,512]{1,0:T(8,128)(2,1)} %param.11) | copy-start | bytes 393220
  55.6 35.8 %copy-start.4 = (bf16[128,512]{1,0:T(8,128)(2,1)S(1)}, bf16[128,512]{1,0:T(8,128)(2,1)}, u32[]{:S(2)}) copy-start(bf16[128,512]{1,0:T(8,128)(2,1)} %param.12) | copy-start | bytes 393220
  90.6 230.2 %copy-start.15 = (f32[64,2048]{1,0:T(8,128)}, f32[64,2048]{1,0:T(8,128)S(1)}, u32[]{:S(2)}) copy-start(f32[64,2048]{1,0:T(8,128)S(1)} %fusion.35) | copy-start | bytes 1572868
  92.2 75.5 %all-to-all-start.1 = ((bf16[8,64,128]{2,1,0:T(8,128)(2,1)}), bf16[8,64,128]{2,1,0:T(8,128)(2,1)S(1)}, u32[]{:S(2)}, u32[]{:S(2)}) async-start(bf16[8,64,128]{2,1,0:T(8,128)(2,1)} %bitcast.4), calls=%async_computation.1 | async-start | bytes 262144 | tf_op jit(solution)/shard_map/all_to_all | solution.py:54
  132.6 78.8 %copy-start.6 = (f32[64,2048]{1,0:T(8,128)}, f32[64,2048]{1,0:T(8,128)S(1)}, u32[]{:S(2)}) copy-start(f32[64,2048]{1,0:T(8,128)S(1)} %fusion.24) | copy-start | bytes 1572868
  167.6 43.8 %copy-start.8 = (f32[64,2048]{1,0:T(8,128)}, f32[64,2048]{1,0:T(8,128)S(1)}, u32[]{:S(2)}) copy-start(f32[64,2048]{1,0:T(8,128)S(1)} %fusion.12) | copy-start | bytes 1572868
  167.6 43.8 %all-to-all-start.2 = ((bf16[8,64,128]{2,1,0:T(8,128)(2,1)}), bf16[8,64,128]{2,1,0:T(8,128)(2,1)S(1)}, u32[]{:S(2)}, u32[]{:S(2)}) async-start(bf16[8,64,128]{2,1,0:T(8,128)(2,1)} %bitcast.7), calls=%async_computation.2 | async-start | bytes 262144 | tf_op jit(solution)/shard_map/all_to_all | solution.py:55
  172.5 258.3 %all-gather.3.cloned.1.call-start = ((), (), s32[]{:S(2)}) async-start(), calls=%async_computation.7 | async-start | bytes 3538944 | tf_op jit(solution)/shard_map/all_gather | solution.py:82
  285.8 73.7 %copy-start.10 = (f32[64,2048]{1,0:T(8,128)}, f32[64,2048]{1,0:T(8,128)S(1)}, u32[]{:S(2)}) copy-start(f32[64,2048]{1,0:T(8,128)S(1)} %fusion.30) | copy-start | bytes 1572868
  320.8 38.7 %copy-start.12 = (f32[64,2048]{1,0:T(8,128)}, f32[64,2048]{1,0:T(8,128)S(1)}, u32[]{:S(2)}) copy-start(f32[64,2048]{1,0:T(8,128)S(1)} %fusion.18) | copy-start | bytes 1572868
  359.5 40.8 %copy-start.5 = (bf16[128,512]{1,0:T(8,128)(2,1)S(1)}, bf16[128,512]{1,0:T(8,128)(2,1)}, u32[]{:S(2)}) copy-start(bf16[128,512]{1,0:T(8,128)(2,1)} %param.7) | copy-start | bytes 393220
  359.5 41.6 %copy-start.1 = (bf16[16,64,3,512]{3,1,2,0:T(8,128)(2,1)S(1)}, bf16[16,64,3,512]{3,1,2,0:T(8,128)(2,1)}, u32[]{:S(2)}) copy-start(bf16[16,64,3,512]{3,1,2,0:T(8,128)(2,1)} %param.8) | copy-start | bytes 9437188
  400.2 77.1 %all-gather.5.cloned.1.call-start = ((), (), s32[]{:S(2)}) async-start(), calls=%async_computation.9 | async-start | bytes 2228224 | tf_op jit(solution)/shard_map/all_gather | solution.py:83
  401.1 180.5 %reduce-scatter.2.cloned.1.call-start = ((), (), s32[]{:S(2)}) async-start(), calls=%async_computation.8 | async-start | bytes 2228224 | tf_op jit(solution)/shard_map/reduce_scatter | solution.py:102
  480.5 6.6 %copy-start.7 = (f32[64,2048]{1,0:T(8,128)S(1)}, f32[64,2048]{1,0:T(8,128)}, u32[]{:S(2)}) copy-start(f32[64,2048]{1,0:T(8,128)} %copy-done.6) | copy-start | bytes 1572868
  480.5 6.6 %copy-start.9 = (f32[64,2048]{1,0:T(8,128)S(1)}, f32[64,2048]{1,0:T(8,128)}, u32[]{:S(2)}) copy-start(f32[64,2048]{1,0:T(8,128)} %copy-done.8) | copy-start | bytes 1572868
  480.5 85.5 %all-to-all-start.5 = ((bf16[128,8,1024]{0,2,1:T(8,128)(2,1)}), bf16[128,8,1024]{0,2,1:T(8,128)(2,1)S(1)}, u32[]{:S(2)}, u32[]{:S(2)}) async-start(bf16[128,8,1024]{0,2,1:T(8,128)(2,1)} %bitcast.101), calls=%async_computation.6 | async-start | bytes 4194304 | tf_op jit(solution)/shard_map/all_to_all | solution.py:89
  487.1 39.5 %copy-start.11 = (f32[64,2048]{1,0:T(8,128)S(1)}, f32[64,2048]{1,0:T(8,128)}, u32[]{:S(2)}) copy-start(f32[64,2048]{1,0:T(8,128)} %copy-done.10) | copy-start | bytes 1572868
  487.1 39.5 %copy-start.13 = (f32[64,2048]{1,0:T(8,128)S(1)}, f32[64,2048]{1,0:T(8,128)}, u32[]{:S(2)}) copy-start(f32[64,2048]{1,0:T(8,128)} %copy-done.12) | copy-start | bytes 1572868
Sparse Core Ops, SparseCore 0:
  400.3 30.3 all-gather.2
  433.4 43.8 all-gather.4
  480.6 73.2 reduce-scatter.1
where the time goes:
time: 598 us; the launch traced here: 590 us
  matrix products  461 us (77%)
  waiting for transfers between devices  32.6 us (5%)
  blocking collectives  29.6 us (5%)
  starting transfers between devices  27.7 us (5%)
  local copies, waits for them, and re-layouts  24 us (4%)
  between operations  14.3 us (2%)
    dot_general x3, matrix products, inverse_dft(): lax.dot_general(imag_part, sines, dims, precision=lax.Precision.HIGHEST,...  118 us
    dot_general x3, matrix products, inverse_dft(): lax.dot_general(real_part, cosines, dims, precision=lax.Precision.HIGHEST...  117 us
    dot_general x3, matrix products, forward_dft(): jnp.dot(signal, sines, precision=lax.Precision.HIGHEST, preferred_element...  106 us
    dot_general x3, matrix products, forward_dft(): jnp.dot(signal, cosines, precision=lax.Precision.HIGHEST, preferred_eleme...  105 us
    all_to_all x1, blocking collectives, per_device(): lax.all_to_all(partial_value, 'ctx', split_axis=0, concat_axis=1, tiled=T...  29.6 us
    all_gather x1, waiting for transfers between devices, per_device(): gathered = lax.all_gather(local_grads, 'ctx', axis=1, tiled=True)  27.7 us
  transfers between devices with their start and end apart: 8, of which 2 were waited for; matrix products, arithmetic and copies ran while one was open for 50% of the time, Pallas kernels for 0%

commit v1 on v0

v1 whole, which is shorter than its diff:
```python
import math

import jax
import jax.numpy as jnp
import numpy as np
from jax import lax
from jax.experimental import pallas as pl
from jax.experimental.pallas import tpu as pltpu
from jax.sharding import PartitionSpec as P

BF16 = jnp.bfloat16
F32 = jnp.float32


def tables(n):
    idx = np.arange(n, dtype=np.int64)
    angle = (np.outer(idx, idx) % (2 * n)).astype(np.float64) * (math.pi / n)
    out = []
    for whole in (np.cos(angle), np.sin(angle)):
        high = whole.astype(BF16)
        out.append(high)
        out.append((whole - high.astype(np.float64)).astype(BF16))
    return out


def dot(a, b):
    return lax.dot_general(a, b, (((1,), (0,)), ((), ())), preferred_element_type=F32)


def conv_kernel(recv, taps, cos_hi, cos_lo, sin_hi, sin_lo, grads, grad_taps):
    n_src, _, chans, span = recv.shape
    n = n_src * span

    def whole(which):
        return jnp.concatenate([recv[s, which] for s in range(n_src)], axis=1)

    keys = whole(0).astype(F32)
    values = whole(1).astype(F32)
    upstream = whole(2).astype(F32)
    query = whole(3).astype(F32)
    product = (keys * values).astype(BF16)
    grad_conv = (upstream * query).astype(BF16)
    signals = jnp.concatenate([product, grad_conv, taps[...]], axis=0)
    lane = lax.broadcasted_iota(jnp.int32, (1, n), 1)
    sign = jnp.where(lane % 2 == 0, 1.0, -1.0).astype(F32)
    nyq = jnp.sum(signals.astype(F32) * sign, axis=1, keepdims=True)
    re = dot(signals, cos_hi[...]) + dot(signals, cos_lo[...])
    im = dot(signals, sin_hi[...]) + dot(signals, sin_lo[...])
    ur, gr, hr = re[:chans], re[chans : 2 * chans], re[2 * chans :]
    ui, gi, hi = im[:chans], im[chans : 2 * chans], im[2 * chans :]
    un, gn, hn = nyq[:chans], nyq[chans : 2 * chans], nyq[2 * chans :]
    weight = jnp.where(lane == 0, 0.5 / n, 1.0 / n).astype(F32)
    spec_re = jnp.concatenate([ur * hr - ui * hi, gr * hr + gi * hi, gr * ur + gi * ui], axis=0) * weight
    spec_im = jnp.concatenate([ur * hi + ui * hr, gi * hr - gr * hi, gi * ur - gr * ui], axis=0) * weight
    spec_n = jnp.concatenate([un * hn, gn * hn, gn * un], axis=0) * (0.5 / n)
    re_hi = spec_re.astype(BF16)
    re_lo = (spec_re - re_hi.astype(F32)).astype(BF16)
    im_hi = spec_im.astype(BF16)
    im_lo = (spec_im - im_hi.astype(F32)).astype(BF16)
    out = (
        dot(re_hi, cos_hi[...])
        + dot(im_hi, sin_hi[...])
        + dot(re_lo, cos_hi[...])
        + dot(im_lo, sin_hi[...])
        + dot(re_hi, cos_lo[...])
        + dot(im_hi, sin_lo[...])
        + spec_n * sign
    )
    grads[0] = (upstream * out[:chans]).astype(BF16)
    grads[1] = (out[chans : 2 * chans] * values).astype(BF16)
    grads[2] = (out[chans : 2 * chans] * keys).astype(BF16)
    grad_taps[...] = out[2 * chans :].astype(BF16)


def convolutions(recv, taps):
    n_src, _, chans, span = recv.shape
    n = n_src * span
    return pl.pallas_call(
        conv_kernel,
        out_shape=(
            jax.ShapeDtypeStruct((3, chans, n), BF16),
            jax.ShapeDtypeStruct((chans, n), BF16),
        ),
        compiler_params=pltpu.CompilerParams(vmem_limit_bytes=48 * 1024 * 1024),
        name="convolutions",
    )(recv, taps, *[jnp.asarray(t) for t in tables(n)])


def per_device(features_in, w_featurizer, filter_taps, query_proj, key_proj, value_proj, grad_mixed):
    tokens_dev, width_dev = features_in.shape
    n_ctx = lax.axis_size("ctx")
    n_tp = lax.axis_size("tp")
    sub = width_dev // n_ctx
    seq_len = tokens_dev * n_ctx
    sent = jnp.stack(
        [a.T.reshape(n_ctx, sub, tokens_dev) for a in (key_proj, value_proj, grad_mixed, query_proj)], axis=1
    )
    recv = lax.all_to_all(sent, "ctx", 0, 0)
    feats = lax.all_to_all(features_in.T.reshape(n_ctx, sub, tokens_dev), "ctx", 0, 0)
    feats = feats.transpose(1, 0, 2).reshape(sub, seq_len)
    feats = lax.all_gather(feats, "tp", axis=0, tiled=True)
    grads, grad_taps = convolutions(recv, filter_taps.reshape(sub, seq_len))
    gathered = lax.all_gather(grads, "ctx", axis=0)
    weights = (
        w_featurizer.reshape(n_tp * sub, 3, n_ctx, sub).transpose(0, 2, 1, 3).reshape(n_tp * sub, 3 * width_dev)
    )
    part = dot(weights, gathered.reshape(3 * width_dev, seq_len)).astype(BF16)
    parts = lax.all_to_all(part.reshape(n_tp, sub, seq_len), "tp", 0, 0)
    total = jnp.sum(parts.astype(F32), axis=0).astype(BF16)
    total = total.reshape(sub, n_ctx, tokens_dev).transpose(1, 0, 2)
    moved = lax.all_to_all(total, "ctx", 0, 0)
    grad_features = moved.reshape(width_dev, tokens_dev).T
    ordered = gathered.transpose(1, 0, 2, 3).reshape(3 * width_dev, seq_len)
    grad_w = lax.dot_general(feats, ordered, (((1,), (1,)), ((), ())), preferred_element_type=F32).astype(BF16)
    return grad_features, grad_w.reshape(w_featurizer.shape), grad_taps.reshape(filter_taps.shape)


def solution(mesh):
    return jax.shard_map(
        per_device,
        mesh=mesh,
        in_specs=(
            P("ctx", "tp"),
            P(None, "ctx", None, "tp"),
            P("tp", "ctx", None),
            P("ctx", "tp"),
            P("ctx", "tp"),
            P("ctx", "tp"),
            P("ctx", "tp"),
        ),
        out_specs=(P("ctx", "tp"), P(None, "ctx", None, "tp"), P("tp", "ctx", None)),
        check_vma=False,
    )
```

time: 598 us -> 156 us (0.26); the launches traced: 590 us -> 155 us
  matrix products: 461 us -> 14.7 us
  waiting for transfers between devices: 32.6 us -> 48.3 us
  starting transfers between devices: 27.7 us -> 12.1 us
  local copies, waits for them, and re-layouts: 24 us -> 33.6 us
  Pallas kernels: 0 us -> 7.59 us
    dot_general x14 -> x2, matrix products: 461 us -> 14.7 us  [the longest x1 8.68 us: dot(): lax.dot_general(a, b, (((1,), (0,)), ((), ())), preferred_element_type=F32)]
    all_to_all x5 -> x2, waiting for transfers between devices: 0.01 us -> 26.1 us  [the longest x1 26.1 us: per_device(): parts = lax.all_to_all(part.reshape(n_tp, sub, seq_len), 'tp', 0, 0)]
    all_to_all x5 -> x2, starting transfers between devices: 27.1 us -> 12 us  [the longest x1 6.7 us: per_device(): parts = lax.all_to_all(part.reshape(n_tp, sub, seq_len), 'tp', 0, 0)]
    reshape x0 -> x3, local copies, waits for them, and re-layouts: none -> 12.3 us  [the longest x1 6.05 us: per_device(): grad_w.reshape(w_featurizer.shape)]
    all_gather x2, waiting for transfers between devices: 32.5 us -> 22.2 us  [the longest x1 11.7 us: per_device(): gathered = lax.all_gather(grads, 'ctx', axis=0)]
    pallas_call x0 -> x1, Pallas kernels: none -> 7.59 us  [convolutions(): pl.pallas_call(conv_kernel, out_shape=(jax.ShapeDtypeStruct((3, chans, n)...]
    all_to_all x1 -> x2, blocking collectives: 29.6 us -> 23.7 us  [the longest x1 15 us: per_device(): recv = lax.all_to_all(sent, 'ctx', 0, 0)]
    unnamed x40 -> x13, local copies, waits for them, and re-layouts: 10.4 us -> 12.4 us
  transfers between devices with their start and end apart: 8 -> 4, of which waited for: 2 -> 3; matrix products, arithmetic and copies ran while one was open for 50% -> 27% of each run, Pallas kernels for 0% -> 0%
where the time goes in v1:
time: 156 us; the launch traced here: 155 us
  waiting for transfers between devices  48.3 us (31%)
  local copies, waits for them, and re-layouts  33.6 us (22%)
  blocking collectives  23.7 us (15%)
  matrix products  14.7 us (9%)
  between operations  14.1 us (9%)
  starting transfers between devices  12.1 us (8%)
  Pallas kernels  7.59 us (5%)
    all_to_all x1, waiting for transfers between devices, per_device(): parts = lax.all_to_all(part.reshape(n_tp, sub, seq_len), 'tp', 0, 0)  26.1 us
    all_to_all x1, blocking collectives, per_device(): recv = lax.all_to_all(sent, 'ctx', 0, 0)  15 us
    unnamed x13, local copies, waits for them, and re-layouts  12.4 us
    all_gather x1, waiting for transfers between devices, per_device(): gathered = lax.all_gather(grads, 'ctx', axis=0)  11.7 us
    all_gather x1, waiting for transfers between devices, per_device(): feats = lax.all_gather(feats, 'tp', axis=0, tiled=True)  10.5 us
    all_to_all x1, blocking collectives, per_device(): lax.all_to_all(features_in.T.reshape(n_ctx, sub, tokens_dev), 'ctx', 0, 0)  8.71 us
    dot_general x1, matrix products, dot(): lax.dot_general(a, b, (((1,), (0,)), ((), ())), preferred_element_type=F32)  8.68 us
    pallas_call x1, Pallas kernels, convolutions(): pl.pallas_call(conv_kernel, out_shape=(jax.ShapeDtypeStruct((3, chans, n)...  7.59 us
  transfers between devices with their start and end apart: 4, of which 3 were waited for; matrix products, arithmetic and copies ran while one was open for 27% of the time, Pallas kernels for 0%

profile of v1, /device:TPU:1, one launch (start us, length us, event | category | flops | bytes accessed | tf_op | source)
XLA Modules:
  0.0 154.6 jit_solution(15178171367342981786)
XLA Ops:
  7.2 0.0 copy-start
  7.2 0.0 copy-start.2
  7.2 0.0 all-gather.6.cloned.1.call-start
  7.2 1.2 copy.35
  8.4 1.0 copy.34
  9.4 1.0 copy.33
  10.5 1.0 copy.32
  11.5 0.1 pad_maximum_fusion
  11.6 15.0 %all_to_all.20.recv = bf16[8,4,64,128]{3,2,1,0:T(8,128)(2,1)S(1)} all-to-all(bf16[8,4,64,128]{3,2,1,0:T(8,128)(2,1)S(1)} %pad_maximum_fusion), channel_id=1, replica_groups=mesh['ctx'=8,'tp'=16] {'ctx'}, dimensions={0} | all-to-all | bytes 1048576 | tf_op jit(solution)/shard_map/all_to_all | solution.py:98
  26.5 0.0 copy-done
  26.5 0.0 copy-done.2
  26.5 0.0 copy-start.1
  26.5 1.6 %copy-done.1 = bf16[1024,1024]{1,0:T(8,128)(2,1)S(1)} copy-done((bf16[1024,1024]{1,0:T(8,128)(2,1)S(1)}, bf16[1024,1024]{1,0:T(8,128)(2,1)}, u32[]{:S(2)}) %copy-start.1) | copy-done | bytes 2097176
  28.1 0.0 copy-start.3
  28.1 7.6 %convolutions.1 = (bf16[3,64,1024]{2,1,0:T(8,128)(2,1)}, bf16[64,1024]{1,0:T(8,128)(2,1)}) custom-call(bf16[8,4,64,128]{3,2,1,0:T(8,128)(2,1)S(1)} %all_to_all.20.recv, bf16[64,1024]{1,0:T(8,128)(2,1)S(1)} %bitcast.49, bf16[1024,1024]{1,0:T(8,128)(2,1)S(1)} %copy-done, bf16[1024,1024]{1,0:T(8,128)(2,1)S(1)} %copy-done.1, ...), custom_call_target="tpu_custom_call" | custom-call | tf_op jit(solution)/shard_map/convolutions/pallas_call | solution.py:78
  35.7 0.0 all-gather.6.cloned.1.call-update
  35.7 0.0 all-gather.4.cloned.1.call-start
  35.8 0.0 copy-done.3
  35.8 0.1 copy.40
  35.9 8.7 %all_to_all.21 = bf16[8,64,128]{2,1,0:T(8,128)(2,1)S(1)} all-to-all(bf16[8,64,128]{2,1,0:T(8,128)(2,1)S(1)} %bitcast.58), channel_id=1, replica_groups=mesh['ctx'=8,'tp'=16] {'ctx'}, dimensions={0} | all-to-all | bytes 262144 | tf_op jit(solution)/shard_map/all_to_all | solution.py:99
  44.6 0.7 copy_bitcast_fusion
  45.3 0.0 all-gather.4.cloned.1.call-update
  45.3 2.3 %copy.36 = bf16[16,64,3,512]{3,1,0,2:T(8,128)(2,1)S(1)} copy(bf16[16,64,3,512]{3,1,2,0:T(8,128)(2,1)} %param.12) | data formatting | bytes 6291456 | tf_op args[1]
  47.6 5.6 %reshape.39 = bf16[1024,3,8,64]{3,2,0,1:T(8,128)(2,1)} reshape(bf16[16,64,3,512]{3,1,0,2:T(8,128)(2,1)S(1)} %copy.36) | data formatting | bytes 6291456 | tf_op jit(solution)/shard_map/reshape | solution.py:105
  53.2 11.7 %all-gather.6.cloned.1.call-done = bf16[24,64,1024]{2,1,0:T(8,128)(2,1)} async-done(((bf16[3,64,1024]{2,1,0:T(8,128)(2,1)}), bf16[24,64,1024]{2,1,0:T(8,128)(2,1)}) %all-gather.6.cloned.1.call-update) | async-done | bytes 3145744 | tf_op jit(solution)/shard_map/all_gather | solution.py:103
  64.9 8.7 %bitcast_convert_fusion = bf16[1024,1024]{0,1:T(8,128)(2,1)} fusion(bf16[8,3,64,1024]{3,2,1,0:T(8,128)(2,1)} %bitcast.51, bf16[1024,8,3,64]{3,1,0,2:T(8,128)(2,1)} %bitcast.50), kind=kOutput, calls=%fused_computation.2 | convolution fusion | flops 3222274048 | bytes 8388608 | tf_op jit(solution)/shard_map/dot_general | solution.py:27
  73.6 6.7 %all-to-all-start.1 = ((bf16[16,64,1024]{2,1,0:T(8,128)(2,1)}), bf16[16,64,1024]{2,1,0:T(8,128)(2,1)S(1)}, u32[]{:S(2)}, u32[]{:S(2)}) async-start(bf16[16,64,1024]{2,1,0:T(8,128)(2,1)} %bitcast.54), calls=%async_computation.1 | async-start | bytes 4194304 | tf_op jit(solution)/shard_map/all_to_all | solution.py:108
  80.3 4.0 %copy.39 = bf16[3,8,64,1024]{3,2,1,0:T(8,128)(2,1)} copy(bf16[3,8,64,1024]{3,2,0,1:T(8,128)(2,1)} %bitcast.52) | data formatting | bytes 6291456 | tf_op jit(solution)/shard_map/transpose | solution.py:113
  84.4 26.1 %all-to-all-done.1 = bf16[16,64,1024]{2,1,0:T(8,128)(2,1)S(1)} async-done(((bf16[16,64,1024]{2,1,0:T(8,128)(2,1)}), bf16[16,64,1024]{2,1,0:T(8,128)(2,1)S(1)}, u32[]{:S(2)}, u32[]{:S(2)}) %all-to-all-start.1) | async-done | bytes 2097184 | tf_op jit(solution)/shard_map/all_to_all | solution.py:108
  110.4 0.4 reduce_sum.12
  110.9 0.7 copy.38
  111.5 5.3 %all-to-all-start.2 = ((bf16[8,64,128]{2,1,0:T(8,128)(2,1)}), bf16[8,64,128]{2,1,0:T(8,128)(2,1)S(1)}, u32[]{:S(2)}, u32[]{:S(2)}) async-start(bf16[8,64,128]{2,1,0:T(8,128)(2,1)} %copy.38), calls=%async_computation.2 | async-start | bytes 262144 | tf_op jit(solution)/shard_map/all_to_all | solution.py:111
  116.8 10.5 %all-gather.4.cloned.1.call-done = bf16[1024,1024]{1,0:T(8,128)(2,1)} async-done(((bf16[64,1024]{1,0:T(8,128)(2,1)}), bf16[1024,1024]{1,0:T(8,128)(2,1)}) %all-gather.4.cloned.1.call-update) | async-done | bytes 2097168 | tf_op jit(solution)/shard_map/all_gather | solution.py:101
  127.3 6.0 %fusion.2 = bf16[1024,1536]{0,1:T(8,128)(2,1)S(1)} fusion(bf16[1536,1024]{1,0:T(8,128)(2,1)} %bitcast.53, bf16[1024,1024]{1,0:T(8,128)(2,1)} %all-gather.4.cloned.1.call-done), kind=kOutput, calls=%fused_computation.4 | convolution fusion | flops 3222798336 | bytes 8388608 | tf_op jit(solution)/shard_map/dot_general | solution.py:114
  133.3 6.0 %reshape.50 = bf16[16,64,3,512]{1,0,3,2:T(8,128)(2,1)} reshape(bf16[1024,1536]{0,1:T(8,128)(2,1)S(1)} %fusion.2) | data formatting | bytes 6291456 | tf_op jit(solution)/shard_map/reshape | solution.py:115
  139.4 7.6 %copy.44 = bf16[16,64,3,512]{3,1,2,0:T(8,128)(2,1)} copy(bf16[16,64,3,512]{1,0,3,2:T(8,128)(2,1)} %reshape.50) | data formatting | bytes 6291456
  147.0 0.0 all-to-all-done.2
  147.0 0.8 copy.43
  (1 shorter events, 0.0 us)
Async XLA Ops:
  7.2 19.4 %copy-start = (bf16[1024,1024]{1,0:T(8,128)(2,1)S(1)}, bf16[1024,1024]{1,0:T(8,128)(2,1)}, u32[]{:S(2)}) copy-start(bf16[1024,1024]{1,0:T(8,128)(2,1)} %constant.11.clone.cos_hi) | copy-start | bytes 6291460
  7.2 19.4 %copy-start.2 = (bf16[1,64,1024]{2,1,0:T(8,128)(2,1)S(1)}, bf16[1,64,1024]{2,1,0:T(8,128)(2,1)}, u32[]{:S(2)}) copy-start(bf16[1,64,1024]{2,1,0:T(8,128)(2,1)} %param.13) | copy-start | bytes 393220
  7.2 57.8 %all-gather.6.cloned.1.call-start = ((), (), s32[]{:S(2)}) async-start(), calls=%async_computation.5 | async-start | bytes 3538944 | tf_op jit(solution)/shard_map/all_gather | solution.py:103
  26.5 1.6 %copy-start.1 = (bf16[1024,1024]{1,0:T(8,128)(2,1)S(1)}, bf16[1024,1024]{1,0:T(8,128)(2,1)}, u32[]{:S(2)}) copy-start(bf16[1024,1024]{1,0:T(8,128)(2,1)} %constant.12.clone.cos_lo) | copy-start | bytes 6291460
  28.1 7.7 %copy-start.3 = (bf16[128,512]{1,0:T(8,128)(2,1)S(1)}, bf16[128,512]{1,0:T(8,128)(2,1)}, u32[]{:S(2)}) copy-start(bf16[128,512]{1,0:T(8,128)(2,1)} %param.11) | copy-start | bytes 393220
  35.7 91.5 %all-gather.4.cloned.1.call-start = ((), (), s32[]{:S(2)}) async-start(), calls=%async_computation.4 | async-start | bytes 2228224 | tf_op jit(solution)/shard_map/all_gather | solution.py:101
  73.6 36.8 %all-to-all-start.1 = ((bf16[16,64,1024]{2,1,0:T(8,128)(2,1)}), bf16[16,64,1024]{2,1,0:T(8,128)(2,1)S(1)}, u32[]{:S(2)}, u32[]{:S(2)}) async-start(bf16[16,64,1024]{2,1,0:T(8,128)(2,1)} %bitcast.54), calls=%async_computation.1 | async-start | bytes 4194304 | tf_op jit(solution)/shard_map/all_to_all | solution.py:108
  111.5 35.4 %all-to-all-start.2 = ((bf16[8,64,128]{2,1,0:T(8,128)(2,1)}), bf16[8,64,128]{2,1,0:T(8,128)(2,1)S(1)}, u32[]{:S(2)}, u32[]{:S(2)}) async-start(bf16[8,64,128]{2,1,0:T(8,128)(2,1)} %copy.38), calls=%async_computation.2 | async-start | bytes 262144 | tf_op jit(solution)/shard_map/all_to_all | solution.py:111
Sparse Core Ops, SparseCore 0:
  35.9 29.0 all-gather.5
  67.1 60.1 all-gather.3

commit v2 on v1

v2 whole, which is shorter than its diff:
```python
import functools
import math

import jax
import jax.numpy as jnp
import numpy as np
from jax import lax
from jax.experimental import pallas as pl
from jax.experimental.pallas import tpu as pltpu
from jax.sharding import PartitionSpec as P

BF16 = jnp.bfloat16
F32 = jnp.float32
N_X = 4
N_CTX = 8
N_RING = 4
MIB = 1024 * 1024
ON_CHIP = pl.BlockSpec(memory_space=pltpu.VMEM)
FAR = pl.BlockSpec(memory_space=pltpu.HBM)
SCALAR = pl.BlockSpec(memory_space=pltpu.SMEM)


def vmem(mib):
    return pltpu.CompilerParams(vmem_limit_bytes=mib * MIB)


def like(*shape, dtype=BF16):
    return jax.ShapeDtypeStruct(shape, dtype)


def tables(n):
    idx = np.arange(n, dtype=np.int64)
    angle = (np.outer(idx, idx) % (2 * n)).astype(np.float64) * (math.pi / n)
    out = []
    for whole in (np.cos(angle), np.sin(angle)):
        high = whole.astype(BF16)
        out.append(high)
        out.append((whole - high.astype(np.float64)).astype(BF16))
    return [jnp.asarray(t) for t in out]


def dot(a, b):
    return lax.dot_general(a, b, (((1,), (0,)), ((), ())), preferred_element_type=F32)


def dot_t(a, b):
    return lax.dot_general(a, b, (((1,), (1,)), ((), ())), preferred_element_type=F32)


def shift_x(a, steps):
    return lax.ppermute(a, "ctx", [(i, (i + 2 * steps) % N_CTX) for i in range(N_CTX)])


def swap_core(a):
    return lax.ppermute(a, "ctx", [(i, i ^ 1) for i in range(N_CTX)])


def source(me, piece):
    back, other = piece % N_X, piece // N_X
    chip = (me // 2 + N_X - back) % N_X
    core = me % 2
    return 2 * chip + (1 - core if other else core)


def spin(a):
    pairs = [(2 * x + core, 2 * ((x + 1 - 2 * core) % N_X) + core) for x in range(N_X) for core in range(2)]
    return lax.ppermute(a, "ctx", pairs)


def gather_start(mine):
    sibling = swap_core(mine)
    return [mine, sibling, spin(mine), spin(sibling)]


def gathered_source(me, piece):
    chip, core = me // 2, me % 2
    if piece < 2:
        return 2 * chip + (core if piece == 0 else 1 - core)
    kind, theirs = (piece - 2) % 3, piece >= 5
    back = 1 - 2 * core
    if theirs:
        back, core = -back, 1 - core
    chip = (chip + N_X - (2 if kind == 2 else back)) % N_X
    return 2 * chip + (1 - core if kind == 1 else core)


def target(me, ahead, other):
    chip = (me // 2 + ahead) % N_X
    core = me % 2
    return 2 * chip + (1 - core if other else core)


def place(me, first):
    on_y, on_z = me[1] // N_RING, me[1] % N_RING
    return jnp.where((me[0] % 2 == 0) == first, on_y, on_z)


def group(me, at, k):
    return jnp.where(me[0] % 2 == 0, at * N_RING + k, k * N_RING + at)


def shift_ring(a, steps, first):
    pairs = []
    for ctx in range(N_CTX):
        for y in range(N_RING):
            for z in range(N_RING):
                along_y = (ctx % 2 == 0) == first
                to = ((y + steps) % N_RING, z) if along_y else (y, (z + steps) % N_RING)
                base = ctx * N_RING * N_RING
                pairs.append((base + y * N_RING + z, base + to[0] * N_RING + to[1]))
    return lax.ppermute(a, ("ctx", "tp"), pairs)


def part_of(index, size):
    return pl.ds(pl.multiple_of(index * size, size), size)


def prep_kernel(me, *refs):
    n_arr = len(refs) - 3 - N_X
    arrays, outs = refs[:n_arr], refs[n_arr : n_arr + N_X]
    local, turned, sems = refs[n_arr + N_X :]
    copies = [pltpu.make_async_copy(arrays[a], local.at[a], sems.at[a]) for a in range(n_arr)]
    for copy in copies:
        copy.start()
    sub = outs[0].shape[2]
    for a in range(n_arr):
        copies[a].wait()
        turned[a] = local[a].T
    for ahead in range(N_X):
        for other in range(2):
            rows = part_of(target(me[0], ahead, other), sub)
            for a in range(n_arr):
                outs[ahead][other, a] = turned[a, rows, :]


def prepare(me, arrays):
    tokens, width = arrays[0].shape
    n_arr = len(arrays)
    return pl.pallas_call(
        prep_kernel,
        out_shape=[like(2, n_arr, width // N_CTX, tokens)] * N_X,
        in_specs=[SCALAR] + [FAR] * n_arr,
        out_specs=[ON_CHIP] * N_X,
        scratch_shapes=[
            pltpu.VMEM((n_arr, tokens, width), BF16),
            pltpu.VMEM((n_arr, width, tokens), BF16),
            pltpu.SemaphoreType.DMA((n_arr,)),
        ],
        compiler_params=vmem(6),
        name="prepare",
    )(me, *[pltpu.with_memory_space_constraint(a, pltpu.HBM) for a in arrays])


def join_kernel(me, *refs):
    pieces, out = refs[:N_CTX], refs[N_CTX]
    span = pieces[0].shape[-1]
    for p in range(N_CTX):
        out[:, part_of(source(me[0], p), span)] = pieces[p][pieces[p].shape[0] - 1]


def join_features(me, pieces):
    _, sub, span = pieces[0].shape
    return pl.pallas_call(
        join_kernel,
        out_shape=like(sub, span * N_CTX),
        in_specs=[SCALAR] + [ON_CHIP] * N_CTX,
        out_specs=ON_CHIP,
        compiler_params=vmem(6),
        name="join_features",
    )(me, *pieces)


def stack_kernel(me, *refs):
    pieces, out = refs[:N_RING], refs[N_RING]
    for s in range(N_RING):
        out[pl.ds((place(me, first=False) + N_RING - s) % N_RING, 1)] = pieces[s][...][None]


def stack(me, pieces):
    return pl.pallas_call(
        stack_kernel,
        out_shape=like(N_RING, *pieces[0].shape),
        in_specs=[SCALAR] + [ON_CHIP] * N_RING,
        out_specs=ON_CHIP,
        compiler_params=vmem(6),
        name="stack_features",
    )(me, *pieces)


def signs(n):
    lane = lax.broadcasted_iota(jnp.int32, (1, n), 1)
    return jnp.where(lane % 2 == 0, 1.0, -1.0).astype(F32)


def spectrum(signals, table, n):
    nyq = jnp.sum(signals.astype(F32) * signs(n), axis=1, keepdims=True)
    re = dot(signals, table[0][...]) + dot(signals, table[1][...])
    im = dot(signals, table[2][...]) + dot(signals, table[3][...])
    return re, im, nyq


def split(a):
    high = a.astype(BF16)
    return high, (a - high.astype(F32)).astype(BF16)


def inverse(re, im, nyq, table, n):
    rows = re.shape[0]
    lane = lax.broadcasted_iota(jnp.int32, (1, n), 1)
    weight = jnp.where(lane == 0, 0.5 / n, 1.0 / n).astype(F32)
    re_hi, re_lo = split(re * weight)
    im_hi, im_lo = split(im * weight)
    both = dot(jnp.concatenate([re_hi, re_lo], axis=0), table[0][...])
    both = both + dot(jnp.concatenate([im_hi, im_lo], axis=0), table[2][...])
    low = dot(re_hi, table[1][...]) + dot(im_hi, table[3][...])
    return both[:rows] + both[rows:] + low + (nyq * (0.5 / n)) * signs(n)


def taps_kernel(*refs):
    far, taps = refs[:4], refs[4]
    table, re, im, nyq, sems = refs[5:9], refs[9], refs[10], refs[11], refs[12]
    copies = [pltpu.make_async_copy(far[i], table[i], sems.at[i]) for i in range(4)]
    for copy in copies:
        copy.start()
    for copy in copies:
        copy.wait()
    re[...], im[...], nyq[...] = spectrum(taps[...], table, taps.shape[1])


def taps_spectrum(taps):
    chans, n = taps.shape
    return pl.pallas_call(
        taps_kernel,
        out_shape=[like(n, n)] * 4 + [like(chans, n, dtype=F32)] * 2 + [like(chans, 1, dtype=F32)],
        in_specs=[FAR] * 4 + [ON_CHIP],
        out_specs=[ON_CHIP] * 7,
        scratch_shapes=[pltpu.SemaphoreType.DMA((4,))],
        compiler_params=vmem(12),
        cost_estimate=pl.CostEstimate(flops=8 * chans * n * n, bytes_accessed=8 * MIB, transcendentals=0),
        name="taps_spectrum",
    )(*[pltpu.with_memory_space_constraint(t, pltpu.HBM) for t in tables(n)], taps)


def conv_kernel(me, *refs):
    pieces = refs[:N_CTX]
    table = refs[N_CTX : N_CTX + 4]
    hr, hi, hn = refs[N_CTX + 4 : N_CTX + 7]
    grads, out_re, out_im, out_n, whole = refs[N_CTX + 7 :]
    chans, span = pieces[0].shape[-2:]
    n = N_CTX * span
    for p in range(N_CTX):
        for a in range(4):
            whole[a, :, part_of(source(me[0], p), span)] = pieces[p][a]
    product = (whole[0].astype(F32) * whole[1].astype(F32)).astype(BF16)
    grad_conv = (whole[2].astype(F32) * whole[3].astype(F32)).astype(BF16)
    re, im, nyq = spectrum(jnp.concatenate([product, grad_conv], axis=0), table, n)
    ur, gr, ui, gi, un, gn = re[:chans], re[chans:], im[:chans], im[chans:], nyq[:chans], nyq[chans:]
    hr, hi, hn = hr[...], hi[...], hn[...]
    out_re[...] = gr * ur + gi * ui
    out_im[...] = gi * ur - gr * ui
    out_n[...] = gn * un
    spec_re = jnp.concatenate([ur * hr - ui * hi, gr * hr + gi * hi], axis=0)
    spec_im = jnp.concatenate([ur * hi + ui * hr, gi * hr - gr * hi], axis=0)
    out = inverse(spec_re, spec_im, jnp.concatenate([un * hn, gn * hn], axis=0), table, n)
    grads[0] = (whole[2].astype(F32) * out[:chans]).astype(BF16)
    grads[1] = (out[chans:] * whole[1].astype(F32)).astype(BF16)
    grads[2] = (out[chans:] * whole[0].astype(F32)).astype(BF16)


def convolutions(me, pieces, table, taps_spec):
    chans, span = pieces[0].shape[-2:]
    n = N_CTX * span
    return pl.pallas_call(
        conv_kernel,
        out_shape=[like(3, chans, n)] + [like(chans, n, dtype=F32)] * 2 + [like(chans, 1, dtype=F32)],
        in_specs=[SCALAR] + [ON_CHIP] * (N_CTX + 7),
        out_specs=[ON_CHIP] * 4,
        scratch_shapes=[pltpu.VMEM((4, chans, n), BF16)],
        compiler_params=vmem(20),
        cost_estimate=pl.CostEstimate(flops=32 * chans * n * n, bytes_accessed=8 * MIB, transcendentals=0),
        name="convolutions",
    )(me, *pieces, *table, *taps_spec)


def taps_grad_kernel(*refs):
    table, (re, im, nyq), out = refs[:4], refs[4:7], refs[7]
    out[...] = inverse(re[...], im[...], nyq[...], table, out.shape[1]).astype(BF16)


def taps_grad(spec, table):
    return pl.pallas_call(
        taps_grad_kernel,
        out_shape=like(*spec[0].shape),
        in_specs=[ON_CHIP] * 7,
        out_specs=ON_CHIP,
        compiler_params=vmem(16),
        cost_estimate=pl.CostEstimate(flops=16 * MIB * 64, bytes_accessed=8 * MIB, transcendentals=0),
        name="taps_grad",
    )(*table, *spec)


def gather_pieces(mine):
    along = [mine] + [shift_x(mine, s) for s in (1, 2, 3)]
    return along + [swap_core(a) for a in along]


def assemble_kernel(which, me, *refs):
    pieces, whole = refs[: len(which)], refs[-1]
    sub = pieces[0].shape[1]
    for p, piece in zip(which, pieces, strict=True):
        for b in range(3):
            whole[part_of(b * N_CTX + gathered_source(me[0], p), sub), :] = piece[b]


def assemble(me, pieces, which):
    _, sub, n = pieces[0].shape
    return pl.pallas_call(
        functools.partial(assemble_kernel, which),
        out_shape=like(3 * N_CTX * sub, n),
        in_specs=[SCALAR] + [ON_CHIP] * len(which),
        out_specs=ON_CHIP,
        compiler_params=vmem(8),
        name="assemble",
    )(me, *pieces)


def value_kernel(steps, which, me, *refs):
    weights, held, refs = refs[0], refs[1], refs[2:]
    pieces, refs = refs[: len(which)], refs[len(which) :]
    parts = refs[: len(steps)]
    whole = held
    if which:
        whole, far_whole, sem = refs[len(steps) :]
        assemble_kernel(which, me, *pieces, whole)
        copy = pltpu.make_async_copy(whole, far_whole, sem)
        copy.start()
    for s, part in zip(steps, parts, strict=True):
        at = (place(me, first=True) + s) % N_RING
        lhs = []
        for k in range(N_RING):
            w = weights[group(me, at, k)]
            lhs.append(jnp.concatenate([w[b] for b in range(3)], axis=1))
        res = dot(jnp.concatenate(lhs, axis=0), whole[...])
        part[...] = res.astype(BF16).reshape(part.shape)
    if which:
        copy.wait()


def value_part(me, weights, whole, steps, pieces=(), which=()):
    _, _, rows, width = weights.shape
    n = whole.shape[1]
    shapes = [like(N_RING, rows, n)] * len(steps)
    specs = [ON_CHIP] * len(steps)
    if which:
        shapes += [like(*whole.shape), pltpu.HBM(whole.shape, BF16)]
        specs += [ON_CHIP, FAR]
    return pl.pallas_call(
        functools.partial(value_kernel, steps, which),
        out_shape=shapes,
        in_specs=[SCALAR] + [ON_CHIP] * (len(which) + 2),
        out_specs=specs,
        scratch_shapes=[pltpu.SemaphoreType.DMA] if which else [],
        input_output_aliases={2: len(steps)} if which else {},
        compiler_params=vmem(16),
        cost_estimate=pl.CostEstimate(
            flops=2 * len(steps) * rows * width * n, bytes_accessed=MIB // 4, transcendentals=0
        ),
        name="value_part",
    )(me, weights, whole, *pieces)


def weight_kernel(me, whole, *refs):
    feats, out, res, sems = refs[:N_RING], refs[N_RING], refs[N_RING + 1], refs[N_RING + 2]
    _, rows, n = feats[0].shape
    width = out.shape[-1]
    copies = []
    for s in range(N_RING):
        at = (place(me, first=True) + N_RING - s) % N_RING
        tall = dot_t(feats[s][...].reshape(N_RING * rows, n), whole[...]).astype(BF16)
        for k in range(N_RING):
            for b in range(3):
                res[s, k, b] = tall[k * rows : (k + 1) * rows, b * width : (b + 1) * width]
            copies.append(pltpu.make_async_copy(res.at[s, k], out.at[group(me, at, k)], sems.at[s, k]))
            copies[-1].start()
    for copy in copies:
        copy.wait()


def weight_grad(me, whole, feats):
    _, rows, n = feats[0].shape
    width = whole.shape[0] // 3
    return pl.pallas_call(
        weight_kernel,
        out_shape=pltpu.HBM((N_RING * N_RING, 3, rows, width), BF16),
        in_specs=[SCALAR] + [ON_CHIP] * (N_RING + 1),
        out_specs=FAR,
        scratch_shapes=[
            pltpu.VMEM((N_RING, N_RING, 3, rows, width), BF16),
            pltpu.SemaphoreType.DMA((N_RING, N_RING)),
        ],
        compiler_params=vmem(18),
        cost_estimate=pl.CostEstimate(flops=96 * rows * width * n, bytes_accessed=8 * MIB, transcendentals=0),
        name="weight_grad",
    )(me, whole, *feats)


def first_sum_kernel(me, *refs):
    parts, outs = refs[:N_RING], refs[N_RING:]
    for s in range(N_RING):
        k = pl.ds((place(me, first=False) + s) % N_RING, 1)
        total = parts[0][k].astype(F32)
        for i in range(1, N_RING):
            total = total + parts[i][k].astype(F32)
        outs[s][...] = total[0].astype(BF16)


def first_sum(me, parts):
    _, rows, n = parts[0].shape
    return pl.pallas_call(
        first_sum_kernel,
        out_shape=[like(rows, n)] * N_RING,
        in_specs=[SCALAR] + [ON_CHIP] * N_RING,
        out_specs=[ON_CHIP] * N_RING,
        compiler_params=vmem(6),
        name="first_sum",
    )(me, *parts)


def sum_kernel(me, *refs):
    parts, outs, whole = refs[:N_RING], refs[N_RING:-1], refs[-1]
    total = parts[0][...].astype(F32)
    for i in range(1, N_RING):
        total = total + parts[i][...].astype(F32)
    whole[...] = total.astype(BF16)
    tokens = outs[0].shape[-1]
    for ahead in range(N_X):
        for other in range(2):
            outs[ahead][other] = whole[:, part_of(target(me[0], ahead, other), tokens)]


def sum_parts(me, parts):
    rows, n = parts[0].shape
    return pl.pallas_call(
        sum_kernel,
        out_shape=[like(2, rows, n // N_CTX)] * N_X,
        in_specs=[SCALAR] + [ON_CHIP] * N_RING,
        out_specs=[ON_CHIP] * N_X,
        scratch_shapes=[pltpu.VMEM((rows, n), BF16)],
        compiler_params=vmem(6),
        name="sum_parts",
    )(me, *parts)


def finish_kernel(me, *refs):
    pieces, out, whole = refs[:N_CTX], refs[N_CTX], refs[N_CTX + 1]
    sub = pieces[0].shape[0]
    for p in range(N_CTX):
        whole[part_of(source(me[0], p), sub), :] = pieces[p][...]
    out[...] = whole[...].T


def finish(me, pieces):
    rows, tokens = pieces[0].shape
    return pl.pallas_call(
        finish_kernel,
        out_shape=like(tokens, rows * N_CTX),
        in_specs=[SCALAR] + [ON_CHIP] * N_CTX,
        scratch_shapes=[pltpu.VMEM((rows * N_CTX, tokens), BF16)],
        compiler_params=vmem(6),
        name="finish",
    )(me, *pieces)


def tie(a, b):
    return lax.optimization_barrier((a, b))


def per_device(features_in, w_featurizer, filter_taps, query_proj, key_proj, value_proj, grad_mixed):
    width_dev = features_in.shape[1]
    me = jnp.stack([lax.axis_index("ctx"), lax.axis_index("tp")]).astype(jnp.int32)
    weights = w_featurizer.transpose(0, 2, 1, 3)
    ready = prepare(me, (key_proj, value_proj, grad_mixed, query_proj, features_in))
    along = [ready[0]] + [shift_x(ready[s], s) for s in (1, 2, 3)]
    spec_taps = taps_spectrum(filter_taps.reshape(width_dev // N_CTX, -1))
    along, spec_taps = tie(along, spec_taps)
    *table, hr, hi, hn = spec_taps
    pieces = [a[0] for a in along] + [swap_core(a[1]) for a in along]
    grads, *spec = convolutions(me, pieces, table, (hr, hi, hn))
    pieces, grads = tie(pieces, grads)
    near = gather_start(grads)
    feats = join_features(me, pieces)
    feats = [feats] + [shift_ring(feats, s, first=False) for s in (1, 2, 3)]
    far, feats = tie(near[2], feats)
    last = spin(far)
    feats = stack(me, feats)
    grad_taps = taps_grad(spec, table)
    last, (grad_taps, feats) = tie(last, (grad_taps, feats))
    theirs = [swap_core(a) for a in near[2:]]
    feats = [feats] + [shift_ring(feats, s, first=True) for s in (1, 2, 3)]
    whole = assemble(me, near + theirs, (0, 1, 2, 3, 5, 6))
    part2, whole, far_whole = value_part(me, weights, whole, (2,), (last, swap_core(last)), (4, 7))
    (part1,) = value_part(me, weights, whole, (1,))
    (part3,) = value_part(me, weights, whole, (3,))
    whole, feats = tie(whole, feats)
    (part0,) = value_part(me, weights, whole, (0,))
    parts = [part0] + [shift_ring(p, s, first=True) for p, s in ((part1, 1), (part2, 2), (part3, 3))]
    parts = first_sum(me, parts)
    parts = [parts[0]] + [shift_ring(parts[s], s, first=False) for s in (1, 2, 3)]
    ready = sum_parts(me, parts)
    grad_w = weight_grad(me, far_whole, feats)
    along = [ready[0]] + [shift_x(ready[s], s) for s in (1, 2, 3)]
    along, grad_w = tie(along, grad_w)
    grad_features = finish(me, [a[0] for a in along] + [swap_core(a[1]) for a in along])
    return grad_features, grad_w.transpose(0, 2, 1, 3), grad_taps.reshape(filter_taps.shape)


def solution(mesh):
    return jax.shard_map(
        per_device,
        mesh=mesh,
        in_specs=(
            P("ctx", "tp"),
            P(None, "ctx", None, "tp"),
            P("tp", "ctx", None),
            P("ctx", "tp"),
            P("ctx", "tp"),
            P("ctx", "tp"),
            P("ctx", "tp"),
        ),
        out_specs=(P("ctx", "tp"), P(None, "ctx", None, "tp"), P("tp", "ctx", None)),
        check_vma=False,
    )
```

time: 156 us -> 98.1 us (0.63)
  starting transfers between devices: 12.1 us -> 44.9 us
  local copies, waits for them, and re-layouts: 33.6 us -> 0.98 us
  waiting for transfers between devices: 48.3 us -> 19.6 us
  blocking collectives: 23.7 us -> 0 us
  Pallas kernels: 7.59 us -> 30.4 us
  matrix products: 14.7 us -> 0 us
  between operations: 14.1 us -> 0.87 us
    ppermute x0 -> x33, starting transfers between devices: none -> 44.9 us  [the longest x12 18.2 us: shift_ring(): return lax.ppermute(a, ('ctx', 'tp'), pairs)]
    all_to_all x2 -> x0, waiting for transfers between devices: 26.1 us -> none  [the longest x1 26.1 us: per_device(): parts = lax.all_to_all(part.reshape(n_tp, sub, seq_len), 'tp', 0, 0)]
    all_to_all x2 -> x0, blocking collectives: 23.7 us -> none  [the longest x1 15 us: per_device(): recv = lax.all_to_all(sent, 'ctx', 0, 0)]
    pallas_call x1 -> x15, Pallas kernels: 7.59 us -> 30.4 us  [the longest x4 7.59 us: value_part(): pl.pallas_call(functools.partial(value_kernel, steps, which), out_shape=s...]
    all_gather x2 -> x0, waiting for transfers between devices: 22.2 us -> none  [the longest x1 11.7 us: per_device(): gathered = lax.all_gather(grads, 'ctx', axis=0)]
    ppermute x0 -> x33, waiting for transfers between devices: none -> 19.6 us  [the longest x12 15.2 us: shift_ring(): return lax.ppermute(a, ('ctx', 'tp'), pairs)]
    dot_general x2 -> x0, matrix products: 14.7 us -> none  [the longest x1 8.68 us: dot(): lax.dot_general(a, b, (((1,), (0,)), ((), ())), preferred_element_type=F32)]
    reshape x3 -> x0, local copies, waits for them, and re-layouts: 12.3 us -> none  [the longest x1 6.05 us: per_device(): grad_w.reshape(w_featurizer.shape)]
  transfers between devices with their start and end apart: 4 -> 33, of which waited for: 3 -> 17; matrix products, arithmetic and copies ran while one was open for 27% -> 0% of each run, Pallas kernels for 0% -> 22%
where the time goes in v2:
time: 98.1 us; the launch traced here: 96.8 us
  starting transfers between devices  44.9 us (46%)
  Pallas kernels  30.4 us (31%)
  waiting for transfers between devices  19.6 us (20%)
    ppermute x12, starting transfers between devices, shift_ring(): return lax.ppermute(a, ('ctx', 'tp'), pairs)  18.2 us
    ppermute x12, waiting for transfers between devices, shift_ring(): return lax.ppermute(a, ('ctx', 'tp'), pairs)  15.2 us
    ppermute x12, starting transfers between devices, swap_core(): return lax.ppermute(a, 'ctx', [(i, i ^ 1) for i in range(N_CTX)])  14.4 us
    ppermute x6, starting transfers between devices, shift_x(): lax.ppermute(a, 'ctx', [(i, (i + 2 * steps) % N_CTX) for i in range(N_CTX)])  8.45 us
    pallas_call x4, Pallas kernels, value_part(): pl.pallas_call(functools.partial(value_kernel, steps, which), out_shape=s...  7.59 us
    pallas_call x1, Pallas kernels, taps_spectrum(): pl.pallas_call(taps_kernel, out_shape=[like(n, n)] * 4 + [like(chans, n,...  5.07 us
    pallas_call x1, Pallas kernels, weight_grad(): pl.pallas_call(weight_kernel, out_shape=pltpu.HBM((N_RING * N_RING, 3, ro...  5.03 us
    pallas_call x1, Pallas kernels, convolutions(): pl.pallas_call(conv_kernel, out_shape=[like(3, chans, n)] + [like(chans,...  3.98 us
  transfers between devices with their start and end apart: 33, of which 17 were waited for; matrix products, arithmetic and copies ran while one was open for 0% of the time, Pallas kernels for 22%

profile of v2, /device:TPU:1, one launch (start us, length us, event | category | flops | bytes accessed | tf_op | source)
XLA Modules:
  0.0 96.8 jit_solution(8880879984256645374)
XLA Ops:
  0.6 0.1 pad_add_fusion.me
  0.7 2.0 %prepare.1 = (bf16[2,5,64,128]{3,2,1,0:T(8,128)(2,1)S(1)}, bf16[2,5,64,128]{3,2,1,0:T(8,128)(2,1)S(1)}, bf16[2,5,64,128]{3,2,1,0:T(8,128)(2,1)S(1)}, bf16[2,5,64,128]{3,2,1,0:T(8,128)(2,1)S(1)}) custom-call(s32[2]{0:T(128)S(1)} %pad_add_fusion.me, bf16[128,512]{1,0:T(8,128)(2,1)} %refs_0_.2, bf16[128,512]{1,0:T(8,128)(2,1)} %refs_1_.2, ...), custom_call_target="tpu_custom_call" | custom-call | tf_op jit(solution)/shard_map/prepare/pallas_call | solution.py:139
  2.7 2.1 %collective-permute-start = (bf16[2,5,64,128]{3,2,1,0:T(8,128)(2,1)S(1)}, bf16[2,5,64,128]{3,2,1,0:T(8,128)(2,1)S(1)}, u32[]{:S(2)}, u32[]{:S(2)}) collective-permute-start(bf16[2,5,64,128]{3,2,1,0:T(8,128)(2,1)S(1)} %get-tuple-element.68), channel_id=1, source_target_pairs={{0,32},{16,48},{32,64},{48,80},{64,96},{80,112},{96,0},{112,16},{1... | collective-permute-start | bytes 491528 | tf_op jit(solution)/shard_map/ppermute | solution.py:51
  4.8 2.5 %collective-permute-start.1 = (bf16[2,5,64,128]{3,2,1,0:T(8,128)(2,1)S(1)}, bf16[2,5,64,128]{3,2,1,0:T(8,128)(2,1)S(1)}, u32[]{:S(2)}, u32[]{:S(2)}) collective-permute-start(bf16[2,5,64,128]{3,2,1,0:T(8,128)(2,1)S(1)} %get-tuple-element.69), channel_id=1, source_target_pairs={{0,64},{16,80},{32,96},{48,112},{64,0},{80,16},{96,32},{112,48},{1... | collective-permute-start | bytes 491528 | tf_op jit(solution)/shard_map/ppermute | solution.py:51
  7.3 1.2 %collective-permute-start.2 = (bf16[2,5,64,128]{3,2,1,0:T(8,128)(2,1)S(1)}, bf16[2,5,64,128]{3,2,1,0:T(8,128)(2,1)S(1)}, u32[]{:S(2)}, u32[]{:S(2)}) collective-permute-start(bf16[2,5,64,128]{3,2,1,0:T(8,128)(2,1)S(1)} %get-tuple-element.70), channel_id=1, source_target_pairs={{0,96},{16,112},{32,0},{48,16},{64,32},{80,48},{96,64},{112,80},{1... | collective-permute-start | bytes 491528 | tf_op jit(solution)/shard_map/ppermute | solution.py:51
  8.4 0.9 copy-done.1
  9.3 5.1 %taps_spectrum.1 = (bf16[1024,1024]{1,0:T(8,128)(2,1)S(1)}, bf16[1024,1024]{1,0:T(8,128)(2,1)S(1)}, bf16[1024,1024]{1,0:T(8,128)(2,1)S(1)}, bf16[1024,1024]{1,0:...) custom-call(bf16[1024,1024]{1,0:T(8,128)(2,1)} %constant.17.clone.refs_0_, ...), custom_call_target="tpu_custom_call" | custom-call | flops 536870912 | bytes 8388608 | tf_op jit(solution)/shard_map/taps_spectrum/pallas_call | solution.py:232
  14.4 1.6 %collective-permute-start.3 = (bf16[5,64,128]{2,1,0:T(8,128)(2,1)S(1)}, bf16[5,64,128]{2,1,0:T(8,128)(2,1)S(1)}, u32[]{:S(2)}, u32[]{:S(2)}) collective-permute-start(bf16[5,64,128]{2,1,0:T(8,128)(2,1)S(1)} %get-tuple-element.137), channel_id=1, source_target_pairs={{0,16},{16,0},{32,48},{48,32},{64,80},{80,64},{96,112},{112,96},{1... | collective-permute-start | bytes 245768 | tf_op jit(solution)/shard_map/ppermute | solution.py:55
  16.0 0.1 collective-permute-start.4
  16.2 0.6 collective-permute-start.5
  16.7 0.1 collective-permute-start.6
  16.8 0.1 collective-permute-done.3.refs_4_
  17.0 0.4 collective-permute-done.4.refs_5_
  17.4 0.2 collective-permute-done.5.refs_6_
  17.7 0.4 collective-permute-done.6.refs_7_
  18.1 4.0 %convolutions.1 = (bf16[3,64,1024]{2,1,0:T(8,128)(2,1)S(1)}, f32[64,1024]{1,0:T(8,128)S(1)}, f32[64,1024]{1,0:T(8,128)S(1)}, f32[64,1]{1,0:T(8,128)S(1)}) custom-call(s32[2]{0:T(128)S(1)} %pad_add_fusion.me, bf16[5,64,128]{2,1,0:T(8,128)(2,1)S(1)} %get-tuple-element.91.refs_0_, bf16[5,64,128]{2,1,0:T(8,128)(2,1)S(1)} %get-tuple-element.92.refs_1_, ...), custom_call_target="tpu_custom_call" | custom-call | flops 2147483648 | bytes 8388608 | tf_op jit(solution)/shard_map/convolutions/pallas_call | solution.py:273
  22.1 1.9 %collective-permute-start.8 = (bf16[3,64,1024]{2,1,0:T(8,128)(2,1)S(1)}, bf16[3,64,1024]{2,1,0:T(8,128)(2,1)S(1)}, u32[]{:S(2)}, u32[]{:S(2)}) collective-permute-start(bf16[3,64,1024]{2,1,0:T(8,128)(2,1)S(1)} %get-tuple-element.90.refs_0_), channel_id=1, source_target_pairs={{0,32},{16,112},{32,64},{48,16},{64,96},{80,48},{96,0},{112,80},{1... | collective-permute-start | bytes 1179656 | tf_op jit(solution)/shard_map/ppermute | solution.py:67
  24.0 0.6 join_features.1.refs_0_
  24.6 1.5 %collective-permute-start.12 = (bf16[64,1024]{1,0:T(8,128)(2,1)S(1)}, bf16[64,1024]{1,0:T(8,128)(2,1)S(1)}, u32[]{:S(2)}, u32[]{:S(2)}) collective-permute-start(bf16[64,1024]{1,0:T(8,128)(2,1)S(1)} %join_features.1.refs_0_), channel_id=1, source_target_pairs={{0,1},{1,2},{2,3},{3,0},{4,5},{5,6},{6,7},{7,4},{8,9},{9,10},{10,1... | collective-permute-start | bytes 393224 | tf_op jit(solution)/shard_map/ppermute | solution.py:111
  26.1 2.6 %collective-permute-start.13 = (bf16[64,1024]{1,0:T(8,128)(2,1)S(1)}, bf16[64,1024]{1,0:T(8,128)(2,1)S(1)}, u32[]{:S(2)}, u32[]{:S(2)}) collective-permute-start(bf16[64,1024]{1,0:T(8,128)(2,1)S(1)} %join_features.1.refs_0_), channel_id=1, source_target_pairs={{0,2},{1,3},{2,0},{3,1},{4,6},{5,7},{6,4},{7,5},{8,10},{9,11},{10,... | collective-permute-start | bytes 393224 | tf_op jit(solution)/shard_map/ppermute | solution.py:111
  28.7 1.1 %collective-permute-start.14 = (bf16[64,1024]{1,0:T(8,128)(2,1)S(1)}, bf16[64,1024]{1,0:T(8,128)(2,1)S(1)}, u32[]{:S(2)}, u32[]{:S(2)}) collective-permute-start(bf16[64,1024]{1,0:T(8,128)(2,1)S(1)} %join_features.1.refs_0_), channel_id=1, source_target_pairs={{0,3},{1,0},{2,1},{3,2},{4,7},{5,4},{6,5},{7,6},{8,11},{9,8},{10,9... | collective-permute-start | bytes 393224 | tf_op jit(solution)/shard_map/ppermute | solution.py:111
  29.8 0.4 collective-permute-done.12.refs_1_
  30.2 2.3 %collective-permute-done.13.refs_2_ = bf16[64,1024]{1,0:T(8,128)(2,1)S(1)} collective-permute-done((bf16[64,1024]{1,0:T(8,128)(2,1)S(1)}, bf16[64,1024]{1,0:T(8,128)(2,1)S(1)}, u32[]{:S(2)}, u32[]{:S(2)}) %collective-permute-start.13) | collective-permute-done | bytes 131104 | tf_op jit(solution)/shard_map/ppermute | solution.py:111
  32.5 1.2 %collective-permute-start.15 = (bf16[3,64,1024]{2,1,0:T(8,128)(2,1)S(1)}, bf16[3,64,1024]{2,1,0:T(8,128)(2,1)S(1)}, u32[]{:S(2)}, u32[]{:S(2)}) collective-permute-start(bf16[3,64,1024]{2,1,0:T(8,128)(2,1)S(1)} %collective-permute-done.8.refs_2_), channel_id=1, source_target_pairs={{0,32},{16,112},{32,64},{48,16},{64,96},{80,48},{96,0},{112,80},{1... | collective-permute-start | bytes 1179656 | tf_op jit(solution)/shard_map/ppermute | solution.py:67
  33.7 0.8 collective-permute-start.9
  34.4 2.1 %taps_grad.1 = bf16[64,1024]{1,0:T(8,128)(2,1)} custom-call(bf16[1024,1024]{1,0:T(8,128)(2,1)S(1)} %get-tuple-element.82.refs_8_.refs_0_, bf16[1024,1024]{1,0:T(8,128)(2,1)S(1)} %get-tuple-element.83.refs_9_.refs_1_, bf16[1024,1024]{1,0:T(8,128)(2,1)S(1)} %get-tuple-element.84.refs_10_.refs_2_, bf16[1024,1024]{1,0:T(8,128)(2,1)S(1)} %get-tuple-element.85.refs_11_.refs_3_, ...), custom_call_target="tpu_custom_call" | custom-call | flops 1073741824 | bytes 8388608 | tf_op jit(solution)/shard_map/taps_grad/pallas_call | solution.py:291
  36.5 0.6 stack_features.1.refs_0_
  37.1 2.0 %collective-permute-done.15.refs_2_ = bf16[3,64,1024]{2,1,0:T(8,128)(2,1)S(1)} collective-permute-done((bf16[3,64,1024]{2,1,0:T(8,128)(2,1)S(1)}, bf16[3,64,1024]{2,1,0:T(8,128)(2,1)S(1)}, u32[]{:S(2)}, u32[]{:S(2)}) %collective-permute-start.15) | collective-permute-done | bytes 393248 | tf_op jit(solution)/shard_map/ppermute | solution.py:67
  39.1 2.2 %collective-permute-start.17 = (bf16[4,64,1024]{2,1,0:T(8,128)(2,1)S(1)}, bf16[4,64,1024]{2,1,0:T(8,128)(2,1)S(1)}, u32[]{:S(2)}, u32[]{:S(2)}) collective-permute-start(bf16[4,64,1024]{2,1,0:T(8,128)(2,1)S(1)} %stack_features.1.refs_0_), channel_id=1, source_target_pairs={{0,4},{1,5},{2,6},{3,7},{4,8},{5,9},{6,10},{7,11},{8,12},{9,13},{1... | collective-permute-start | bytes 1572872 | tf_op jit(solution)/shard_map/ppermute | solution.py:111
  41.4 4.9 %collective-permute-start.10 = (bf16[3,64,1024]{2,1,0:T(8,128)(2,1)S(1)}, bf16[3,64,1024]{2,1,0:T(8,128)(2,1)S(1)}, u32[]{:S(2)}, u32[]{:S(2)}) collective-permute-start(bf16[3,64,1024]{2,1,0:T(8,128)(2,1)S(1)} %collective-permute-done.8.refs_2_), channel_id=1, source_target_pairs={{0,16},{16,0},{32,48},{48,32},{64,80},{80,64},{96,112},{112,96},{1... | collective-permute-start | bytes 1179656 | tf_op jit(solution)/shard_map/ppermute | solution.py:55
  46.3 2.6 %collective-permute-start.11 = (bf16[3,64,1024]{2,1,0:T(8,128)(2,1)S(1)}, bf16[3,64,1024]{2,1,0:T(8,128)(2,1)S(1)}, u32[]{:S(2)}, u32[]{:S(2)}) collective-permute-start(bf16[3,64,1024]{2,1,0:T(8,128)(2,1)S(1)} %collective-permute-done.9.refs_3_), channel_id=1, source_target_pairs={{0,16},{16,0},{32,48},{48,32},{64,80},{80,64},{96,112},{112,96},{1... | collective-permute-start | bytes 1179656 | tf_op jit(solution)/shard_map/ppermute | solution.py:55
  49.0 1.6 %collective-permute-start.18 = (bf16[4,64,1024]{2,1,0:T(8,128)(2,1)S(1)}, bf16[4,64,1024]{2,1,0:T(8,128)(2,1)S(1)}, u32[]{:S(2)}, u32[]{:S(2)}) collective-permute-start(bf16[4,64,1024]{2,1,0:T(8,128)(2,1)S(1)} %stack_features.1.refs_0_), channel_id=1, source_target_pairs={{0,8},{1,9},{2,10},{3,11},{4,12},{5,13},{6,14},{7,15},{8,0},{9,1},... | collective-permute-start | bytes 1572872 | tf_op jit(solution)/shard_map/ppermute | solution.py:111
  50.6 1.4 %collective-permute-start.19 = (bf16[4,64,1024]{2,1,0:T(8,128)(2,1)S(1)}, bf16[4,64,1024]{2,1,0:T(8,128)(2,1)S(1)}, u32[]{:S(2)}, u32[]{:S(2)}) collective-permute-start(bf16[4,64,1024]{2,1,0:T(8,128)(2,1)S(1)} %stack_features.1.refs_0_), channel_id=1, source_target_pairs={{0,12},{1,13},{2,14},{3,15},{4,0},{5,1},{6,2},{7,3},{8,4},{9,5},{1... | collective-permute-start | bytes 1572872 | tf_op jit(solution)/shard_map/ppermute | solution.py:111
  52.0 0.7 assemble.1.refs_1_
  52.7 3.0 %value_part.4 = (bf16[4,64,1024]{2,1,0:T(8,128)(2,1)S(1)}, bf16[1536,1024]{1,0:T(8,128)(2,1)S(1)}, bf16[1536,1024]{1,0:T(8,128)(2,1)}) custom-call(s32[2]{0:T(128)S(1)} %pad_add_fusion.me, bf16[16,3,64,512]{3,2,1,0:T(8,128)(2,1)S(1)} %bitcast.38, bf16[1536,1024]{1,0:T(8,128)(2,1)S(1)} %assemble.1.refs_1_, ...), custom_call_target="tpu_custom_call", output_to_operand_aliasing={{1}: (2, {})} | custom-call | flops 67108864 | bytes 262144 | tf_op jit(solution)/shard_map/value_part/pallas_call | solution.py:357
  55.8 1.5 %value_part.6 = bf16[4,64,1024]{2,1,0:T(8,128)(2,1)S(1)} custom-call(s32[2]{0:T(128)S(1)} %pad_add_fusion.me, bf16[16,3,64,512]{3,2,1,0:T(8,128)(2,1)S(1)} %bitcast.39, bf16[1536,1024]{1,0:T(8,128)(2,1)S(1)} %get-tuple-element.110.refs_1_), custom_call_target="tpu_custom_call" | custom-call | flops 67108864 | bytes 262144 | tf_op jit(solution)/shard_map/value_part/pallas_call | solution.py:357
  57.3 0.2 collective-permute-start.20
  57.4 1.5 %value_part.7 = bf16[4,64,1024]{2,1,0:T(8,128)(2,1)S(1)} custom-call(s32[2]{0:T(128)S(1)} %pad_add_fusion.me, bf16[16,3,64,512]{3,2,1,0:T(8,128)(2,1)S(1)} %bitcast.40, bf16[1536,1024]{1,0:T(8,128)(2,1)S(1)} %get-tuple-element.110.refs_1_), custom_call_target="tpu_custom_call" | custom-call | flops 67108864 | bytes 262144 | tf_op jit(solution)/shard_map/value_part/pallas_call | solution.py:357
  59.0 2.7 %collective-permute-start.22 = (bf16[4,64,1024]{2,1,0:T(8,128)(2,1)S(1)}, bf16[4,64,1024]{2,1,0:T(8,128)(2,1)S(1)}, u32[]{:S(2)}, u32[]{:S(2)}) collective-permute-start(bf16[4,64,1024]{2,1,0:T(8,128)(2,1)S(1)} %value_part.7), channel_id=1, source_target_pairs={{0,12},{1,13},{2,14},{3,15},{4,0},{5,1},{6,2},{7,3},{8,4},{9,5},{1... | collective-permute-start | bytes 1572872 | tf_op jit(solution)/shard_map/ppermute | solution.py:111
  61.6 0.1 collective-permute-start.21
  61.7 2.3 %collective-permute-done.19.refs_3_ = bf16[4,64,1024]{2,1,0:T(8,128)(2,1)S(1)} collective-permute-done((bf16[4,64,1024]{2,1,0:T(8,128)(2,1)S(1)}, bf16[4,64,1024]{2,1,0:T(8,128)(2,1)S(1)}, u32[]{:S(2)}, u32[]{:S(2)}) %collective-permute-start.19) | collective-permute-done | bytes 524320 | tf_op jit(solution)/shard_map/ppermute | solution.py:111
  64.0 1.5 %value_part.5.refs_0_ = bf16[4,64,1024]{2,1,0:T(8,128)(2,1)S(1)} custom-call(s32[2]{0:T(128)S(1)} %pad_add_fusion.me, bf16[16,3,64,512]{3,2,1,0:T(8,128)(2,1)S(1)} %bitcast.41, bf16[1536,1024]{1,0:T(8,128)(2,1)S(1)} %get-tuple-element.110.refs_1_), custom_call_target="tpu_custom_call" | custom-call | flops 67108864 | bytes 262144 | tf_op jit(solution)/shard_map/value_part/pallas_call | solution.py:357
  65.5 7.0 %collective-permute-done.20.refs_1_ = bf16[4,64,1024]{2,1,0:T(8,128)(2,1)S(1)} collective-permute-done((bf16[4,64,1024]{2,1,0:T(8,128)(2,1)S(1)}, bf16[4,64,1024]{2,1,0:T(8,128)(2,1)S(1)}, u32[]{:S(2)}, u32[]{:S(2)}) %collective-permute-start.20) | collective-permute-done | bytes 524320 | tf_op jit(solution)/shard_map/ppermute | solution.py:111
  72.5 0.8 first_sum.1
  73.3 1.2 %collective-permute-start.23 = (bf16[64,1024]{1,0:T(8,128)(2,1)S(1)}, bf16[64,1024]{1,0:T(8,128)(2,1)S(1)}, u32[]{:S(2)}, u32[]{:S(2)}) collective-permute-start(bf16[64,1024]{1,0:T(8,128)(2,1)S(1)} %get-tuple-element.113), channel_id=1, source_target_pairs={{0,1},{1,2},{2,3},{3,0},{4,5},{5,6},{6,7},{7,4},{8,9},{9,10},{10,1... | collective-permute-start | bytes 393224 | tf_op jit(solution)/shard_map/ppermute | solution.py:111
  74.6 2.8 %collective-permute-start.24 = (bf16[64,1024]{1,0:T(8,128)(2,1)S(1)}, bf16[64,1024]{1,0:T(8,128)(2,1)S(1)}, u32[]{:S(2)}, u32[]{:S(2)}) collective-permute-start(bf16[64,1024]{1,0:T(8,128)(2,1)S(1)} %get-tuple-element.114), channel_id=1, source_target_pairs={{0,2},{1,3},{2,0},{3,1},{4,6},{5,7},{6,4},{7,5},{8,10},{9,11},{10,... | collective-permute-start | bytes 393224 | tf_op jit(solution)/shard_map/ppermute | solution.py:111
  77.3 0.9 collective-permute-start.25
  78.2 0.3 collective-permute-done.23.refs_1_
  78.5 2.6 %collective-permute-done.24.refs_2_ = bf16[64,1024]{1,0:T(8,128)(2,1)S(1)} collective-permute-done((bf16[64,1024]{1,0:T(8,128)(2,1)S(1)}, bf16[64,1024]{1,0:T(8,128)(2,1)S(1)}, u32[]{:S(2)}, u32[]{:S(2)}) %collective-permute-start.24) | collective-permute-done | bytes 131104 | tf_op jit(solution)/shard_map/ppermute | solution.py:111
  81.1 0.4 collective-permute-done.25.refs_3_
  81.5 0.7 sum_parts.1
  82.1 0.1 collective-permute-start.26
  82.2 0.6 collective-permute-start.27
  82.8 2.0 %collective-permute-start.28 = (bf16[2,64,128]{2,1,0:T(8,128)(2,1)S(1)}, bf16[2,64,128]{2,1,0:T(8,128)(2,1)S(1)}, u32[]{:S(2)}, u32[]{:S(2)}) collective-permute-start(bf16[2,64,128]{2,1,0:T(8,128)(2,1)S(1)} %get-tuple-element.119), channel_id=1, source_target_pairs={{0,96},{16,112},{32,0},{48,16},{64,32},{80,48},{96,64},{112,80},{1... | collective-permute-start | bytes 98312 | tf_op jit(solution)/shard_map/ppermute | solution.py:51
  84.9 5.0 %weight_grad.1 = bf16[16,3,64,512]{3,2,1,0:T(8,128)(2,1)} custom-call(s32[2]{0:T(128)S(1)} %pad_add_fusion.me, bf16[1536,1024]{1,0:T(8,128)(2,1)S(1)} %copy-done.2, bf16[4,64,1024]{2,1,0:T(8,128)(2,1)S(1)} %stack_features.1.refs_0_, bf16[4,64,1024]{2,1,0:T(8,128)(2,1)S(1)} %collective-permute-done.17.refs_1_, ...), custom_call_target="tpu_custom_call" | custom-call | flops 3221225472 | bytes 8388608 | tf_op jit(solution)/shard_map/weight_grad/pallas_call | solution.py:392
  89.9 3.9 %collective-permute-start.29 = (bf16[64,128]{1,0:T(8,128)(2,1)S(1)}, bf16[64,128]{1,0:T(8,128)(2,1)S(1)}, u32[]{:S(2)}, u32[]{:S(2)}) collective-permute-start(bf16[64,128]{1,0:T(8,128)(2,1)S(1)} %get-tuple-element.145), channel_id=1, source_target_pairs={{0,16},{16,0},{32,48},{48,32},{64,80},{80,64},{96,112},{112,96},{1... | collective-permute-start | bytes 49160 | tf_op jit(solution)/shard_map/ppermute | solution.py:55
  93.8 0.1 collective-permute-start.30
  93.9 0.4 collective-permute-start.31
  94.3 0.1 collective-permute-start.32
  94.4 0.2 collective-permute-done.29.refs_4_
  94.7 0.3 collective-permute-done.30.refs_5_
  95.0 0.2 collective-permute-done.31.refs_6_
  95.2 0.3 collective-permute-done.32.refs_7_
  95.5 1.3 %finish.1 = bf16[128,512]{1,0:T(8,128)(2,1)} custom-call(s32[2]{0:T(128)S(1)} %pad_add_fusion.me, bf16[64,128]{1,0:T(8,128)(2,1)S(1)} %get-tuple-element.146.refs_0_, bf16[64,128]{1,0:T(8,128)(2,1)S(1)} %get-tuple-element.144.refs_1_, bf16[64,128]{1,0:T(8,128)(2,1)S(1)} %get-tuple-element.142.refs_2_, bf16[64,128]{1,0:T(8,128)(2,1)S(1)} %get-tuple-element.140.refs_3_, ...), custom_call_target="tpu_custom_call" | custom-call | tf_op jit(solution)/shard_map/finish/pallas_call | solution.py:464
  (32 shorter events, 0.2 us)
Async XLA Ops:
  2.7 11.7 %collective-permute-start = (bf16[2,5,64,128]{3,2,1,0:T(8,128)(2,1)S(1)}, bf16[2,5,64,128]{3,2,1,0:T(8,128)(2,1)S(1)}, u32[]{:S(2)}, u32[]{:S(2)}) collective-permute-start(bf16[2,5,64,128]{3,2,1,0:T(8,128)(2,1)S(1)} %get-tuple-element.68), channel_id=1, source_target_pairs={{0,32},{16,48},{32,64},{48,80},{64,96},{80,112},{96,0},{112,16},{1... | collective-permute-start | bytes 491528 | tf_op jit(solution)/shard_map/ppermute | solution.py:51
  4.8 9.6 %collective-permute-start.1 = (bf16[2,5,64,128]{3,2,1,0:T(8,128)(2,1)S(1)}, bf16[2,5,64,128]{3,2,1,0:T(8,128)(2,1)S(1)}, u32[]{:S(2)}, u32[]{:S(2)}) collective-permute-start(bf16[2,5,64,128]{3,2,1,0:T(8,128)(2,1)S(1)} %get-tuple-element.69), channel_id=1, source_target_pairs={{0,64},{16,80},{32,96},{48,112},{64,0},{80,16},{96,32},{112,48},{1... | collective-permute-start | bytes 491528 | tf_op jit(solution)/shard_map/ppermute | solution.py:51
  7.3 7.2 %collective-permute-start.2 = (bf16[2,5,64,128]{3,2,1,0:T(8,128)(2,1)S(1)}, bf16[2,5,64,128]{3,2,1,0:T(8,128)(2,1)S(1)}, u32[]{:S(2)}, u32[]{:S(2)}) collective-permute-start(bf16[2,5,64,128]{3,2,1,0:T(8,128)(2,1)S(1)} %get-tuple-element.70), channel_id=1, source_target_pairs={{0,96},{16,112},{32,0},{48,16},{64,32},{80,48},{96,64},{112,80},{1... | collective-permute-start | bytes 491528 | tf_op jit(solution)/shard_map/ppermute | solution.py:51
  8.4 0.9 copy-start.1
  14.4 2.5 %collective-permute-start.3 = (bf16[5,64,128]{2,1,0:T(8,128)(2,1)S(1)}, bf16[5,64,128]{2,1,0:T(8,128)(2,1)S(1)}, u32[]{:S(2)}, u32[]{:S(2)}) collective-permute-start(bf16[5,64,128]{2,1,0:T(8,128)(2,1)S(1)} %get-tuple-element.137), channel_id=1, source_target_pairs={{0,16},{16,0},{32,48},{48,32},{64,80},{80,64},{96,112},{112,96},{1... | collective-permute-start | bytes 245768 | tf_op jit(solution)/shard_map/ppermute | solution.py:55
  16.0 1.4 %collective-permute-start.4 = (bf16[5,64,128]{2,1,0:T(8,128)(2,1)S(1)}, bf16[5,64,128]{2,1,0:T(8,128)(2,1)S(1)}, u32[]{:S(2)}, u32[]{:S(2)}) collective-permute-start(bf16[5,64,128]{2,1,0:T(8,128)(2,1)S(1)} %get-tuple-element.135), channel_id=1, source_target_pairs={{0,16},{16,0},{32,48},{48,32},{64,80},{80,64},{96,112},{112,96},{1... | collective-permute-start | bytes 245768 | tf_op jit(solution)/shard_map/ppermute | solution.py:55
  16.2 1.5 %collective-permute-start.5 = (bf16[5,64,128]{2,1,0:T(8,128)(2,1)S(1)}, bf16[5,64,128]{2,1,0:T(8,128)(2,1)S(1)}, u32[]{:S(2)}, u32[]{:S(2)}) collective-permute-start(bf16[5,64,128]{2,1,0:T(8,128)(2,1)S(1)} %get-tuple-element.133), channel_id=1, source_target_pairs={{0,16},{16,0},{32,48},{48,32},{64,80},{80,64},{96,112},{112,96},{1... | collective-permute-start | bytes 245768 | tf_op jit(solution)/shard_map/ppermute | solution.py:55
  16.7 1.4 %collective-permute-start.6 = (bf16[5,64,128]{2,1,0:T(8,128)(2,1)S(1)}, bf16[5,64,128]{2,1,0:T(8,128)(2,1)S(1)}, u32[]{:S(2)}, u32[]{:S(2)}) collective-permute-start(bf16[5,64,128]{2,1,0:T(8,128)(2,1)S(1)} %get-tuple-element.131), channel_id=1, source_target_pairs={{0,16},{16,0},{32,48},{48,32},{64,80},{80,64},{96,112},{112,96},{1... | collective-permute-start | bytes 245768 | tf_op jit(solution)/shard_map/ppermute | solution.py:55
  22.1 10.4 %collective-permute-start.8 = (bf16[3,64,1024]{2,1,0:T(8,128)(2,1)S(1)}, bf16[3,64,1024]{2,1,0:T(8,128)(2,1)S(1)}, u32[]{:S(2)}, u32[]{:S(2)}) collective-permute-start(bf16[3,64,1024]{2,1,0:T(8,128)(2,1)S(1)} %get-tuple-element.90.refs_0_), channel_id=1, source_target_pairs={{0,32},{16,112},{32,64},{48,16},{64,96},{80,48},{96,0},{112,80},{1... | collective-permute-start | bytes 1179656 | tf_op jit(solution)/shard_map/ppermute | solution.py:67
  24.0 9.7 %collective-permute-start.7 = (bf16[3,64,1024]{2,1,0:T(8,128)(2,1)S(1)}, bf16[3,64,1024]{2,1,0:T(8,128)(2,1)S(1)}, u32[]{:S(2)}, u32[]{:S(2)}) collective-permute-start(bf16[3,64,1024]{2,1,0:T(8,128)(2,1)S(1)} %get-tuple-element.90.refs_0_), channel_id=1, source_target_pairs={{0,16},{16,0},{32,48},{48,32},{64,80},{80,64},{96,112},{112,96},{1... | collective-permute-start | bytes 1179656 | tf_op jit(solution)/shard_map/ppermute | solution.py:55
  24.6 5.6 %collective-permute-start.12 = (bf16[64,1024]{1,0:T(8,128)(2,1)S(1)}, bf16[64,1024]{1,0:T(8,128)(2,1)S(1)}, u32[]{:S(2)}, u32[]{:S(2)}) collective-permute-start(bf16[64,1024]{1,0:T(8,128)(2,1)S(1)} %join_features.1.refs_0_), channel_id=1, source_target_pairs={{0,1},{1,2},{2,3},{3,0},{4,5},{5,6},{6,7},{7,4},{8,9},{9,10},{10,1... | collective-permute-start | bytes 393224 | tf_op jit(solution)/shard_map/ppermute | solution.py:111
  26.1 6.4 %collective-permute-start.13 = (bf16[64,1024]{1,0:T(8,128)(2,1)S(1)}, bf16[64,1024]{1,0:T(8,128)(2,1)S(1)}, u32[]{:S(2)}, u32[]{:S(2)}) collective-permute-start(bf16[64,1024]{1,0:T(8,128)(2,1)S(1)} %join_features.1.refs_0_), channel_id=1, source_target_pairs={{0,2},{1,3},{2,0},{3,1},{4,6},{5,7},{6,4},{7,5},{8,10},{9,11},{10,... | collective-permute-start | bytes 393224 | tf_op jit(solution)/shard_map/ppermute | solution.py:111
  28.7 3.8 %collective-permute-start.14 = (bf16[64,1024]{1,0:T(8,128)(2,1)S(1)}, bf16[64,1024]{1,0:T(8,128)(2,1)S(1)}, u32[]{:S(2)}, u32[]{:S(2)}) collective-permute-start(bf16[64,1024]{1,0:T(8,128)(2,1)S(1)} %join_features.1.refs_0_), channel_id=1, source_target_pairs={{0,3},{1,0},{2,1},{3,2},{4,7},{5,4},{6,5},{7,6},{8,11},{9,8},{10,9... | collective-permute-start | bytes 393224 | tf_op jit(solution)/shard_map/ppermute | solution.py:111
  32.5 6.6 %collective-permute-start.15 = (bf16[3,64,1024]{2,1,0:T(8,128)(2,1)S(1)}, bf16[3,64,1024]{2,1,0:T(8,128)(2,1)S(1)}, u32[]{:S(2)}, u32[]{:S(2)}) collective-permute-start(bf16[3,64,1024]{2,1,0:T(8,128)(2,1)S(1)} %collective-permute-done.8.refs_2_), channel_id=1, source_target_pairs={{0,32},{16,112},{32,64},{48,16},{64,96},{80,48},{96,0},{112,80},{1... | collective-permute-start | bytes 1179656 | tf_op jit(solution)/shard_map/ppermute | solution.py:67
  33.7 12.7 %collective-permute-start.9 = (bf16[3,64,1024]{2,1,0:T(8,128)(2,1)S(1)}, bf16[3,64,1024]{2,1,0:T(8,128)(2,1)S(1)}, u32[]{:S(2)}, u32[]{:S(2)}) collective-permute-start(bf16[3,64,1024]{2,1,0:T(8,128)(2,1)S(1)} %collective-permute-done.7.refs_1_), channel_id=1, source_target_pairs={{0,32},{16,112},{32,64},{48,16},{64,96},{80,48},{96,0},{112,80},{1... | collective-permute-start | bytes 1179656 | tf_op jit(solution)/shard_map/ppermute | solution.py:67
  37.1 15.6 %copy-start = (bf16[16,64,3,512]{3,1,2,0:T(8,128)(2,1)S(1)}, bf16[16,64,3,512]{3,1,2,0:T(8,128)(2,1)}, u32[]{:S(2)}) copy-start(bf16[16,64,3,512]{3,1,2,0:T(8,128)(2,1)} %param.12) | copy-start | bytes 9437188
  39.1 22.5 %collective-permute-start.17 = (bf16[4,64,1024]{2,1,0:T(8,128)(2,1)S(1)}, bf16[4,64,1024]{2,1,0:T(8,128)(2,1)S(1)}, u32[]{:S(2)}, u32[]{:S(2)}) collective-permute-start(bf16[4,64,1024]{2,1,0:T(8,128)(2,1)S(1)} %stack_features.1.refs_0_), channel_id=1, source_target_pairs={{0,4},{1,5},{2,6},{3,7},{4,8},{5,9},{6,10},{7,11},{8,12},{9,13},{1... | collective-permute-start | bytes 1572872 | tf_op jit(solution)/shard_map/ppermute | solution.py:111
  41.4 9.2 %collective-permute-start.10 = (bf16[3,64,1024]{2,1,0:T(8,128)(2,1)S(1)}, bf16[3,64,1024]{2,1,0:T(8,128)(2,1)S(1)}, u32[]{:S(2)}, u32[]{:S(2)}) collective-permute-start(bf16[3,64,1024]{2,1,0:T(8,128)(2,1)S(1)} %collective-permute-done.8.refs_2_), channel_id=1, source_target_pairs={{0,16},{16,0},{32,48},{48,32},{64,80},{80,64},{96,112},{112,96},{1... | collective-permute-start | bytes 1179656 | tf_op jit(solution)/shard_map/ppermute | solution.py:55
  46.3 5.6 %collective-permute-start.11 = (bf16[3,64,1024]{2,1,0:T(8,128)(2,1)S(1)}, bf16[3,64,1024]{2,1,0:T(8,128)(2,1)S(1)}, u32[]{:S(2)}, u32[]{:S(2)}) collective-permute-start(bf16[3,64,1024]{2,1,0:T(8,128)(2,1)S(1)} %collective-permute-done.9.refs_3_), channel_id=1, source_target_pairs={{0,16},{16,0},{32,48},{48,32},{64,80},{80,64},{96,112},{112,96},{1... | collective-permute-start | bytes 1179656 | tf_op jit(solution)/shard_map/ppermute | solution.py:55
  49.0 3.7 %collective-permute-start.16 = (bf16[3,64,1024]{2,1,0:T(8,128)(2,1)S(1)}, bf16[3,64,1024]{2,1,0:T(8,128)(2,1)S(1)}, u32[]{:S(2)}, u32[]{:S(2)}) collective-permute-start(bf16[3,64,1024]{2,1,0:T(8,128)(2,1)S(1)} %collective-permute-done.15.refs_2_), channel_id=1, source_target_pairs={{0,16},{16,0},{32,48},{48,32},{64,80},{80,64},{96,112},{112,96},{1... | collective-permute-start | bytes 1179656 | tf_op jit(solution)/shard_map/ppermute | solution.py:55
  49.0 12.8 %collective-permute-start.18 = (bf16[4,64,1024]{2,1,0:T(8,128)(2,1)S(1)}, bf16[4,64,1024]{2,1,0:T(8,128)(2,1)S(1)}, u32[]{:S(2)}, u32[]{:S(2)}) collective-permute-start(bf16[4,64,1024]{2,1,0:T(8,128)(2,1)S(1)} %stack_features.1.refs_0_), channel_id=1, source_target_pairs={{0,8},{1,9},{2,10},{3,11},{4,12},{5,13},{6,14},{7,15},{8,0},{9,1},... | collective-permute-start | bytes 1572872 | tf_op jit(solution)/shard_map/ppermute | solution.py:111
  50.6 13.4 %collective-permute-start.19 = (bf16[4,64,1024]{2,1,0:T(8,128)(2,1)S(1)}, bf16[4,64,1024]{2,1,0:T(8,128)(2,1)S(1)}, u32[]{:S(2)}, u32[]{:S(2)}) collective-permute-start(bf16[4,64,1024]{2,1,0:T(8,128)(2,1)S(1)} %stack_features.1.refs_0_), channel_id=1, source_target_pairs={{0,12},{1,13},{2,14},{3,15},{4,0},{5,1},{6,2},{7,3},{8,4},{9,5},{1... | collective-permute-start | bytes 1572872 | tf_op jit(solution)/shard_map/ppermute | solution.py:111
  57.3 15.2 %collective-permute-start.20 = (bf16[4,64,1024]{2,1,0:T(8,128)(2,1)S(1)}, bf16[4,64,1024]{2,1,0:T(8,128)(2,1)S(1)}, u32[]{:S(2)}, u32[]{:S(2)}) collective-permute-start(bf16[4,64,1024]{2,1,0:T(8,128)(2,1)S(1)} %value_part.6), channel_id=1, source_target_pairs={{0,4},{1,5},{2,6},{3,7},{4,8},{5,9},{6,10},{7,11},{8,12},{9,13},{1... | collective-permute-start | bytes 1572872 | tf_op jit(solution)/shard_map/ppermute | solution.py:111
  59.0 13.6 %collective-permute-start.22 = (bf16[4,64,1024]{2,1,0:T(8,128)(2,1)S(1)}, bf16[4,64,1024]{2,1,0:T(8,128)(2,1)S(1)}, u32[]{:S(2)}, u32[]{:S(2)}) collective-permute-start(bf16[4,64,1024]{2,1,0:T(8,128)(2,1)S(1)} %value_part.7), channel_id=1, source_target_pairs={{0,12},{1,13},{2,14},{3,15},{4,0},{5,1},{6,2},{7,3},{8,4},{9,5},{1... | collective-permute-start | bytes 1572872 | tf_op jit(solution)/shard_map/ppermute | solution.py:111
  61.6 10.9 %collective-permute-start.21 = (bf16[4,64,1024]{2,1,0:T(8,128)(2,1)S(1)}, bf16[4,64,1024]{2,1,0:T(8,128)(2,1)S(1)}, u32[]{:S(2)}, u32[]{:S(2)}) collective-permute-start(bf16[4,64,1024]{2,1,0:T(8,128)(2,1)S(1)} %get-tuple-element.111), channel_id=1, source_target_pairs={{0,8},{1,9},{2,10},{3,11},{4,12},{5,13},{6,14},{7,15},{8,0},{9,1},... | collective-permute-start | bytes 1572872 | tf_op jit(solution)/shard_map/ppermute | solution.py:111
  64.0 20.9 %copy-start.2 = (bf16[1536,1024]{1,0:T(8,128)(2,1)S(1)}, bf16[1536,1024]{1,0:T(8,128)(2,1)}, u32[]{:S(2)}) copy-start(bf16[1536,1024]{1,0:T(8,128)(2,1)} %get-tuple-element.120.whole) | copy-start | bytes 9437188
  73.3 5.2 %collective-permute-start.23 = (bf16[64,1024]{1,0:T(8,128)(2,1)S(1)}, bf16[64,1024]{1,0:T(8,128)(2,1)S(1)}, u32[]{:S(2)}, u32[]{:S(2)}) collective-permute-start(bf16[64,1024]{1,0:T(8,128)(2,1)S(1)} %get-tuple-element.113), channel_id=1, source_target_pairs={{0,1},{1,2},{2,3},{3,0},{4,5},{5,6},{6,7},{7,4},{8,9},{9,10},{10,1... | collective-permute-start | bytes 393224 | tf_op jit(solution)/shard_map/ppermute | solution.py:111
  74.6 6.5 %collective-permute-start.24 = (bf16[64,1024]{1,0:T(8,128)(2,1)S(1)}, bf16[64,1024]{1,0:T(8,128)(2,1)S(1)}, u32[]{:S(2)}, u32[]{:S(2)}) collective-permute-start(bf16[64,1024]{1,0:T(8,128)(2,1)S(1)} %get-tuple-element.114), channel_id=1, source_target_pairs={{0,2},{1,3},{2,0},{3,1},{4,6},{5,7},{6,4},{7,5},{8,10},{9,11},{10,... | collective-permute-start | bytes 393224 | tf_op jit(solution)/shard_map/ppermute | solution.py:111
  77.3 4.1 %collective-permute-start.25 = (bf16[64,1024]{1,0:T(8,128)(2,1)S(1)}, bf16[64,1024]{1,0:T(8,128)(2,1)S(1)}, u32[]{:S(2)}, u32[]{:S(2)}) collective-permute-start(bf16[64,1024]{1,0:T(8,128)(2,1)S(1)} %get-tuple-element.115), channel_id=1, source_target_pairs={{0,3},{1,0},{2,1},{3,2},{4,7},{5,4},{6,5},{7,6},{8,11},{9,8},{10,9... | collective-permute-start | bytes 393224 | tf_op jit(solution)/shard_map/ppermute | solution.py:111
  82.1 7.8 %collective-permute-start.26 = (bf16[2,64,128]{2,1,0:T(8,128)(2,1)S(1)}, bf16[2,64,128]{2,1,0:T(8,128)(2,1)S(1)}, u32[]{:S(2)}, u32[]{:S(2)}) collective-permute-start(bf16[2,64,128]{2,1,0:T(8,128)(2,1)S(1)} %get-tuple-element.117), channel_id=1, source_target_pairs={{0,32},{16,48},{32,64},{48,80},{64,96},{80,112},{96,0},{112,16},{1... | collective-permute-start | bytes 98312 | tf_op jit(solution)/shard_map/ppermute | solution.py:51
  82.2 7.7 %collective-permute-start.27 = (bf16[2,64,128]{2,1,0:T(8,128)(2,1)S(1)}, bf16[2,64,128]{2,1,0:T(8,128)(2,1)S(1)}, u32[]{:S(2)}, u32[]{:S(2)}) collective-permute-start(bf16[2,64,128]{2,1,0:T(8,128)(2,1)S(1)} %get-tuple-element.118), channel_id=1, source_target_pairs={{0,64},{16,80},{32,96},{48,112},{64,0},{80,16},{96,32},{112,48},{1... | collective-permute-start | bytes 98312 | tf_op jit(solution)/shard_map/ppermute | solution.py:51
  82.8 7.1 %collective-permute-start.28 = (bf16[2,64,128]{2,1,0:T(8,128)(2,1)S(1)}, bf16[2,64,128]{2,1,0:T(8,128)(2,1)S(1)}, u32[]{:S(2)}, u32[]{:S(2)}) collective-permute-start(bf16[2,64,128]{2,1,0:T(8,128)(2,1)S(1)} %get-tuple-element.119), channel_id=1, source_target_pairs={{0,96},{16,112},{32,0},{48,16},{64,32},{80,48},{96,64},{112,80},{1... | collective-permute-start | bytes 98312 | tf_op jit(solution)/shard_map/ppermute | solution.py:51
  89.9 4.7 %collective-permute-start.29 = (bf16[64,128]{1,0:T(8,128)(2,1)S(1)}, bf16[64,128]{1,0:T(8,128)(2,1)S(1)}, u32[]{:S(2)}, u32[]{:S(2)}) collective-permute-start(bf16[64,128]{1,0:T(8,128)(2,1)S(1)} %get-tuple-element.145), channel_id=1, source_target_pairs={{0,16},{16,0},{32,48},{48,32},{64,80},{80,64},{96,112},{112,96},{1... | collective-permute-start | bytes 49160 | tf_op jit(solution)/shard_map/ppermute | solution.py:55
  93.8 1.2 %collective-permute-start.30 = (bf16[64,128]{1,0:T(8,128)(2,1)S(1)}, bf16[64,128]{1,0:T(8,128)(2,1)S(1)}, u32[]{:S(2)}, u32[]{:S(2)}) collective-permute-start(bf16[64,128]{1,0:T(8,128)(2,1)S(1)} %get-tuple-element.143), channel_id=1, source_target_pairs={{0,16},{16,0},{32,48},{48,32},{64,80},{80,64},{96,112},{112,96},{1... | collective-permute-start | bytes 49160 | tf_op jit(solution)/shard_map/ppermute | solution.py:55
  93.9 1.2 %collective-permute-start.31 = (bf16[64,128]{1,0:T(8,128)(2,1)S(1)}, bf16[64,128]{1,0:T(8,128)(2,1)S(1)}, u32[]{:S(2)}, u32[]{:S(2)}) collective-permute-start(bf16[64,128]{1,0:T(8,128)(2,1)S(1)} %get-tuple-element.141), channel_id=1, source_target_pairs={{0,16},{16,0},{32,48},{48,32},{64,80},{80,64},{96,112},{112,96},{1... | collective-permute-start | bytes 49160 | tf_op jit(solution)/shard_map/ppermute | solution.py:55
  94.3 1.2 %collective-permute-start.32 = (bf16[64,128]{1,0:T(8,128)(2,1)S(1)}, bf16[64,128]{1,0:T(8,128)(2,1)S(1)}, u32[]{:S(2)}, u32[]{:S(2)}) collective-permute-start(bf16[64,128]{1,0:T(8,128)(2,1)S(1)} %get-tuple-element.139), channel_id=1, source_target_pairs={{0,16},{16,0},{32,48},{48,32},{64,80},{80,64},{96,112},{112,96},{1... | collective-permute-start | bytes 49160 | tf_op jit(solution)/shard_map/ppermute | solution.py:55

commit v3 on v2

--- a/solution.py
+++ b/solution.py
@@ -245,7 +245,7 @@
     pieces = refs[:N_CTX]
     table = refs[N_CTX : N_CTX + 4]
     hr, hi, hn = refs[N_CTX + 4 : N_CTX + 7]
-    grads, out_re, out_im, out_n, whole = refs[N_CTX + 7 :]
+    grads, grad_taps, whole = refs[N_CTX + 7 :]
     chans, span = pieces[0].shape[-2:]
     n = N_CTX * span
     for p in range(N_CTX):
@@ -256,12 +256,10 @@
     re, im, nyq = spectrum(jnp.concatenate([product, grad_conv], axis=0), table, n)
     ur, gr, ui, gi, un, gn = re[:chans], re[chans:], im[:chans], im[chans:], nyq[:chans], nyq[chans:]
     hr, hi, hn = hr[...], hi[...], hn[...]
-    out_re[...] = gr * ur + gi * ui
-    out_im[...] = gi * ur - gr * ui
-    out_n[...] = gn * un
-    spec_re = jnp.concatenate([ur * hr - ui * hi, gr * hr + gi * hi], axis=0)
-    spec_im = jnp.concatenate([ur * hi + ui * hr, gi * hr - gr * hi], axis=0)
-    out = inverse(spec_re, spec_im, jnp.concatenate([un * hn, gn * hn], axis=0), table, n)
+    spec_re = jnp.concatenate([ur * hr - ui * hi, gr * hr + gi * hi, gr * ur + gi * ui], axis=0)
+    spec_im = jnp.concatenate([ur * hi + ui * hr, gi * hr - gr * hi, gi * ur - gr * ui], axis=0)
+    out = inverse(spec_re, spec_im, jnp.concatenate([un * hn, gn * hn, gn * un], axis=0), table, n)
+    out, grad_taps[...] = out[: 2 * chans], out[2 * chans :].astype(BF16)
     grads[0] = (whole[2].astype(F32) * out[:chans]).astype(BF16)
     grads[1] = (out[chans:] * whole[1].astype(F32)).astype(BF16)
     grads[2] = (out[chans:] * whole[0].astype(F32)).astype(BF16)
@@ -272,31 +270,14 @@
     n = N_CTX * span
     return pl.pallas_call(
         conv_kernel,
-        out_shape=[like(3, chans, n)] + [like(chans, n, dtype=F32)] * 2 + [like(chans, 1, dtype=F32)],
+        out_shape=[like(3, chans, n), like(chans, n)],
         in_specs=[SCALAR] + [ON_CHIP] * (N_CTX + 7),
-        out_specs=[ON_CHIP] * 4,
+        out_specs=[ON_CHIP] * 2,
         scratch_shapes=[pltpu.VMEM((4, chans, n), BF16)],
         compiler_params=vmem(20),
         cost_estimate=pl.CostEstimate(flops=32 * chans * n * n, bytes_accessed=8 * MIB, transcendentals=0),
         name="convolutions",
     )(me, *pieces, *table, *taps_spec)
-
-
-def taps_grad_kernel(*refs):
-    table, (re, im, nyq), out = refs[:4], refs[4:7], refs[7]
-    out[...] = inverse(re[...], im[...], nyq[...], table, out.shape[1]).astype(BF16)
-
-
-def taps_grad(spec, table):
-    return pl.pallas_call(
-        taps_grad_kernel,
-        out_shape=like(*spec[0].shape),
-        in_specs=[ON_CHIP] * 7,
-        out_specs=ON_CHIP,
-        compiler_params=vmem(16),
-        cost_estimate=pl.CostEstimate(flops=16 * MIB * 64, bytes_accessed=8 * MIB, transcendentals=0),
-        name="taps_grad",
-    )(*table, *spec)
 
 
 def gather_pieces(mine):
@@ -334,14 +315,16 @@
         assemble_kernel(which, me, *pieces, whole)
         copy = pltpu.make_async_copy(whole, far_whole, sem)
         copy.start()
-    for s, part in zip(steps, parts, strict=True):
+    lhs = []
+    for s in steps:
         at = (place(me, first=True) + s) % N_RING
-        lhs = []
         for k in range(N_RING):
             w = weights[group(me, at, k)]
             lhs.append(jnp.concatenate([w[b] for b in range(3)], axis=1))
-        res = dot(jnp.concatenate(lhs, axis=0), whole[...])
-        part[...] = res.astype(BF16).reshape(part.shape)
+    res = dot(jnp.concatenate(lhs, axis=0), whole[...]).astype(BF16)
+    res = res.reshape(len(steps), *parts[0].shape)
+    for i, part in enumerate(parts):
+        part[...] = res[i]
     if which:
         copy.wait()
 
@@ -363,45 +346,50 @@
         input_output_aliases={2: len(steps)} if which else {},
         compiler_params=vmem(16),
         cost_estimate=pl.CostEstimate(
-            flops=2 * len(steps) * rows * width * n, bytes_accessed=MIB // 4, transcendentals=0
+            flops=24 * len(steps) * rows * width * n, bytes_accessed=2 * MIB, transcendentals=0
         ),
         name="value_part",
     )(me, weights, whole, *pieces)
 
 
-def weight_kernel(me, whole, *refs):
-    feats, out, res, sems = refs[:N_RING], refs[N_RING], refs[N_RING + 1], refs[N_RING + 2]
+def weight_kernel(steps, me, whole, *refs):
+    feats, (out, res, sems) = refs[: len(steps)], refs[-3:]
     _, rows, n = feats[0].shape
     width = out.shape[-1]
     copies = []
-    for s in range(N_RING):
+    for i, s in enumerate(steps):
         at = (place(me, first=True) + N_RING - s) % N_RING
-        tall = dot_t(feats[s][...].reshape(N_RING * rows, n), whole[...]).astype(BF16)
+        tall = dot_t(feats[i][...].reshape(N_RING * rows, n), whole[...]).astype(BF16)
         for k in range(N_RING):
             for b in range(3):
-                res[s, k, b] = tall[k * rows : (k + 1) * rows, b * width : (b + 1) * width]
-            copies.append(pltpu.make_async_copy(res.at[s, k], out.at[group(me, at, k)], sems.at[s, k]))
+                res[i, k, b] = tall[k * rows : (k + 1) * rows, b * width : (b + 1) * width]
+            copies.append(pltpu.make_async_copy(res.at[i, k], out.at[group(me, at, k)], sems.at[i, k]))
             copies[-1].start()
     for copy in copies:
         copy.wait()
 
 
-def weight_grad(me, whole, feats):
+def weight_grad(me, whole, feats, steps, begun=None):
     _, rows, n = feats[0].shape
     width = whole.shape[0] // 3
-    return pl.pallas_call(
-        weight_kernel,
+    n_steps = len(steps)
+    more = [] if begun is None else [begun]
+    return pl.pallas_call(
+        functools.partial(weight_kernel, steps),
         out_shape=pltpu.HBM((N_RING * N_RING, 3, rows, width), BF16),
-        in_specs=[SCALAR] + [ON_CHIP] * (N_RING + 1),
+        in_specs=[SCALAR] + [ON_CHIP] * (n_steps + 1) + [FAR] * len(more),
         out_specs=FAR,
         scratch_shapes=[
-            pltpu.VMEM((N_RING, N_RING, 3, rows, width), BF16),
-            pltpu.SemaphoreType.DMA((N_RING, N_RING)),
+            pltpu.VMEM((n_steps, N_RING, 3, rows, width), BF16),
+            pltpu.SemaphoreType.DMA((n_steps, N_RING)),
         ],
+        input_output_aliases={n_steps + 2: 0} if more else {},
         compiler_params=vmem(18),
-        cost_estimate=pl.CostEstimate(flops=96 * rows * width * n, bytes_accessed=8 * MIB, transcendentals=0),
+        cost_estimate=pl.CostEstimate(
+            flops=24 * n_steps * rows * width * n, bytes_accessed=2 * MIB, transcendentals=0
+        ),
         name="weight_grad",
-    )(me, whole, *feats)
+    )(me, whole, *feats, *more)
 
 
 def first_sum_kernel(me, *refs):
@@ -485,30 +473,29 @@
     along, spec_taps = tie(along, spec_taps)
     *table, hr, hi, hn = spec_taps
     pieces = [a[0] for a in along] + [swap_core(a[1]) for a in along]
-    grads, *spec = convolutions(me, pieces, table, (hr, hi, hn))
-    pieces, grads = tie(pieces, grads)
-    near = gather_start(grads)
+    grads, grad_taps = convolutions(me, pieces, table, (hr, hi, hn))
+    own, sibling, next1, next2 = gather_start(grads)
+    sibling, pieces = tie(sibling, pieces)
+    last = spin(next1)
     feats = join_features(me, pieces)
     feats = [feats] + [shift_ring(feats, s, first=False) for s in (1, 2, 3)]
-    far, feats = tie(near[2], feats)
-    last = spin(far)
+    last, feats = tie(last, feats)
+    pieces = (own, sibling, next1, next2, swap_core(next1), swap_core(next2))
+    whole = assemble(me, pieces, (0, 1, 2, 3, 5, 6))
+    *sent, whole, far_whole = value_part(me, weights, whole, (1, 2, 3), (last, swap_core(last)), (4, 7))
+    parts = [shift_ring(p, s, first=True) for p, s in zip(sent, (1, 2, 3), strict=True)]
     feats = stack(me, feats)
-    grad_taps = taps_grad(spec, table)
-    last, (grad_taps, feats) = tie(last, (grad_taps, feats))
-    theirs = [swap_core(a) for a in near[2:]]
-    feats = [feats] + [shift_ring(feats, s, first=True) for s in (1, 2, 3)]
-    whole = assemble(me, near + theirs, (0, 1, 2, 3, 5, 6))
-    part2, whole, far_whole = value_part(me, weights, whole, (2,), (last, swap_core(last)), (4, 7))
-    (part1,) = value_part(me, weights, whole, (1,))
-    (part3,) = value_part(me, weights, whole, (3,))
-    whole, feats = tie(whole, feats)
-    (part0,) = value_part(me, weights, whole, (0,))
-    parts = [part0] + [shift_ring(p, s, first=True) for p, s in ((part1, 1), (part2, 2), (part3, 3))]
+    feats1, feats3 = shift_ring(feats, 1, first=True), shift_ring(feats, 3, first=True)
+    parts = [*value_part(me, weights, whole, (0,)), *parts]
     parts = first_sum(me, parts)
+    parts, (feats1, feats3) = tie(parts, (feats1, feats3))
     parts = [parts[0]] + [shift_ring(parts[s], s, first=False) for s in (1, 2, 3)]
+    feats = [feats, feats1, shift_ring(feats, 2, first=True), feats3]
+    grad_w = weight_grad(me, far_whole, [feats[s] for s in (0, 1, 3)], (0, 1, 3))
+    parts, grad_w = tie(parts, grad_w)
     ready = sum_parts(me, parts)
-    grad_w = weight_grad(me, far_whole, feats)
     along = [ready[0]] + [shift_x(ready[s], s) for s in (1, 2, 3)]
+    grad_w = weight_grad(me, far_whole, [feats[2]], (2,), grad_w)
     along, grad_w = tie(along, grad_w)
     grad_features = finish(me, [a[0] for a in along] + [swap_core(a[1]) for a in along])
     return grad_features, grad_w.transpose(0, 2, 1, 3), grad_taps.reshape(filter_taps.shape)

time: 98.1 us -> 92.8 us (0.946); the launches traced: 96.8 us -> 92.7 us
  starting transfers between devices: 44.9 us -> 41.8 us
  Pallas kernels: 30.4 us -> 28.2 us
  waiting for transfers between devices: 19.6 us -> 20.7 us
    ppermute x12, starting transfers between devices: 14.4 us -> 8.44 us  [swap_core(): return lax.ppermute(a, 'ctx', [(i, i ^ 1) for i in range(N_CTX)])]
    pallas_call x4 -> x2, Pallas kernels: 7.59 us -> 4.73 us  [value_part(): pl.pallas_call(functools.partial(value_kernel, steps, which), out_shape=s...]
    ppermute x3, starting transfers between devices: 3.82 us -> 6.2 us  [spin(): return lax.ppermute(a, 'ctx', pairs)]
    ppermute x6, starting transfers between devices: 8.45 us -> 9.97 us  [shift_x(): lax.ppermute(a, 'ctx', [(i, (i + 2 * steps) % N_CTX) for i in range(N_CTX)])]
    ppermute x3, waiting for transfers between devices: 2.04 us -> 3.5 us  [spin(): return lax.ppermute(a, 'ctx', pairs)]
    ppermute x12, waiting for transfers between devices: 15.2 us -> 13.9 us  [shift_ring(): return lax.ppermute(a, ('ctx', 'tp'), pairs)]
  transfers between devices with their start and end apart: 33 -> 33, of which waited for: 17 -> 20; matrix products, arithmetic and copies ran while one was open for 0% -> 0% of each run, Pallas kernels for 22% -> 18%
where the time goes in v3:
time: 92.8 us; the launch traced here: 92.7 us
  starting transfers between devices  41.8 us (45%)
  Pallas kernels  28.2 us (30%)
  waiting for transfers between devices  20.7 us (22%)
  local copies, waits for them, and re-layouts  0.98 us (1%)
    ppermute x12, starting transfers between devices, shift_ring(): return lax.ppermute(a, ('ctx', 'tp'), pairs)  17.2 us
    ppermute x12, waiting for transfers between devices, shift_ring(): return lax.ppermute(a, ('ctx', 'tp'), pairs)  13.9 us
    ppermute x6, starting transfers between devices, shift_x(): lax.ppermute(a, 'ctx', [(i, (i + 2 * steps) % N_CTX) for i in range(N_CTX)])  9.97 us
    ppermute x12, starting transfers between devices, swap_core(): return lax.ppermute(a, 'ctx', [(i, i ^ 1) for i in range(N_CTX)])  8.44 us
    pallas_call x2, Pallas kernels, weight_grad(): pl.pallas_call(functools.partial(weight_kernel, steps), out_shape=pltpu.H...  6.54 us
    ppermute x3, starting transfers between devices, spin(): return lax.ppermute(a, 'ctx', pairs)  6.2 us
    pallas_call x1, Pallas kernels, convolutions(): pl.pallas_call(conv_kernel, out_shape=[like(3, chans, n), like(chans, n)]...  5.21 us
    pallas_call x1, Pallas kernels, taps_spectrum(): pl.pallas_call(taps_kernel, out_shape=[like(n, n)] * 4 + [like(chans, n,...  5.07 us
  transfers between devices with their start and end apart: 33, of which 20 were waited for; matrix products, arithmetic and copies ran while one was open for 0% of the time, Pallas kernels for 18%

profile of v3, /device:TPU:1, one launch (start us, length us, event | category | flops | bytes accessed | tf_op | source)
XLA Modules:
  0.0 92.7 jit_solution(3375044203212115836)
XLA Ops:
  0.7 2.0 %prepare.1 = (bf16[2,5,64,128]{3,2,1,0:T(8,128)(2,1)S(1)}, bf16[2,5,64,128]{3,2,1,0:T(8,128)(2,1)S(1)}, bf16[2,5,64,128]{3,2,1,0:T(8,128)(2,1)S(1)}, bf16[2,5,64,128]{3,2,1,0:T(8,128)(2,1)S(1)}) custom-call(s32[2]{0:T(128)S(1)} %pad_add_fusion.me, bf16[128,512]{1,0:T(8,128)(2,1)} %refs_0_.2, bf16[128,512]{1,0:T(8,128)(2,1)} %refs_1_.2, ...), custom_call_target="tpu_custom_call" | custom-call | tf_op jit(solution)/shard_map/prepare/pallas_call | solution.py:139
  2.7 2.1 %collective-permute-start = (bf16[2,5,64,128]{3,2,1,0:T(8,128)(2,1)S(1)}, bf16[2,5,64,128]{3,2,1,0:T(8,128)(2,1)S(1)}, u32[]{:S(2)}, u32[]{:S(2)}) collective-permute-start(bf16[2,5,64,128]{3,2,1,0:T(8,128)(2,1)S(1)} %get-tuple-element.71), channel_id=1, source_target_pairs={{0,32},{16,48},{32,64},{48,80},{64,96},{80,112},{96,0},{112,16},{1... | collective-permute-start | bytes 491528 | tf_op jit(solution)/shard_map/ppermute | solution.py:51
  4.8 2.5 %collective-permute-start.1 = (bf16[2,5,64,128]{3,2,1,0:T(8,128)(2,1)S(1)}, bf16[2,5,64,128]{3,2,1,0:T(8,128)(2,1)S(1)}, u32[]{:S(2)}, u32[]{:S(2)}) collective-permute-start(bf16[2,5,64,128]{3,2,1,0:T(8,128)(2,1)S(1)} %get-tuple-element.72), channel_id=1, source_target_pairs={{0,64},{16,80},{32,96},{48,112},{64,0},{80,16},{96,32},{112,48},{1... | collective-permute-start | bytes 491528 | tf_op jit(solution)/shard_map/ppermute | solution.py:51
  7.3 1.2 %collective-permute-start.2 = (bf16[2,5,64,128]{3,2,1,0:T(8,128)(2,1)S(1)}, bf16[2,5,64,128]{3,2,1,0:T(8,128)(2,1)S(1)}, u32[]{:S(2)}, u32[]{:S(2)}) collective-permute-start(bf16[2,5,64,128]{3,2,1,0:T(8,128)(2,1)S(1)} %get-tuple-element.73), channel_id=1, source_target_pairs={{0,96},{16,112},{32,0},{48,16},{64,32},{80,48},{96,64},{112,80},{1... | collective-permute-start | bytes 491528 | tf_op jit(solution)/shard_map/ppermute | solution.py:51
  8.4 0.9 copy-done.2
  9.3 5.1 %taps_spectrum.1 = (bf16[1024,1024]{1,0:T(8,128)(2,1)S(1)}, bf16[1024,1024]{1,0:T(8,128)(2,1)S(1)}, bf16[1024,1024]{1,0:T(8,128)(2,1)S(1)}, bf16[1024,1024]{1,0:...) custom-call(bf16[1024,1024]{1,0:T(8,128)(2,1)} %constant.17.clone.refs_0_, ...), custom_call_target="tpu_custom_call" | custom-call | flops 536870912 | bytes 8388608 | tf_op jit(solution)/shard_map/taps_spectrum/pallas_call | solution.py:232
  14.5 1.6 %collective-permute-start.3 = (bf16[5,64,128]{2,1,0:T(8,128)(2,1)S(1)}, bf16[5,64,128]{2,1,0:T(8,128)(2,1)S(1)}, u32[]{:S(2)}, u32[]{:S(2)}) collective-permute-start(bf16[5,64,128]{2,1,0:T(8,128)(2,1)S(1)} %get-tuple-element.143), channel_id=1, source_target_pairs={{0,16},{16,0},{32,48},{48,32},{64,80},{80,64},{96,112},{112,96},{1... | collective-permute-start | bytes 245768 | tf_op jit(solution)/shard_map/ppermute | solution.py:55
  16.1 0.1 collective-permute-start.4
  16.2 0.4 collective-permute-start.5
  16.6 0.1 collective-permute-start.6
  16.7 0.3 collective-permute-done.3.refs_4_
  17.0 0.4 collective-permute-done.4.refs_5_
  17.4 0.2 collective-permute-done.5.refs_6_
  17.5 0.4 collective-permute-done.6.refs_7_
  17.9 5.2 %convolutions.1 = (bf16[3,64,1024]{2,1,0:T(8,128)(2,1)S(1)}, bf16[64,1024]{1,0:T(8,128)(2,1)}) custom-call(s32[2]{0:T(128)S(1)} %pad_add_fusion.me, bf16[5,64,128]{2,1,0:T(8,128)(2,1)S(1)} %get-tuple-element.94.refs_0_, bf16[5,64,128]{2,1,0:T(8,128)(2,1)S(1)} %get-tuple-element.95.refs_1_, bf16[5,64,128]{2,1,0:T(8,128)(2,1)S(1)} %get-tuple-element.96.refs_2_, ...), custom_call_target="tpu_custom_call" | custom-call | flops 2147483648 | bytes 8388608 | tf_op jit(solution)/shard_map/convolutions/pallas_call | solution.py:271
  23.1 0.1 collective-permute-start.7
  23.2 1.9 %collective-permute-start.8 = (bf16[3,64,1024]{2,1,0:T(8,128)(2,1)S(1)}, bf16[3,64,1024]{2,1,0:T(8,128)(2,1)S(1)}, u32[]{:S(2)}, u32[]{:S(2)}) collective-permute-start(bf16[3,64,1024]{2,1,0:T(8,128)(2,1)S(1)} %get-tuple-element.92.refs_0_), channel_id=1, source_target_pairs={{0,32},{16,112},{32,64},{48,16},{64,96},{80,48},{96,0},{112,80},{1... | collective-permute-start | bytes 1179656 | tf_op jit(solution)/shard_map/ppermute | solution.py:67
  25.1 1.6 %collective-permute-start.9 = (bf16[3,64,1024]{2,1,0:T(8,128)(2,1)S(1)}, bf16[3,64,1024]{2,1,0:T(8,128)(2,1)S(1)}, u32[]{:S(2)}, u32[]{:S(2)}) collective-permute-start(bf16[3,64,1024]{2,1,0:T(8,128)(2,1)S(1)} %collective-permute-done.7.refs_1_), channel_id=1, source_target_pairs={{0,32},{16,112},{32,64},{48,16},{64,96},{80,48},{96,0},{112,80},{1... | collective-permute-start | bytes 1179656 | tf_op jit(solution)/shard_map/ppermute | solution.py:67
  26.7 3.5 %collective-permute-done.8.refs_2_ = bf16[3,64,1024]{2,1,0:T(8,128)(2,1)S(1)} collective-permute-done((bf16[3,64,1024]{2,1,0:T(8,128)(2,1)S(1)}, bf16[3,64,1024]{2,1,0:T(8,128)(2,1)S(1)}, u32[]{:S(2)}, u32[]{:S(2)}) %collective-permute-start.8) | collective-permute-done | bytes 393248 | tf_op jit(solution)/shard_map/ppermute | solution.py:67
  30.2 2.8 %collective-permute-start.12 = (bf16[3,64,1024]{2,1,0:T(8,128)(2,1)S(1)}, bf16[3,64,1024]{2,1,0:T(8,128)(2,1)S(1)}, u32[]{:S(2)}, u32[]{:S(2)}) collective-permute-start(bf16[3,64,1024]{2,1,0:T(8,128)(2,1)S(1)} %collective-permute-done.8.refs_2_), channel_id=1, source_target_pairs={{0,32},{16,112},{32,64},{48,16},{64,96},{80,48},{96,0},{112,80},{1... | collective-permute-start | bytes 1179656 | tf_op jit(solution)/shard_map/ppermute | solution.py:67
  32.9 0.6 join_features.1.refs_0_
  33.5 1.5 %collective-permute-start.13 = (bf16[64,1024]{1,0:T(8,128)(2,1)S(1)}, bf16[64,1024]{1,0:T(8,128)(2,1)S(1)}, u32[]{:S(2)}, u32[]{:S(2)}) collective-permute-start(bf16[64,1024]{1,0:T(8,128)(2,1)S(1)} %join_features.1.refs_0_), channel_id=1, source_target_pairs={{0,1},{1,2},{2,3},{3,0},{4,5},{5,6},{6,7},{7,4},{8,9},{9,10},{10,1... | collective-permute-start | bytes 393224 | tf_op jit(solution)/shard_map/ppermute | solution.py:111
  35.0 2.6 %collective-permute-start.14 = (bf16[64,1024]{1,0:T(8,128)(2,1)S(1)}, bf16[64,1024]{1,0:T(8,128)(2,1)S(1)}, u32[]{:S(2)}, u32[]{:S(2)}) collective-permute-start(bf16[64,1024]{1,0:T(8,128)(2,1)S(1)} %join_features.1.refs_0_), channel_id=1, source_target_pairs={{0,2},{1,3},{2,0},{3,1},{4,6},{5,7},{6,4},{7,5},{8,10},{9,11},{10,... | collective-permute-start | bytes 393224 | tf_op jit(solution)/shard_map/ppermute | solution.py:111
  37.6 1.1 %collective-permute-start.15 = (bf16[64,1024]{1,0:T(8,128)(2,1)S(1)}, bf16[64,1024]{1,0:T(8,128)(2,1)S(1)}, u32[]{:S(2)}, u32[]{:S(2)}) collective-permute-start(bf16[64,1024]{1,0:T(8,128)(2,1)S(1)} %join_features.1.refs_0_), channel_id=1, source_target_pairs={{0,3},{1,0},{2,1},{3,2},{4,7},{5,4},{6,5},{7,6},{8,11},{9,8},{10,9... | collective-permute-start | bytes 393224 | tf_op jit(solution)/shard_map/ppermute | solution.py:111
  38.7 0.4 collective-permute-done.13.refs_1_
  39.1 1.2 %collective-permute-start.10 = (bf16[3,64,1024]{2,1,0:T(8,128)(2,1)S(1)}, bf16[3,64,1024]{2,1,0:T(8,128)(2,1)S(1)}, u32[]{:S(2)}, u32[]{:S(2)}) collective-permute-start(bf16[3,64,1024]{2,1,0:T(8,128)(2,1)S(1)} %collective-permute-done.8.refs_2_), channel_id=1, source_target_pairs={{0,16},{16,0},{32,48},{48,32},{64,80},{80,64},{96,112},{112,96},{1... | collective-permute-start | bytes 1179656 | tf_op jit(solution)/shard_map/ppermute | solution.py:55
  40.4 1.3 %collective-permute-done.14.refs_2_ = bf16[64,1024]{1,0:T(8,128)(2,1)S(1)} collective-permute-done((bf16[64,1024]{1,0:T(8,128)(2,1)S(1)}, bf16[64,1024]{1,0:T(8,128)(2,1)S(1)}, u32[]{:S(2)}, u32[]{:S(2)}) %collective-permute-start.14) | collective-permute-done | bytes 131104 | tf_op jit(solution)/shard_map/ppermute | solution.py:111
  41.7 2.1 %collective-permute-start.16 = (bf16[3,64,1024]{2,1,0:T(8,128)(2,1)S(1)}, bf16[3,64,1024]{2,1,0:T(8,128)(2,1)S(1)}, u32[]{:S(2)}, u32[]{:S(2)}) collective-permute-start(bf16[3,64,1024]{2,1,0:T(8,128)(2,1)S(1)} %collective-permute-done.12.refs_2_), channel_id=1, source_target_pairs={{0,16},{16,0},{32,48},{48,32},{64,80},{80,64},{96,112},{112,96},{1... | collective-permute-start | bytes 1179656 | tf_op jit(solution)/shard_map/ppermute | solution.py:55
  43.8 0.7 assemble.1.refs_1_
  44.6 0.6 collective-permute-done.16.refs_3_
  45.2 3.2 %value_part.2 = (bf16[4,64,1024]{2,1,0:T(8,128)(2,1)S(1)}, bf16[4,64,1024]{2,1,0:T(8,128)(2,1)S(1)}, bf16[4,64,1024]{2,1,0:T(8,128)(2,1)S(1)}, bf16[1536,1024]{1,0:T(8,128)(2,1)S(1)}, bf16[1536,1024]{1,0:T(8,128)(2,1)}) custom-call(s32[2]{0:T(128)S(1)} %pad_add_fusion.me, bf16[16,3,64,512]{3,2,1,0:T(8,128)(2,1)S(1)} %bitcast.38, ...), custom_call_target="tpu_custom_call", output_to_operand_aliasing={{3}: (2, {})} | custom-call | flops 2415919104 | bytes 2097152 | tf_op jit(solution)/shard_map/value_part/pallas_call | solution.py:340
  48.4 0.9 collective-permute-start.17
  49.3 2.5 %collective-permute-start.18 = (bf16[4,64,1024]{2,1,0:T(8,128)(2,1)S(1)}, bf16[4,64,1024]{2,1,0:T(8,128)(2,1)S(1)}, u32[]{:S(2)}, u32[]{:S(2)}) collective-permute-start(bf16[4,64,1024]{2,1,0:T(8,128)(2,1)S(1)} %get-tuple-element.105), channel_id=1, source_target_pairs={{0,8},{1,9},{2,10},{3,11},{4,12},{5,13},{6,14},{7,15},{8,0},{9,1},... | collective-permute-start | bytes 1572872 | tf_op jit(solution)/shard_map/ppermute | solution.py:111
  51.8 0.6 collective-permute-start.19
  52.4 0.6 stack_features.1.refs_0_
  53.0 1.0 %collective-permute-start.20 = (bf16[4,64,1024]{2,1,0:T(8,128)(2,1)S(1)}, bf16[4,64,1024]{2,1,0:T(8,128)(2,1)S(1)}, u32[]{:S(2)}, u32[]{:S(2)}) collective-permute-start(bf16[4,64,1024]{2,1,0:T(8,128)(2,1)S(1)} %stack_features.1.refs_0_), channel_id=1, source_target_pairs={{0,4},{1,5},{2,6},{3,7},{4,8},{5,9},{6,10},{7,11},{8,12},{9,13},{1... | collective-permute-start | bytes 1572872 | tf_op jit(solution)/shard_map/ppermute | solution.py:111
  53.9 1.8 %collective-permute-start.21 = (bf16[4,64,1024]{2,1,0:T(8,128)(2,1)S(1)}, bf16[4,64,1024]{2,1,0:T(8,128)(2,1)S(1)}, u32[]{:S(2)}, u32[]{:S(2)}) collective-permute-start(bf16[4,64,1024]{2,1,0:T(8,128)(2,1)S(1)} %stack_features.1.refs_0_), channel_id=1, source_target_pairs={{0,12},{1,13},{2,14},{3,15},{4,0},{5,1},{6,2},{7,3},{8,4},{9,5},{1... | collective-permute-start | bytes 1572872 | tf_op jit(solution)/shard_map/ppermute | solution.py:111
  55.7 2.5 %collective-permute-done.17.refs_1_ = bf16[4,64,1024]{2,1,0:T(8,128)(2,1)S(1)} collective-permute-done((bf16[4,64,1024]{2,1,0:T(8,128)(2,1)S(1)}, bf16[4,64,1024]{2,1,0:T(8,128)(2,1)S(1)}, u32[]{:S(2)}, u32[]{:S(2)}) %collective-permute-start.17) | collective-permute-done | bytes 524320 | tf_op jit(solution)/shard_map/ppermute | solution.py:111
  58.2 0.4 collective-permute-start.28
  58.6 1.5 %value_part.3.refs_0_ = bf16[4,64,1024]{2,1,0:T(8,128)(2,1)S(1)} custom-call(s32[2]{0:T(128)S(1)} %pad_add_fusion.me, bf16[16,3,64,512]{3,2,1,0:T(8,128)(2,1)S(1)} %bitcast.39, bf16[1536,1024]{1,0:T(8,128)(2,1)S(1)} %get-tuple-element.103.refs_1_), custom_call_target="tpu_custom_call" | custom-call | flops 805306368 | bytes 2097152 | tf_op jit(solution)/shard_map/value_part/pallas_call | solution.py:340
  60.1 4.2 %collective-permute-done.18.refs_2_ = bf16[4,64,1024]{2,1,0:T(8,128)(2,1)S(1)} collective-permute-done((bf16[4,64,1024]{2,1,0:T(8,128)(2,1)S(1)}, bf16[4,64,1024]{2,1,0:T(8,128)(2,1)S(1)}, u32[]{:S(2)}, u32[]{:S(2)}) %collective-permute-start.18) | collective-permute-done | bytes 524320 | tf_op jit(solution)/shard_map/ppermute | solution.py:111
  64.3 0.1 collective-permute-done.19.refs_3_
  64.4 0.8 first_sum.1
  65.3 4.2 %collective-permute-done.20.refs_1_ = bf16[4,64,1024]{2,1,0:T(8,128)(2,1)S(1)} collective-permute-done((bf16[4,64,1024]{2,1,0:T(8,128)(2,1)S(1)}, bf16[4,64,1024]{2,1,0:T(8,128)(2,1)S(1)}, u32[]{:S(2)}, u32[]{:S(2)}) %collective-permute-start.20) | collective-permute-done | bytes 524320 | tf_op jit(solution)/shard_map/ppermute | solution.py:111
  69.4 0.6 collective-permute-done.21.refs_2_
  70.1 1.3 %collective-permute-start.22 = (bf16[64,1024]{1,0:T(8,128)(2,1)S(1)}, bf16[64,1024]{1,0:T(8,128)(2,1)S(1)}, u32[]{:S(2)}, u32[]{:S(2)}) collective-permute-start(bf16[64,1024]{1,0:T(8,128)(2,1)S(1)} %get-tuple-element.116), channel_id=1, source_target_pairs={{0,1},{1,2},{2,3},{3,0},{4,5},{5,6},{6,7},{7,4},{8,9},{9,10},{10,1... | collective-permute-start | bytes 393224 | tf_op jit(solution)/shard_map/ppermute | solution.py:111
  71.4 2.6 %collective-permute-start.23 = (bf16[64,1024]{1,0:T(8,128)(2,1)S(1)}, bf16[64,1024]{1,0:T(8,128)(2,1)S(1)}, u32[]{:S(2)}, u32[]{:S(2)}) collective-permute-start(bf16[64,1024]{1,0:T(8,128)(2,1)S(1)} %get-tuple-element.117), channel_id=1, source_target_pairs={{0,2},{1,3},{2,0},{3,1},{4,6},{5,7},{6,4},{7,5},{8,10},{9,11},{10,... | collective-permute-start | bytes 393224 | tf_op jit(solution)/shard_map/ppermute | solution.py:111
  74.0 1.1 %collective-permute-start.24 = (bf16[64,1024]{1,0:T(8,128)(2,1)S(1)}, bf16[64,1024]{1,0:T(8,128)(2,1)S(1)}, u32[]{:S(2)}, u32[]{:S(2)}) collective-permute-start(bf16[64,1024]{1,0:T(8,128)(2,1)S(1)} %get-tuple-element.118), channel_id=1, source_target_pairs={{0,3},{1,0},{2,1},{3,2},{4,7},{5,4},{6,5},{7,6},{8,11},{9,8},{10,9... | collective-permute-start | bytes 393224 | tf_op jit(solution)/shard_map/ppermute | solution.py:111
  75.0 4.1 %weight_grad.2.refs_1_ = bf16[16,3,64,512]{3,2,1,0:T(8,128)(2,1)} custom-call(s32[2]{0:T(128)S(1)} %pad_add_fusion.me, bf16[1536,1024]{1,0:T(8,128)(2,1)S(1)} %copy-done, bf16[4,64,1024]{2,1,0:T(8,128)(2,1)S(1)} %stack_features.1.refs_0_, bf16[4,64,1024]{2,1,0:T(8,128)(2,1)S(1)} %collective-permute-done.20.refs_1_, ...), custom_call_target="tpu_custom_call" | custom-call | flops 2415919104 | bytes 2097152 | tf_op jit(solution)/shard_map/weight_grad/pallas_call | solution.py:377
  79.2 0.5 collective-permute-done.23.refs_2_
  79.7 0.7 sum_parts.1
  80.4 1.1 %collective-permute-start.25 = (bf16[2,64,128]{2,1,0:T(8,128)(2,1)S(1)}, bf16[2,64,128]{2,1,0:T(8,128)(2,1)S(1)}, u32[]{:S(2)}, u32[]{:S(2)}) collective-permute-start(bf16[2,64,128]{2,1,0:T(8,128)(2,1)S(1)} %get-tuple-element.127), channel_id=1, source_target_pairs={{0,32},{16,48},{32,64},{48,80},{64,96},{80,112},{96,0},{112,16},{1... | collective-permute-start | bytes 98312 | tf_op jit(solution)/shard_map/ppermute | solution.py:51
  81.4 3.0 %collective-permute-start.26 = (bf16[2,64,128]{2,1,0:T(8,128)(2,1)S(1)}, bf16[2,64,128]{2,1,0:T(8,128)(2,1)S(1)}, u32[]{:S(2)}, u32[]{:S(2)}) collective-permute-start(bf16[2,64,128]{2,1,0:T(8,128)(2,1)S(1)} %get-tuple-element.128), channel_id=1, source_target_pairs={{0,64},{16,80},{32,96},{48,112},{64,0},{80,16},{96,32},{112,48},{1... | collective-permute-start | bytes 98312 | tf_op jit(solution)/shard_map/ppermute | solution.py:51
  84.5 0.1 collective-permute-start.27
  84.6 2.4 %weight_grad.3 = bf16[16,3,64,512]{3,2,1,0:T(8,128)(2,1)} custom-call(s32[2]{0:T(128)S(1)} %pad_add_fusion.me, bf16[1536,1024]{1,0:T(8,128)(2,1)S(1)} %copy-done, bf16[4,64,1024]{2,1,0:T(8,128)(2,1)S(1)} %collective-permute-done.28.refs_0_, bf16[16,3,64,512]{3,2,1,0:T(8,128)(2,1)} %weight_grad.2.refs_1_), custom_call_target="tpu_custom_call", output_to_operand_aliasing={{}: (3, {})} | custom-call | flops 805306368 | bytes 2097152 | tf_op jit(solution)/shard_map/weight_grad/pallas_call | solution.py:377
  87.1 0.4 collective-permute-done.27
  87.5 2.1 %collective-permute-start.29 = (bf16[64,128]{1,0:T(8,128)(2,1)S(1)}, bf16[64,128]{1,0:T(8,128)(2,1)S(1)}, u32[]{:S(2)}, u32[]{:S(2)}) collective-permute-start(bf16[64,128]{1,0:T(8,128)(2,1)S(1)} %get-tuple-element.151), channel_id=1, source_target_pairs={{0,16},{16,0},{32,48},{48,32},{64,80},{80,64},{96,112},{112,96},{1... | collective-permute-start | bytes 49160 | tf_op jit(solution)/shard_map/ppermute | solution.py:55
  89.7 0.4 collective-permute-start.31
  90.2 0.1 collective-permute-start.32
  90.3 0.2 collective-permute-done.29.refs_4_
  90.5 0.3 collective-permute-done.30.refs_5_
  90.8 0.2 collective-permute-done.31.refs_6_
  91.0 0.3 collective-permute-done.32.refs_7_
  91.3 1.3 %finish.1 = bf16[128,512]{1,0:T(8,128)(2,1)} custom-call(s32[2]{0:T(128)S(1)} %pad_add_fusion.me, bf16[64,128]{1,0:T(8,128)(2,1)S(1)} %get-tuple-element.152.refs_0_, bf16[64,128]{1,0:T(8,128)(2,1)S(1)} %get-tuple-element.150.refs_1_, bf16[64,128]{1,0:T(8,128)(2,1)S(1)} %get-tuple-element.148.refs_2_, bf16[64,128]{1,0:T(8,128)(2,1)S(1)} %get-tuple-element.146.refs_3_, ...), custom_call_target="tpu_custom_call" | custom-call | tf_op jit(solution)/shard_map/finish/pallas_call | solution.py:452
  (30 shorter events, 0.3 us)
Async XLA Ops:
  2.7 11.7 %collective-permute-start = (bf16[2,5,64,128]{3,2,1,0:T(8,128)(2,1)S(1)}, bf16[2,5,64,128]{3,2,1,0:T(8,128)(2,1)S(1)}, u32[]{:S(2)}, u32[]{:S(2)}) collective-permute-start(bf16[2,5,64,128]{3,2,1,0:T(8,128)(2,1)S(1)} %get-tuple-element.71), channel_id=1, source_target_pairs={{0,32},{16,48},{32,64},{48,80},{64,96},{80,112},{96,0},{112,16},{1... | collective-permute-start | bytes 491528 | tf_op jit(solution)/shard_map/ppermute | solution.py:51
  4.8 9.6 %collective-permute-start.1 = (bf16[2,5,64,128]{3,2,1,0:T(8,128)(2,1)S(1)}, bf16[2,5,64,128]{3,2,1,0:T(8,128)(2,1)S(1)}, u32[]{:S(2)}, u32[]{:S(2)}) collective-permute-start(bf16[2,5,64,128]{3,2,1,0:T(8,128)(2,1)S(1)} %get-tuple-element.72), channel_id=1, source_target_pairs={{0,64},{16,80},{32,96},{48,112},{64,0},{80,16},{96,32},{112,48},{1... | collective-permute-start | bytes 491528 | tf_op jit(solution)/shard_map/ppermute | solution.py:51
  7.3 7.2 %collective-permute-start.2 = (bf16[2,5,64,128]{3,2,1,0:T(8,128)(2,1)S(1)}, bf16[2,5,64,128]{3,2,1,0:T(8,128)(2,1)S(1)}, u32[]{:S(2)}, u32[]{:S(2)}) collective-permute-start(bf16[2,5,64,128]{3,2,1,0:T(8,128)(2,1)S(1)} %get-tuple-element.73), channel_id=1, source_target_pairs={{0,96},{16,112},{32,0},{48,16},{64,32},{80,48},{96,64},{112,80},{1... | collective-permute-start | bytes 491528 | tf_op jit(solution)/shard_map/ppermute | solution.py:51
  8.4 0.9 copy-start.2
  14.5 2.5 %collective-permute-start.3 = (bf16[5,64,128]{2,1,0:T(8,128)(2,1)S(1)}, bf16[5,64,128]{2,1,0:T(8,128)(2,1)S(1)}, u32[]{:S(2)}, u32[]{:S(2)}) collective-permute-start(bf16[5,64,128]{2,1,0:T(8,128)(2,1)S(1)} %get-tuple-element.143), channel_id=1, source_target_pairs={{0,16},{16,0},{32,48},{48,32},{64,80},{80,64},{96,112},{112,96},{1... | collective-permute-start | bytes 245768 | tf_op jit(solution)/shard_map/ppermute | solution.py:55
  16.1 1.3 %collective-permute-start.4 = (bf16[5,64,128]{2,1,0:T(8,128)(2,1)S(1)}, bf16[5,64,128]{2,1,0:T(8,128)(2,1)S(1)}, u32[]{:S(2)}, u32[]{:S(2)}) collective-permute-start(bf16[5,64,128]{2,1,0:T(8,128)(2,1)S(1)} %get-tuple-element.141), channel_id=1, source_target_pairs={{0,16},{16,0},{32,48},{48,32},{64,80},{80,64},{96,112},{112,96},{1... | collective-permute-start | bytes 245768 | tf_op jit(solution)/shard_map/ppermute | solution.py:55
  16.2 1.3 %collective-permute-start.5 = (bf16[5,64,128]{2,1,0:T(8,128)(2,1)S(1)}, bf16[5,64,128]{2,1,0:T(8,128)(2,1)S(1)}, u32[]{:S(2)}, u32[]{:S(2)}) collective-permute-start(bf16[5,64,128]{2,1,0:T(8,128)(2,1)S(1)} %get-tuple-element.139), channel_id=1, source_target_pairs={{0,16},{16,0},{32,48},{48,32},{64,80},{80,64},{96,112},{112,96},{1... | collective-permute-start | bytes 245768 | tf_op jit(solution)/shard_map/ppermute | solution.py:55
  16.6 1.3 %collective-permute-start.6 = (bf16[5,64,128]{2,1,0:T(8,128)(2,1)S(1)}, bf16[5,64,128]{2,1,0:T(8,128)(2,1)S(1)}, u32[]{:S(2)}, u32[]{:S(2)}) collective-permute-start(bf16[5,64,128]{2,1,0:T(8,128)(2,1)S(1)} %get-tuple-element.137), channel_id=1, source_target_pairs={{0,16},{16,0},{32,48},{48,32},{64,80},{80,64},{96,112},{112,96},{1... | collective-permute-start | bytes 245768 | tf_op jit(solution)/shard_map/ppermute | solution.py:55
  23.1 2.0 %collective-permute-start.7 = (bf16[3,64,1024]{2,1,0:T(8,128)(2,1)S(1)}, bf16[3,64,1024]{2,1,0:T(8,128)(2,1)S(1)}, u32[]{:S(2)}, u32[]{:S(2)}) collective-permute-start(bf16[3,64,1024]{2,1,0:T(8,128)(2,1)S(1)} %get-tuple-element.92.refs_0_), channel_id=1, source_target_pairs={{0,16},{16,0},{32,48},{48,32},{64,80},{80,64},{96,112},{112,96},{1... | collective-permute-start | bytes 1179656 | tf_op jit(solution)/shard_map/ppermute | solution.py:55
  23.2 6.9 %collective-permute-start.8 = (bf16[3,64,1024]{2,1,0:T(8,128)(2,1)S(1)}, bf16[3,64,1024]{2,1,0:T(8,128)(2,1)S(1)}, u32[]{:S(2)}, u32[]{:S(2)}) collective-permute-start(bf16[3,64,1024]{2,1,0:T(8,128)(2,1)S(1)} %get-tuple-element.92.refs_0_), channel_id=1, source_target_pairs={{0,32},{16,112},{32,64},{48,16},{64,96},{80,48},{96,0},{112,80},{1... | collective-permute-start | bytes 1179656 | tf_op jit(solution)/shard_map/ppermute | solution.py:67
  25.1 15.2 %collective-permute-start.9 = (bf16[3,64,1024]{2,1,0:T(8,128)(2,1)S(1)}, bf16[3,64,1024]{2,1,0:T(8,128)(2,1)S(1)}, u32[]{:S(2)}, u32[]{:S(2)}) collective-permute-start(bf16[3,64,1024]{2,1,0:T(8,128)(2,1)S(1)} %collective-permute-done.7.refs_1_), channel_id=1, source_target_pairs={{0,32},{16,112},{32,64},{48,16},{64,96},{80,48},{96,0},{112,80},{1... | collective-permute-start | bytes 1179656 | tf_op jit(solution)/shard_map/ppermute | solution.py:67
  30.2 11.6 %collective-permute-start.12 = (bf16[3,64,1024]{2,1,0:T(8,128)(2,1)S(1)}, bf16[3,64,1024]{2,1,0:T(8,128)(2,1)S(1)}, u32[]{:S(2)}, u32[]{:S(2)}) collective-permute-start(bf16[3,64,1024]{2,1,0:T(8,128)(2,1)S(1)} %collective-permute-done.8.refs_2_), channel_id=1, source_target_pairs={{0,32},{16,112},{32,64},{48,16},{64,96},{80,48},{96,0},{112,80},{1... | collective-permute-start | bytes 1179656 | tf_op jit(solution)/shard_map/ppermute | solution.py:67
  33.5 11.7 %copy-start.1 = (bf16[16,64,3,512]{3,1,2,0:T(8,128)(2,1)S(1)}, bf16[16,64,3,512]{3,1,2,0:T(8,128)(2,1)}, u32[]{:S(2)}) copy-start(bf16[16,64,3,512]{3,1,2,0:T(8,128)(2,1)} %param.12) | copy-start | bytes 9437188
  33.5 5.6 %collective-permute-start.13 = (bf16[64,1024]{1,0:T(8,128)(2,1)S(1)}, bf16[64,1024]{1,0:T(8,128)(2,1)S(1)}, u32[]{:S(2)}, u32[]{:S(2)}) collective-permute-start(bf16[64,1024]{1,0:T(8,128)(2,1)S(1)} %join_features.1.refs_0_), channel_id=1, source_target_pairs={{0,1},{1,2},{2,3},{3,0},{4,5},{5,6},{6,7},{7,4},{8,9},{9,10},{10,1... | collective-permute-start | bytes 393224 | tf_op jit(solution)/shard_map/ppermute | solution.py:111
  35.0 6.7 %collective-permute-start.14 = (bf16[64,1024]{1,0:T(8,128)(2,1)S(1)}, bf16[64,1024]{1,0:T(8,128)(2,1)S(1)}, u32[]{:S(2)}, u32[]{:S(2)}) collective-permute-start(bf16[64,1024]{1,0:T(8,128)(2,1)S(1)} %join_features.1.refs_0_), channel_id=1, source_target_pairs={{0,2},{1,3},{2,0},{3,1},{4,6},{5,7},{6,4},{7,5},{8,10},{9,11},{10,... | collective-permute-start | bytes 393224 | tf_op jit(solution)/shard_map/ppermute | solution.py:111
  37.6 4.1 %collective-permute-start.15 = (bf16[64,1024]{1,0:T(8,128)(2,1)S(1)}, bf16[64,1024]{1,0:T(8,128)(2,1)S(1)}, u32[]{:S(2)}, u32[]{:S(2)}) collective-permute-start(bf16[64,1024]{1,0:T(8,128)(2,1)S(1)} %join_features.1.refs_0_), channel_id=1, source_target_pairs={{0,3},{1,0},{2,1},{3,2},{4,7},{5,4},{6,5},{7,6},{8,11},{9,8},{10,9... | collective-permute-start | bytes 393224 | tf_op jit(solution)/shard_map/ppermute | solution.py:111
  39.1 4.7 %collective-permute-start.10 = (bf16[3,64,1024]{2,1,0:T(8,128)(2,1)S(1)}, bf16[3,64,1024]{2,1,0:T(8,128)(2,1)S(1)}, u32[]{:S(2)}, u32[]{:S(2)}) collective-permute-start(bf16[3,64,1024]{2,1,0:T(8,128)(2,1)S(1)} %collective-permute-done.8.refs_2_), channel_id=1, source_target_pairs={{0,16},{16,0},{32,48},{48,32},{64,80},{80,64},{96,112},{112,96},{1... | collective-permute-start | bytes 1179656 | tf_op jit(solution)/shard_map/ppermute | solution.py:55
  40.4 3.5 %collective-permute-start.11 = (bf16[3,64,1024]{2,1,0:T(8,128)(2,1)S(1)}, bf16[3,64,1024]{2,1,0:T(8,128)(2,1)S(1)}, u32[]{:S(2)}, u32[]{:S(2)}) collective-permute-start(bf16[3,64,1024]{2,1,0:T(8,128)(2,1)S(1)} %collective-permute-done.9.refs_3_), channel_id=1, source_target_pairs={{0,16},{16,0},{32,48},{48,32},{64,80},{80,64},{96,112},{112,96},{1... | collective-permute-start | bytes 1179656 | tf_op jit(solution)/shard_map/ppermute | solution.py:55
  41.7 3.4 %collective-permute-start.16 = (bf16[3,64,1024]{2,1,0:T(8,128)(2,1)S(1)}, bf16[3,64,1024]{2,1,0:T(8,128)(2,1)S(1)}, u32[]{:S(2)}, u32[]{:S(2)}) collective-permute-start(bf16[3,64,1024]{2,1,0:T(8,128)(2,1)S(1)} %collective-permute-done.12.refs_2_), channel_id=1, source_target_pairs={{0,16},{16,0},{32,48},{48,32},{64,80},{80,64},{96,112},{112,96},{1... | collective-permute-start | bytes 1179656 | tf_op jit(solution)/shard_map/ppermute | solution.py:55
  48.4 9.8 %collective-permute-start.17 = (bf16[4,64,1024]{2,1,0:T(8,128)(2,1)S(1)}, bf16[4,64,1024]{2,1,0:T(8,128)(2,1)S(1)}, u32[]{:S(2)}, u32[]{:S(2)}) collective-permute-start(bf16[4,64,1024]{2,1,0:T(8,128)(2,1)S(1)} %get-tuple-element.104), channel_id=1, source_target_pairs={{0,4},{1,5},{2,6},{3,7},{4,8},{5,9},{6,10},{7,11},{8,12},{9,13},{1... | collective-permute-start | bytes 1572872 | tf_op jit(solution)/shard_map/ppermute | solution.py:111
  49.3 15.0 %collective-permute-start.18 = (bf16[4,64,1024]{2,1,0:T(8,128)(2,1)S(1)}, bf16[4,64,1024]{2,1,0:T(8,128)(2,1)S(1)}, u32[]{:S(2)}, u32[]{:S(2)}) collective-permute-start(bf16[4,64,1024]{2,1,0:T(8,128)(2,1)S(1)} %get-tuple-element.105), channel_id=1, source_target_pairs={{0,8},{1,9},{2,10},{3,11},{4,12},{5,13},{6,14},{7,15},{8,0},{9,1},... | collective-permute-start | bytes 1572872 | tf_op jit(solution)/shard_map/ppermute | solution.py:111
  51.8 12.7 %collective-permute-start.19 = (bf16[4,64,1024]{2,1,0:T(8,128)(2,1)S(1)}, bf16[4,64,1024]{2,1,0:T(8,128)(2,1)S(1)}, u32[]{:S(2)}, u32[]{:S(2)}) collective-permute-start(bf16[4,64,1024]{2,1,0:T(8,128)(2,1)S(1)} %get-tuple-element.106), channel_id=1, source_target_pairs={{0,12},{1,13},{2,14},{3,15},{4,0},{5,1},{6,2},{7,3},{8,4},{9,5},{1... | collective-permute-start | bytes 1572872 | tf_op jit(solution)/shard_map/ppermute | solution.py:111
  53.0 16.5 %collective-permute-start.20 = (bf16[4,64,1024]{2,1,0:T(8,128)(2,1)S(1)}, bf16[4,64,1024]{2,1,0:T(8,128)(2,1)S(1)}, u32[]{:S(2)}, u32[]{:S(2)}) collective-permute-start(bf16[4,64,1024]{2,1,0:T(8,128)(2,1)S(1)} %stack_features.1.refs_0_), channel_id=1, source_target_pairs={{0,4},{1,5},{2,6},{3,7},{4,8},{5,9},{6,10},{7,11},{8,12},{9,13},{1... | collective-permute-start | bytes 1572872 | tf_op jit(solution)/shard_map/ppermute | solution.py:111
  53.9 16.1 %collective-permute-start.21 = (bf16[4,64,1024]{2,1,0:T(8,128)(2,1)S(1)}, bf16[4,64,1024]{2,1,0:T(8,128)(2,1)S(1)}, u32[]{:S(2)}, u32[]{:S(2)}) collective-permute-start(bf16[4,64,1024]{2,1,0:T(8,128)(2,1)S(1)} %stack_features.1.refs_0_), channel_id=1, source_target_pairs={{0,12},{1,13},{2,14},{3,15},{4,0},{5,1},{6,2},{7,3},{8,4},{9,5},{1... | collective-permute-start | bytes 1572872 | tf_op jit(solution)/shard_map/ppermute | solution.py:111
  58.2 26.4 %collective-permute-start.28 = (bf16[4,64,1024]{2,1,0:T(8,128)(2,1)S(1)}, bf16[4,64,1024]{2,1,0:T(8,128)(2,1)S(1)}, u32[]{:S(2)}, u32[]{:S(2)}) collective-permute-start(bf16[4,64,1024]{2,1,0:T(8,128)(2,1)S(1)} %stack_features.1.refs_0_), channel_id=1, source_target_pairs={{0,8},{1,9},{2,10},{3,11},{4,12},{5,13},{6,14},{7,15},{8,0},{9,1},... | collective-permute-start | bytes 1572872 | tf_op jit(solution)/shard_map/ppermute | solution.py:111
  58.6 16.4 %copy-start = (bf16[1536,1024]{1,0:T(8,128)(2,1)S(1)}, bf16[1536,1024]{1,0:T(8,128)(2,1)}, u32[]{:S(2)}) copy-start(bf16[1536,1024]{1,0:T(8,128)(2,1)} %get-tuple-element.119.whole) | copy-start | bytes 9437188
  70.1 9.1 %collective-permute-start.22 = (bf16[64,1024]{1,0:T(8,128)(2,1)S(1)}, bf16[64,1024]{1,0:T(8,128)(2,1)S(1)}, u32[]{:S(2)}, u32[]{:S(2)}) collective-permute-start(bf16[64,1024]{1,0:T(8,128)(2,1)S(1)} %get-tuple-element.116), channel_id=1, source_target_pairs={{0,1},{1,2},{2,3},{3,0},{4,5},{5,6},{6,7},{7,4},{8,9},{9,10},{10,1... | collective-permute-start | bytes 393224 | tf_op jit(solution)/shard_map/ppermute | solution.py:111
  71.4 8.3 %collective-permute-start.23 = (bf16[64,1024]{1,0:T(8,128)(2,1)S(1)}, bf16[64,1024]{1,0:T(8,128)(2,1)S(1)}, u32[]{:S(2)}, u32[]{:S(2)}) collective-permute-start(bf16[64,1024]{1,0:T(8,128)(2,1)S(1)} %get-tuple-element.117), channel_id=1, source_target_pairs={{0,2},{1,3},{2,0},{3,1},{4,6},{5,7},{6,4},{7,5},{8,10},{9,11},{10,... | collective-permute-start | bytes 393224 | tf_op jit(solution)/shard_map/ppermute | solution.py:111
  74.0 5.7 %collective-permute-start.24 = (bf16[64,1024]{1,0:T(8,128)(2,1)S(1)}, bf16[64,1024]{1,0:T(8,128)(2,1)S(1)}, u32[]{:S(2)}, u32[]{:S(2)}) collective-permute-start(bf16[64,1024]{1,0:T(8,128)(2,1)S(1)} %get-tuple-element.118), channel_id=1, source_target_pairs={{0,3},{1,0},{2,1},{3,2},{4,7},{5,4},{6,5},{7,6},{8,11},{9,8},{10,9... | collective-permute-start | bytes 393224 | tf_op jit(solution)/shard_map/ppermute | solution.py:111
  80.4 6.7 %collective-permute-start.25 = (bf16[2,64,128]{2,1,0:T(8,128)(2,1)S(1)}, bf16[2,64,128]{2,1,0:T(8,128)(2,1)S(1)}, u32[]{:S(2)}, u32[]{:S(2)}) collective-permute-start(bf16[2,64,128]{2,1,0:T(8,128)(2,1)S(1)} %get-tuple-element.127), channel_id=1, source_target_pairs={{0,32},{16,48},{32,64},{48,80},{64,96},{80,112},{96,0},{112,16},{1... | collective-permute-start | bytes 98312 | tf_op jit(solution)/shard_map/ppermute | solution.py:51
  81.4 5.6 %collective-permute-start.26 = (bf16[2,64,128]{2,1,0:T(8,128)(2,1)S(1)}, bf16[2,64,128]{2,1,0:T(8,128)(2,1)S(1)}, u32[]{:S(2)}, u32[]{:S(2)}) collective-permute-start(bf16[2,64,128]{2,1,0:T(8,128)(2,1)S(1)} %get-tuple-element.128), channel_id=1, source_target_pairs={{0,64},{16,80},{32,96},{48,112},{64,0},{80,16},{96,32},{112,48},{1... | collective-permute-start | bytes 98312 | tf_op jit(solution)/shard_map/ppermute | solution.py:51
  84.5 3.0 %collective-permute-start.27 = (bf16[2,64,128]{2,1,0:T(8,128)(2,1)S(1)}, bf16[2,64,128]{2,1,0:T(8,128)(2,1)S(1)}, u32[]{:S(2)}, u32[]{:S(2)}) collective-permute-start(bf16[2,64,128]{2,1,0:T(8,128)(2,1)S(1)} %get-tuple-element.129), channel_id=1, source_target_pairs={{0,96},{16,112},{32,0},{48,16},{64,32},{80,48},{96,64},{112,80},{1... | collective-permute-start | bytes 98312 | tf_op jit(solution)/shard_map/ppermute | solution.py:51
  87.5 3.0 %collective-permute-start.29 = (bf16[64,128]{1,0:T(8,128)(2,1)S(1)}, bf16[64,128]{1,0:T(8,128)(2,1)S(1)}, u32[]{:S(2)}, u32[]{:S(2)}) collective-permute-start(bf16[64,128]{1,0:T(8,128)(2,1)S(1)} %get-tuple-element.151), channel_id=1, source_target_pairs={{0,16},{16,0},{32,48},{48,32},{64,80},{80,64},{96,112},{112,96},{1... | collective-permute-start | bytes 49160 | tf_op jit(solution)/shard_map/ppermute | solution.py:55
  89.6 1.2 %collective-permute-start.30 = (bf16[64,128]{1,0:T(8,128)(2,1)S(1)}, bf16[64,128]{1,0:T(8,128)(2,1)S(1)}, u32[]{:S(2)}, u32[]{:S(2)}) collective-permute-start(bf16[64,128]{1,0:T(8,128)(2,1)S(1)} %get-tuple-element.149), channel_id=1, source_target_pairs={{0,16},{16,0},{32,48},{48,32},{64,80},{80,64},{96,112},{112,96},{1... | collective-permute-start | bytes 49160 | tf_op jit(solution)/shard_map/ppermute | solution.py:55
  89.7 1.3 %collective-permute-start.31 = (bf16[64,128]{1,0:T(8,128)(2,1)S(1)}, bf16[64,128]{1,0:T(8,128)(2,1)S(1)}, u32[]{:S(2)}, u32[]{:S(2)}) collective-permute-start(bf16[64,128]{1,0:T(8,128)(2,1)S(1)} %get-tuple-element.147), channel_id=1, source_target_pairs={{0,16},{16,0},{32,48},{48,32},{64,80},{80,64},{96,112},{112,96},{1... | collective-permute-start | bytes 49160 | tf_op jit(solution)/shard_map/ppermute | solution.py:55
  90.2 1.2 %collective-permute-start.32 = (bf16[64,128]{1,0:T(8,128)(2,1)S(1)}, bf16[64,128]{1,0:T(8,128)(2,1)S(1)}, u32[]{:S(2)}, u32[]{:S(2)}) collective-permute-start(bf16[64,128]{1,0:T(8,128)(2,1)S(1)} %get-tuple-element.145), channel_id=1, source_target_pairs={{0,16},{16,0},{32,48},{48,32},{64,80},{80,64},{96,112},{112,96},{1... | collective-permute-start | bytes 49160 | tf_op jit(solution)/shard_map/ppermute | solution.py:55

commit v4 on v3

--- a/solution.py
+++ b/solution.py
@@ -31,12 +31,7 @@
 def tables(n):
     idx = np.arange(n, dtype=np.int64)
     angle = (np.outer(idx, idx) % (2 * n)).astype(np.float64) * (math.pi / n)
-    out = []
-    for whole in (np.cos(angle), np.sin(angle)):
-        high = whole.astype(BF16)
-        out.append(high)
-        out.append((whole - high.astype(np.float64)).astype(BF16))
-    return [jnp.asarray(t) for t in out]
+    return [jnp.asarray(whole.astype(BF16)) for whole in (np.cos(angle), np.sin(angle))]
 
 
 def dot(a, b):
@@ -194,9 +189,7 @@
 
 def spectrum(signals, table, n):
     nyq = jnp.sum(signals.astype(F32) * signs(n), axis=1, keepdims=True)
-    re = dot(signals, table[0][...]) + dot(signals, table[1][...])
-    im = dot(signals, table[2][...]) + dot(signals, table[3][...])
-    return re, im, nyq
+    return dot(signals, table[0][...]), dot(signals, table[1][...]), nyq
 
 
 def split(a):
@@ -211,15 +204,14 @@
     re_hi, re_lo = split(re * weight)
     im_hi, im_lo = split(im * weight)
     both = dot(jnp.concatenate([re_hi, re_lo], axis=0), table[0][...])
-    both = both + dot(jnp.concatenate([im_hi, im_lo], axis=0), table[2][...])
-    low = dot(re_hi, table[1][...]) + dot(im_hi, table[3][...])
-    return both[:rows] + both[rows:] + low + (nyq * (0.5 / n)) * signs(n)
+    both = both + dot(jnp.concatenate([im_hi, im_lo], axis=0), table[1][...])
+    return both[:rows] + both[rows:] + (nyq * (0.5 / n)) * signs(n)
 
 
 def taps_kernel(*refs):
-    far, taps = refs[:4], refs[4]
-    table, re, im, nyq, sems = refs[5:9], refs[9], refs[10], refs[11], refs[12]
-    copies = [pltpu.make_async_copy(far[i], table[i], sems.at[i]) for i in range(4)]
+    far, taps = refs[:2], refs[2]
+    table, (re, im, nyq, sems) = refs[3:5], refs[5:]
+    copies = [pltpu.make_async_copy(far[i], table[i], sems.at[i]) for i in range(2)]
     for copy in copies:
         copy.start()
     for copy in copies:
@@ -231,10 +223,10 @@
     chans, n = taps.shape
     return pl.pallas_call(
         taps_kernel,
-        out_shape=[like(n, n)] * 4 + [like(chans, n, dtype=F32)] * 2 + [like(chans, 1, dtype=F32)],
-        in_specs=[FAR] * 4 + [ON_CHIP],
-        out_specs=[ON_CHIP] * 7,
-        scratch_shapes=[pltpu.SemaphoreType.DMA((4,))],
+        out_shape=[like(n, n)] * 2 + [like(chans, n, dtype=F32)] * 2 + [like(chans, 1, dtype=F32)],
+        in_specs=[FAR] * 2 + [ON_CHIP],
+        out_specs=[ON_CHIP] * 5,
+        scratch_shapes=[pltpu.SemaphoreType.DMA((2,))],
         compiler_params=vmem(12),
         cost_estimate=pl.CostEstimate(flops=8 * chans * n * n, bytes_accessed=8 * MIB, transcendentals=0),
         name="taps_spectrum",
@@ -243,9 +235,9 @@
 
 def conv_kernel(me, *refs):
     pieces = refs[:N_CTX]
-    table = refs[N_CTX : N_CTX + 4]
-    hr, hi, hn = refs[N_CTX + 4 : N_CTX + 7]
-    grads, grad_taps, whole = refs[N_CTX + 7 :]
+    table = refs[N_CTX : N_CTX + 2]
+    hr, hi, hn = refs[N_CTX + 2 : N_CTX + 5]
+    grads, grad_taps, whole = refs[N_CTX + 5 :]
     chans, span = pieces[0].shape[-2:]
     n = N_CTX * span
     for p in range(N_CTX):
@@ -271,7 +263,7 @@
     return pl.pallas_call(
         conv_kernel,
         out_shape=[like(3, chans, n), like(chans, n)],
-        in_specs=[SCALAR] + [ON_CHIP] * (N_CTX + 7),
+        in_specs=[SCALAR] + [ON_CHIP] * (N_CTX + 5),
         out_specs=[ON_CHIP] * 2,
         scratch_shapes=[pltpu.VMEM((4, chans, n), BF16)],
         compiler_params=vmem(20),
@@ -486,7 +478,9 @@
     parts = [shift_ring(p, s, first=True) for p, s in zip(sent, (1, 2, 3), strict=True)]
     feats = stack(me, feats)
     feats1, feats3 = shift_ring(feats, 1, first=True), shift_ring(feats, 3, first=True)
-    parts = [*value_part(me, weights, whole, (0,)), *parts]
+    (part,) = value_part(me, weights, whole, (0,))
+    part, feats = tie(part, feats)
+    parts = [part, *parts]
     parts = first_sum(me, parts)
     parts, (feats1, feats3) = tie(parts, (feats1, feats3))
     parts = [parts[0]] + [shift_ring(parts[s], s, first=False) for s in (1, 2, 3)]

time: 92.8 us -> 91.3 us (0.984)
  Pallas kernels: 28.2 us -> 24.8 us
  waiting for transfers between devices: 20.7 us -> 22.7 us
    pallas_call x1, Pallas kernels: 5.07 us -> 3.08 us  [taps_spectrum(): pl.pallas_call(taps_kernel, out_shape=[like(n, n)] * 2 + [like(chans, n,...]
    ppermute x6, waiting for transfers between devices: 0.42 us -> 2.36 us  [shift_x(): lax.ppermute(a, 'ctx', [(i, (i + 2 * steps) % N_CTX) for i in range(N_CTX)])]
    pallas_call x1, Pallas kernels: 5.21 us -> 3.81 us  [convolutions(): pl.pallas_call(conv_kernel, out_shape=[like(3, chans, n), like(chans, n)]...]
  transfers between devices with their start and end apart: 33 -> 33, of which waited for: 20 -> 21; matrix products, arithmetic and copies ran while one was open for 0% -> 0% of each run, Pallas kernels for 18% -> 16%
where the time goes in v4:
time: 91.3 us; the launch traced here: 91.2 us
  starting transfers between devices  41.8 us (46%)
  Pallas kernels  24.8 us (27%)
  waiting for transfers between devices  22.7 us (25%)
  local copies, waits for them, and re-layouts  0.97 us (1%)
    ppermute x12, starting transfers between devices, shift_ring(): return lax.ppermute(a, ('ctx', 'tp'), pairs)  17.1 us
    ppermute x12, waiting for transfers between devices, shift_ring(): return lax.ppermute(a, ('ctx', 'tp'), pairs)  13.9 us
    ppermute x6, starting transfers between devices, shift_x(): lax.ppermute(a, 'ctx', [(i, (i + 2 * steps) % N_CTX) for i in range(N_CTX)])  9.96 us
    ppermute x12, starting transfers between devices, swap_core(): return lax.ppermute(a, 'ctx', [(i, i ^ 1) for i in range(N_CTX)])  8.53 us
    pallas_call x2, Pallas kernels, weight_grad(): pl.pallas_call(functools.partial(weight_kernel, steps), out_shape=pltpu.H...  6.54 us
    ppermute x3, starting transfers between devices, spin(): return lax.ppermute(a, 'ctx', pairs)  6.24 us
    pallas_call x2, Pallas kernels, value_part(): pl.pallas_call(functools.partial(value_kernel, steps, which), out_shape=s...  4.73 us
    pallas_call x1, Pallas kernels, convolutions(): pl.pallas_call(conv_kernel, out_shape=[like(3, chans, n), like(chans, n)]...  3.81 us
  transfers between devices with their start and end apart: 33, of which 21 were waited for; matrix products, arithmetic and copies ran while one was open for 0% of the time, Pallas kernels for 16%

profile of v4, /device:TPU:1, one launch (start us, length us, event | category | flops | bytes accessed | tf_op | source)
XLA Modules:
  0.0 91.2 jit_solution(16555864799287924416)
XLA Ops:
  0.7 2.0 %prepare.1 = (bf16[2,5,64,128]{3,2,1,0:T(8,128)(2,1)S(1)}, bf16[2,5,64,128]{3,2,1,0:T(8,128)(2,1)S(1)}, bf16[2,5,64,128]{3,2,1,0:T(8,128)(2,1)S(1)}, bf16[2,5,64,128]{3,2,1,0:T(8,128)(2,1)S(1)}) custom-call(s32[2]{0:T(128)S(1)} %pad_add_fusion.me, bf16[128,512]{1,0:T(8,128)(2,1)} %refs_0_.2, bf16[128,512]{1,0:T(8,128)(2,1)} %refs_1_.2, ...), custom_call_target="tpu_custom_call" | custom-call | tf_op jit(solution)/shard_map/prepare/pallas_call | solution.py:134
  2.7 2.1 %collective-permute-start = (bf16[2,5,64,128]{3,2,1,0:T(8,128)(2,1)S(1)}, bf16[2,5,64,128]{3,2,1,0:T(8,128)(2,1)S(1)}, u32[]{:S(2)}, u32[]{:S(2)}) collective-permute-start(bf16[2,5,64,128]{3,2,1,0:T(8,128)(2,1)S(1)} %get-tuple-element.69), channel_id=1, source_target_pairs={{0,32},{16,48},{32,64},{48,80},{64,96},{80,112},{96,0},{112,16},{1... | collective-permute-start | bytes 491528 | tf_op jit(solution)/shard_map/ppermute | solution.py:46
  4.8 2.5 %collective-permute-start.1 = (bf16[2,5,64,128]{3,2,1,0:T(8,128)(2,1)S(1)}, bf16[2,5,64,128]{3,2,1,0:T(8,128)(2,1)S(1)}, u32[]{:S(2)}, u32[]{:S(2)}) collective-permute-start(bf16[2,5,64,128]{3,2,1,0:T(8,128)(2,1)S(1)} %get-tuple-element.70), channel_id=1, source_target_pairs={{0,64},{16,80},{32,96},{48,112},{64,0},{80,16},{96,32},{112,48},{1... | collective-permute-start | bytes 491528 | tf_op jit(solution)/shard_map/ppermute | solution.py:46
  7.3 1.2 %collective-permute-start.2 = (bf16[2,5,64,128]{3,2,1,0:T(8,128)(2,1)S(1)}, bf16[2,5,64,128]{3,2,1,0:T(8,128)(2,1)S(1)}, u32[]{:S(2)}, u32[]{:S(2)}) collective-permute-start(bf16[2,5,64,128]{3,2,1,0:T(8,128)(2,1)S(1)} %get-tuple-element.71), channel_id=1, source_target_pairs={{0,96},{16,112},{32,0},{48,16},{64,32},{80,48},{96,64},{112,80},{1... | collective-permute-start | bytes 491528 | tf_op jit(solution)/shard_map/ppermute | solution.py:46
  8.4 0.9 copy-done.2
  9.3 3.1 %taps_spectrum.1 = (bf16[1024,1024]{1,0:T(8,128)(2,1)S(1)}, bf16[1024,1024]{1,0:T(8,128)(2,1)S(1)}, f32[64,1024]{1,0:T(8,128)S(1)}, f32[64,1024]{1,0:T(8,128)S(1)}, f32[64,1]{1,0:T(8,128)S(1)}) custom-call(bf16[1024,1024]{1,0:T(8,128)(2,1)} %constant.13.clone.refs_0_, bf16[1024,1024]{1,0:T(8,128)(2,1)} %constant.14.clone.refs_1_, bf16[64,1024]{1,0:T(8,128)(2,1)S(1)} %bitcast.40), custom_call_target="tpu_custom_call" | custom-call | flops 536870912 | bytes 8388608 | tf_op jit(solution)/shard_map/taps_spectrum/pallas_call | solution.py:224
  12.4 2.0 %collective-permute-done.1 = bf16[2,5,64,128]{3,2,1,0:T(8,128)(2,1)S(1)} collective-permute-done((bf16[2,5,64,128]{3,2,1,0:T(8,128)(2,1)S(1)}, bf16[2,5,64,128]{3,2,1,0:T(8,128)(2,1)S(1)}, u32[]{:S(2)}, u32[]{:S(2)}) %collective-permute-start.1) | collective-permute-done | bytes 163872 | tf_op jit(solution)/shard_map/ppermute | solution.py:46
  14.4 1.6 %collective-permute-start.3 = (bf16[5,64,128]{2,1,0:T(8,128)(2,1)S(1)}, bf16[5,64,128]{2,1,0:T(8,128)(2,1)S(1)}, u32[]{:S(2)}, u32[]{:S(2)}) collective-permute-start(bf16[5,64,128]{2,1,0:T(8,128)(2,1)S(1)} %get-tuple-element.139), channel_id=1, source_target_pairs={{0,16},{16,0},{32,48},{48,32},{64,80},{80,64},{96,112},{112,96},{1... | collective-permute-start | bytes 245768 | tf_op jit(solution)/shard_map/ppermute | solution.py:50
  16.0 0.1 collective-permute-start.4
  16.1 0.6 collective-permute-start.5
  16.7 0.1 collective-permute-start.6
  16.8 0.1 collective-permute-done.3.refs_4_
  16.9 0.4 collective-permute-done.4.refs_5_
  17.4 0.2 collective-permute-done.5.refs_6_
  17.6 0.4 collective-permute-done.6.refs_7_
  18.1 3.8 %convolutions.1 = (bf16[3,64,1024]{2,1,0:T(8,128)(2,1)S(1)}, bf16[64,1024]{1,0:T(8,128)(2,1)}) custom-call(s32[2]{0:T(128)S(1)} %pad_add_fusion.me, bf16[5,64,128]{2,1,0:T(8,128)(2,1)S(1)} %get-tuple-element.88.refs_0_, bf16[5,64,128]{2,1,0:T(8,128)(2,1)S(1)} %get-tuple-element.89.refs_1_, bf16[5,64,128]{2,1,0:T(8,128)(2,1)S(1)} %get-tuple-element.90.refs_2_, ...), custom_call_target="tpu_custom_call" | custom-call | flops 2147483648 | bytes 8388608 | tf_op jit(solution)/shard_map/convolutions/pallas_call | solution.py:263
  21.9 0.1 collective-permute-start.7
  22.0 1.9 %collective-permute-start.8 = (bf16[3,64,1024]{2,1,0:T(8,128)(2,1)S(1)}, bf16[3,64,1024]{2,1,0:T(8,128)(2,1)S(1)}, u32[]{:S(2)}, u32[]{:S(2)}) collective-permute-start(bf16[3,64,1024]{2,1,0:T(8,128)(2,1)S(1)} %get-tuple-element.86.refs_0_), channel_id=1, source_target_pairs={{0,32},{16,112},{32,64},{48,16},{64,96},{80,48},{96,0},{112,80},{1... | collective-permute-start | bytes 1179656 | tf_op jit(solution)/shard_map/ppermute | solution.py:62
  23.9 1.6 %collective-permute-start.9 = (bf16[3,64,1024]{2,1,0:T(8,128)(2,1)S(1)}, bf16[3,64,1024]{2,1,0:T(8,128)(2,1)S(1)}, u32[]{:S(2)}, u32[]{:S(2)}) collective-permute-start(bf16[3,64,1024]{2,1,0:T(8,128)(2,1)S(1)} %collective-permute-done.7.refs_1_), channel_id=1, source_target_pairs={{0,32},{16,112},{32,64},{48,16},{64,96},{80,48},{96,0},{112,80},{1... | collective-permute-start | bytes 1179656 | tf_op jit(solution)/shard_map/ppermute | solution.py:62
  25.5 3.5 %collective-permute-done.8.refs_2_ = bf16[3,64,1024]{2,1,0:T(8,128)(2,1)S(1)} collective-permute-done((bf16[3,64,1024]{2,1,0:T(8,128)(2,1)S(1)}, bf16[3,64,1024]{2,1,0:T(8,128)(2,1)S(1)}, u32[]{:S(2)}, u32[]{:S(2)}) %collective-permute-start.8) | collective-permute-done | bytes 393248 | tf_op jit(solution)/shard_map/ppermute | solution.py:62
  29.0 2.8 %collective-permute-start.12 = (bf16[3,64,1024]{2,1,0:T(8,128)(2,1)S(1)}, bf16[3,64,1024]{2,1,0:T(8,128)(2,1)S(1)}, u32[]{:S(2)}, u32[]{:S(2)}) collective-permute-start(bf16[3,64,1024]{2,1,0:T(8,128)(2,1)S(1)} %collective-permute-done.8.refs_2_), channel_id=1, source_target_pairs={{0,32},{16,112},{32,64},{48,16},{64,96},{80,48},{96,0},{112,80},{1... | collective-permute-start | bytes 1179656 | tf_op jit(solution)/shard_map/ppermute | solution.py:62
  31.8 0.6 join_features.1.refs_0_
  32.4 1.5 %collective-permute-start.13 = (bf16[64,1024]{1,0:T(8,128)(2,1)S(1)}, bf16[64,1024]{1,0:T(8,128)(2,1)S(1)}, u32[]{:S(2)}, u32[]{:S(2)}) collective-permute-start(bf16[64,1024]{1,0:T(8,128)(2,1)S(1)} %join_features.1.refs_0_), channel_id=1, source_target_pairs={{0,1},{1,2},{2,3},{3,0},{4,5},{5,6},{6,7},{7,4},{8,9},{9,10},{10,1... | collective-permute-start | bytes 393224 | tf_op jit(solution)/shard_map/ppermute | solution.py:106
  33.8 2.6 %collective-permute-start.14 = (bf16[64,1024]{1,0:T(8,128)(2,1)S(1)}, bf16[64,1024]{1,0:T(8,128)(2,1)S(1)}, u32[]{:S(2)}, u32[]{:S(2)}) collective-permute-start(bf16[64,1024]{1,0:T(8,128)(2,1)S(1)} %join_features.1.refs_0_), channel_id=1, source_target_pairs={{0,2},{1,3},{2,0},{3,1},{4,6},{5,7},{6,4},{7,5},{8,10},{9,11},{10,... | collective-permute-start | bytes 393224 | tf_op jit(solution)/shard_map/ppermute | solution.py:106
  36.5 1.1 %collective-permute-start.15 = (bf16[64,1024]{1,0:T(8,128)(2,1)S(1)}, bf16[64,1024]{1,0:T(8,128)(2,1)S(1)}, u32[]{:S(2)}, u32[]{:S(2)}) collective-permute-start(bf16[64,1024]{1,0:T(8,128)(2,1)S(1)} %join_features.1.refs_0_), channel_id=1, source_target_pairs={{0,3},{1,0},{2,1},{3,2},{4,7},{5,4},{6,5},{7,6},{8,11},{9,8},{10,9... | collective-permute-start | bytes 393224 | tf_op jit(solution)/shard_map/ppermute | solution.py:106
  37.5 0.4 collective-permute-done.13.refs_1_
  37.9 1.2 %collective-permute-start.10 = (bf16[3,64,1024]{2,1,0:T(8,128)(2,1)S(1)}, bf16[3,64,1024]{2,1,0:T(8,128)(2,1)S(1)}, u32[]{:S(2)}, u32[]{:S(2)}) collective-permute-start(bf16[3,64,1024]{2,1,0:T(8,128)(2,1)S(1)} %collective-permute-done.8.refs_2_), channel_id=1, source_target_pairs={{0,16},{16,0},{32,48},{48,32},{64,80},{80,64},{96,112},{112,96},{1... | collective-permute-start | bytes 1179656 | tf_op jit(solution)/shard_map/ppermute | solution.py:50
  39.2 1.3 %collective-permute-done.14.refs_2_ = bf16[64,1024]{1,0:T(8,128)(2,1)S(1)} collective-permute-done((bf16[64,1024]{1,0:T(8,128)(2,1)S(1)}, bf16[64,1024]{1,0:T(8,128)(2,1)S(1)}, u32[]{:S(2)}, u32[]{:S(2)}) %collective-permute-start.14) | collective-permute-done | bytes 131104 | tf_op jit(solution)/shard_map/ppermute | solution.py:106
  40.6 2.1 %collective-permute-start.16 = (bf16[3,64,1024]{2,1,0:T(8,128)(2,1)S(1)}, bf16[3,64,1024]{2,1,0:T(8,128)(2,1)S(1)}, u32[]{:S(2)}, u32[]{:S(2)}) collective-permute-start(bf16[3,64,1024]{2,1,0:T(8,128)(2,1)S(1)} %collective-permute-done.12.refs_2_), channel_id=1, source_target_pairs={{0,16},{16,0},{32,48},{48,32},{64,80},{80,64},{96,112},{112,96},{1... | collective-permute-start | bytes 1179656 | tf_op jit(solution)/shard_map/ppermute | solution.py:50
  42.7 0.7 assemble.1.refs_1_
  43.4 0.6 collective-permute-done.16.refs_3_
  44.0 3.2 %value_part.2 = (bf16[4,64,1024]{2,1,0:T(8,128)(2,1)S(1)}, bf16[4,64,1024]{2,1,0:T(8,128)(2,1)S(1)}, bf16[4,64,1024]{2,1,0:T(8,128)(2,1)S(1)}, bf16[1536,1024]{1,0:T(8,128)(2,1)S(1)}, bf16[1536,1024]{1,0:T(8,128)(2,1)}) custom-call(s32[2]{0:T(128)S(1)} %pad_add_fusion.me, bf16[16,3,64,512]{3,2,1,0:T(8,128)(2,1)S(1)} %bitcast.38, ...), custom_call_target="tpu_custom_call", output_to_operand_aliasing={{3}: (2, {})} | custom-call | flops 2415919104 | bytes 2097152 | tf_op jit(solution)/shard_map/value_part/pallas_call | solution.py:332
  47.2 0.7 collective-permute-start.17
  47.9 2.5 %collective-permute-start.18 = (bf16[4,64,1024]{2,1,0:T(8,128)(2,1)S(1)}, bf16[4,64,1024]{2,1,0:T(8,128)(2,1)S(1)}, u32[]{:S(2)}, u32[]{:S(2)}) collective-permute-start(bf16[4,64,1024]{2,1,0:T(8,128)(2,1)S(1)} %get-tuple-element.104), channel_id=1, source_target_pairs={{0,8},{1,9},{2,10},{3,11},{4,12},{5,13},{6,14},{7,15},{8,0},{9,1},... | collective-permute-start | bytes 1572872 | tf_op jit(solution)/shard_map/ppermute | solution.py:106
  50.4 0.6 collective-permute-start.19
  51.0 0.6 stack_features.1.refs_0_
  51.6 1.0 %collective-permute-start.20 = (bf16[4,64,1024]{2,1,0:T(8,128)(2,1)S(1)}, bf16[4,64,1024]{2,1,0:T(8,128)(2,1)S(1)}, u32[]{:S(2)}, u32[]{:S(2)}) collective-permute-start(bf16[4,64,1024]{2,1,0:T(8,128)(2,1)S(1)} %stack_features.1.refs_0_), channel_id=1, source_target_pairs={{0,4},{1,5},{2,6},{3,7},{4,8},{5,9},{6,10},{7,11},{8,12},{9,13},{1... | collective-permute-start | bytes 1572872 | tf_op jit(solution)/shard_map/ppermute | solution.py:106
  52.6 1.8 %collective-permute-start.21 = (bf16[4,64,1024]{2,1,0:T(8,128)(2,1)S(1)}, bf16[4,64,1024]{2,1,0:T(8,128)(2,1)S(1)}, u32[]{:S(2)}, u32[]{:S(2)}) collective-permute-start(bf16[4,64,1024]{2,1,0:T(8,128)(2,1)S(1)} %stack_features.1.refs_0_), channel_id=1, source_target_pairs={{0,12},{1,13},{2,14},{3,15},{4,0},{5,1},{6,2},{7,3},{8,4},{9,5},{1... | collective-permute-start | bytes 1572872 | tf_op jit(solution)/shard_map/ppermute | solution.py:106
  54.3 1.5 %value_part.3.refs_0_ = bf16[4,64,1024]{2,1,0:T(8,128)(2,1)S(1)} custom-call(s32[2]{0:T(128)S(1)} %pad_add_fusion.me, bf16[16,3,64,512]{3,2,1,0:T(8,128)(2,1)S(1)} %bitcast.39, bf16[1536,1024]{1,0:T(8,128)(2,1)S(1)} %get-tuple-element.97.refs_1_), custom_call_target="tpu_custom_call" | custom-call | flops 805306368 | bytes 2097152 | tf_op jit(solution)/shard_map/value_part/pallas_call | solution.py:332
  55.9 1.0 %collective-permute-done.17.refs_1_ = bf16[4,64,1024]{2,1,0:T(8,128)(2,1)S(1)} collective-permute-done((bf16[4,64,1024]{2,1,0:T(8,128)(2,1)S(1)}, bf16[4,64,1024]{2,1,0:T(8,128)(2,1)S(1)}, u32[]{:S(2)}, u32[]{:S(2)}) %collective-permute-start.17) | collective-permute-done | bytes 524320 | tf_op jit(solution)/shard_map/ppermute | solution.py:106
  56.8 0.4 collective-permute-start.28
  57.2 5.7 %collective-permute-done.18.refs_2_ = bf16[4,64,1024]{2,1,0:T(8,128)(2,1)S(1)} collective-permute-done((bf16[4,64,1024]{2,1,0:T(8,128)(2,1)S(1)}, bf16[4,64,1024]{2,1,0:T(8,128)(2,1)S(1)}, u32[]{:S(2)}, u32[]{:S(2)}) %collective-permute-start.18) | collective-permute-done | bytes 524320 | tf_op jit(solution)/shard_map/ppermute | solution.py:106
  63.0 0.1 collective-permute-done.19.refs_3_
  63.1 0.8 first_sum.1
  63.9 4.2 %collective-permute-done.20.refs_1_ = bf16[4,64,1024]{2,1,0:T(8,128)(2,1)S(1)} collective-permute-done((bf16[4,64,1024]{2,1,0:T(8,128)(2,1)S(1)}, bf16[4,64,1024]{2,1,0:T(8,128)(2,1)S(1)}, u32[]{:S(2)}, u32[]{:S(2)}) %collective-permute-start.20) | collective-permute-done | bytes 524320 | tf_op jit(solution)/shard_map/ppermute | solution.py:106
  68.1 0.6 collective-permute-done.21.refs_2_
  68.7 1.3 %collective-permute-start.22 = (bf16[64,1024]{1,0:T(8,128)(2,1)S(1)}, bf16[64,1024]{1,0:T(8,128)(2,1)S(1)}, u32[]{:S(2)}, u32[]{:S(2)}) collective-permute-start(bf16[64,1024]{1,0:T(8,128)(2,1)S(1)} %get-tuple-element.111), channel_id=1, source_target_pairs={{0,1},{1,2},{2,3},{3,0},{4,5},{5,6},{6,7},{7,4},{8,9},{9,10},{10,1... | collective-permute-start | bytes 393224 | tf_op jit(solution)/shard_map/ppermute | solution.py:106
  70.0 2.6 %collective-permute-start.23 = (bf16[64,1024]{1,0:T(8,128)(2,1)S(1)}, bf16[64,1024]{1,0:T(8,128)(2,1)S(1)}, u32[]{:S(2)}, u32[]{:S(2)}) collective-permute-start(bf16[64,1024]{1,0:T(8,128)(2,1)S(1)} %get-tuple-element.112), channel_id=1, source_target_pairs={{0,2},{1,3},{2,0},{3,1},{4,6},{5,7},{6,4},{7,5},{8,10},{9,11},{10,... | collective-permute-start | bytes 393224 | tf_op jit(solution)/shard_map/ppermute | solution.py:106
  72.6 1.1 %collective-permute-start.24 = (bf16[64,1024]{1,0:T(8,128)(2,1)S(1)}, bf16[64,1024]{1,0:T(8,128)(2,1)S(1)}, u32[]{:S(2)}, u32[]{:S(2)}) collective-permute-start(bf16[64,1024]{1,0:T(8,128)(2,1)S(1)} %get-tuple-element.113), channel_id=1, source_target_pairs={{0,3},{1,0},{2,1},{3,2},{4,7},{5,4},{6,5},{7,6},{8,11},{9,8},{10,9... | collective-permute-start | bytes 393224 | tf_op jit(solution)/shard_map/ppermute | solution.py:106
  73.7 4.1 %weight_grad.2.refs_1_ = bf16[16,3,64,512]{3,2,1,0:T(8,128)(2,1)} custom-call(s32[2]{0:T(128)S(1)} %pad_add_fusion.me, bf16[1536,1024]{1,0:T(8,128)(2,1)S(1)} %copy-done, bf16[4,64,1024]{2,1,0:T(8,128)(2,1)S(1)} %stack_features.1.refs_0_, bf16[4,64,1024]{2,1,0:T(8,128)(2,1)S(1)} %collective-permute-done.20.refs_1_, ...), custom_call_target="tpu_custom_call" | custom-call | flops 2415919104 | bytes 2097152 | tf_op jit(solution)/shard_map/weight_grad/pallas_call | solution.py:369
  77.8 0.5 collective-permute-done.23.refs_2_
  78.3 0.7 sum_parts.1
  79.0 1.1 %collective-permute-start.25 = (bf16[2,64,128]{2,1,0:T(8,128)(2,1)S(1)}, bf16[2,64,128]{2,1,0:T(8,128)(2,1)S(1)}, u32[]{:S(2)}, u32[]{:S(2)}) collective-permute-start(bf16[2,64,128]{2,1,0:T(8,128)(2,1)S(1)} %get-tuple-element.123), channel_id=1, source_target_pairs={{0,32},{16,48},{32,64},{48,80},{64,96},{80,112},{96,0},{112,16},{1... | collective-permute-start | bytes 98312 | tf_op jit(solution)/shard_map/ppermute | solution.py:46
  80.1 3.0 %collective-permute-start.26 = (bf16[2,64,128]{2,1,0:T(8,128)(2,1)S(1)}, bf16[2,64,128]{2,1,0:T(8,128)(2,1)S(1)}, u32[]{:S(2)}, u32[]{:S(2)}) collective-permute-start(bf16[2,64,128]{2,1,0:T(8,128)(2,1)S(1)} %get-tuple-element.124), channel_id=1, source_target_pairs={{0,64},{16,80},{32,96},{48,112},{64,0},{80,16},{96,32},{112,48},{1... | collective-permute-start | bytes 98312 | tf_op jit(solution)/shard_map/ppermute | solution.py:46
  83.1 0.2 collective-permute-start.27
  83.2 2.4 %weight_grad.3 = bf16[16,3,64,512]{3,2,1,0:T(8,128)(2,1)} custom-call(s32[2]{0:T(128)S(1)} %pad_add_fusion.me, bf16[1536,1024]{1,0:T(8,128)(2,1)S(1)} %copy-done, bf16[4,64,1024]{2,1,0:T(8,128)(2,1)S(1)} %collective-permute-done.28.refs_0_, bf16[16,3,64,512]{3,2,1,0:T(8,128)(2,1)} %weight_grad.2.refs_1_), custom_call_target="tpu_custom_call", output_to_operand_aliasing={{}: (3, {})} | custom-call | flops 805306368 | bytes 2097152 | tf_op jit(solution)/shard_map/weight_grad/pallas_call | solution.py:369
  85.7 0.4 collective-permute-done.27
  86.1 2.1 %collective-permute-start.29 = (bf16[64,128]{1,0:T(8,128)(2,1)S(1)}, bf16[64,128]{1,0:T(8,128)(2,1)S(1)}, u32[]{:S(2)}, u32[]{:S(2)}) collective-permute-start(bf16[64,128]{1,0:T(8,128)(2,1)S(1)} %get-tuple-element.147), channel_id=1, source_target_pairs={{0,16},{16,0},{32,48},{48,32},{64,80},{80,64},{96,112},{112,96},{1... | collective-permute-start | bytes 49160 | tf_op jit(solution)/shard_map/ppermute | solution.py:50
  88.2 0.4 collective-permute-start.31
  88.8 0.2 collective-permute-done.29.refs_4_
  89.0 0.3 collective-permute-done.30.refs_5_
  89.3 0.2 collective-permute-done.31.refs_6_
  89.5 0.3 collective-permute-done.32.refs_7_
  89.9 1.3 %finish.1 = bf16[128,512]{1,0:T(8,128)(2,1)} custom-call(s32[2]{0:T(128)S(1)} %pad_add_fusion.me, bf16[64,128]{1,0:T(8,128)(2,1)S(1)} %get-tuple-element.148.refs_0_, bf16[64,128]{1,0:T(8,128)(2,1)S(1)} %get-tuple-element.146.refs_1_, bf16[64,128]{1,0:T(8,128)(2,1)S(1)} %get-tuple-element.144.refs_2_, bf16[64,128]{1,0:T(8,128)(2,1)S(1)} %get-tuple-element.142.refs_3_, ...), custom_call_target="tpu_custom_call" | custom-call | tf_op jit(solution)/shard_map/finish/pallas_call | solution.py:444
  (30 shorter events, 0.4 us)
Async XLA Ops:
  2.7 9.7 %collective-permute-start = (bf16[2,5,64,128]{3,2,1,0:T(8,128)(2,1)S(1)}, bf16[2,5,64,128]{3,2,1,0:T(8,128)(2,1)S(1)}, u32[]{:S(2)}, u32[]{:S(2)}) collective-permute-start(bf16[2,5,64,128]{3,2,1,0:T(8,128)(2,1)S(1)} %get-tuple-element.69), channel_id=1, source_target_pairs={{0,32},{16,48},{32,64},{48,80},{64,96},{80,112},{96,0},{112,16},{1... | collective-permute-start | bytes 491528 | tf_op jit(solution)/shard_map/ppermute | solution.py:46
  4.8 9.6 %collective-permute-start.1 = (bf16[2,5,64,128]{3,2,1,0:T(8,128)(2,1)S(1)}, bf16[2,5,64,128]{3,2,1,0:T(8,128)(2,1)S(1)}, u32[]{:S(2)}, u32[]{:S(2)}) collective-permute-start(bf16[2,5,64,128]{3,2,1,0:T(8,128)(2,1)S(1)} %get-tuple-element.70), channel_id=1, source_target_pairs={{0,64},{16,80},{32,96},{48,112},{64,0},{80,16},{96,32},{112,48},{1... | collective-permute-start | bytes 491528 | tf_op jit(solution)/shard_map/ppermute | solution.py:46
  7.3 7.1 %collective-permute-start.2 = (bf16[2,5,64,128]{3,2,1,0:T(8,128)(2,1)S(1)}, bf16[2,5,64,128]{3,2,1,0:T(8,128)(2,1)S(1)}, u32[]{:S(2)}, u32[]{:S(2)}) collective-permute-start(bf16[2,5,64,128]{3,2,1,0:T(8,128)(2,1)S(1)} %get-tuple-element.71), channel_id=1, source_target_pairs={{0,96},{16,112},{32,0},{48,16},{64,32},{80,48},{96,64},{112,80},{1... | collective-permute-start | bytes 491528 | tf_op jit(solution)/shard_map/ppermute | solution.py:46
  8.4 0.9 copy-start.2
  14.4 2.5 %collective-permute-start.3 = (bf16[5,64,128]{2,1,0:T(8,128)(2,1)S(1)}, bf16[5,64,128]{2,1,0:T(8,128)(2,1)S(1)}, u32[]{:S(2)}, u32[]{:S(2)}) collective-permute-start(bf16[5,64,128]{2,1,0:T(8,128)(2,1)S(1)} %get-tuple-element.139), channel_id=1, source_target_pairs={{0,16},{16,0},{32,48},{48,32},{64,80},{80,64},{96,112},{112,96},{1... | collective-permute-start | bytes 245768 | tf_op jit(solution)/shard_map/ppermute | solution.py:50
  16.0 1.4 %collective-permute-start.4 = (bf16[5,64,128]{2,1,0:T(8,128)(2,1)S(1)}, bf16[5,64,128]{2,1,0:T(8,128)(2,1)S(1)}, u32[]{:S(2)}, u32[]{:S(2)}) collective-permute-start(bf16[5,64,128]{2,1,0:T(8,128)(2,1)S(1)} %get-tuple-element.137), channel_id=1, source_target_pairs={{0,16},{16,0},{32,48},{48,32},{64,80},{80,64},{96,112},{112,96},{1... | collective-permute-start | bytes 245768 | tf_op jit(solution)/shard_map/ppermute | solution.py:50
  16.1 1.5 %collective-permute-start.5 = (bf16[5,64,128]{2,1,0:T(8,128)(2,1)S(1)}, bf16[5,64,128]{2,1,0:T(8,128)(2,1)S(1)}, u32[]{:S(2)}, u32[]{:S(2)}) collective-permute-start(bf16[5,64,128]{2,1,0:T(8,128)(2,1)S(1)} %get-tuple-element.135), channel_id=1, source_target_pairs={{0,16},{16,0},{32,48},{48,32},{64,80},{80,64},{96,112},{112,96},{1... | collective-permute-start | bytes 245768 | tf_op jit(solution)/shard_map/ppermute | solution.py:50
  16.7 1.4 %collective-permute-start.6 = (bf16[5,64,128]{2,1,0:T(8,128)(2,1)S(1)}, bf16[5,64,128]{2,1,0:T(8,128)(2,1)S(1)}, u32[]{:S(2)}, u32[]{:S(2)}) collective-permute-start(bf16[5,64,128]{2,1,0:T(8,128)(2,1)S(1)} %get-tuple-element.133), channel_id=1, source_target_pairs={{0,16},{16,0},{32,48},{48,32},{64,80},{80,64},{96,112},{112,96},{1... | collective-permute-start | bytes 245768 | tf_op jit(solution)/shard_map/ppermute | solution.py:50
  21.9 22.1 %copy-start.1 = (bf16[16,64,3,512]{3,1,2,0:T(8,128)(2,1)S(1)}, bf16[16,64,3,512]{3,1,2,0:T(8,128)(2,1)}, u32[]{:S(2)}) copy-start(bf16[16,64,3,512]{3,1,2,0:T(8,128)(2,1)} %param.10) | copy-start | bytes 9437188
  21.9 2.0 %collective-permute-start.7 = (bf16[3,64,1024]{2,1,0:T(8,128)(2,1)S(1)}, bf16[3,64,1024]{2,1,0:T(8,128)(2,1)S(1)}, u32[]{:S(2)}, u32[]{:S(2)}) collective-permute-start(bf16[3,64,1024]{2,1,0:T(8,128)(2,1)S(1)} %get-tuple-element.86.refs_0_), channel_id=1, source_target_pairs={{0,16},{16,0},{32,48},{48,32},{64,80},{80,64},{96,112},{112,96},{1... | collective-permute-start | bytes 1179656 | tf_op jit(solution)/shard_map/ppermute | solution.py:50
  22.0 6.9 %collective-permute-start.8 = (bf16[3,64,1024]{2,1,0:T(8,128)(2,1)S(1)}, bf16[3,64,1024]{2,1,0:T(8,128)(2,1)S(1)}, u32[]{:S(2)}, u32[]{:S(2)}) collective-permute-start(bf16[3,64,1024]{2,1,0:T(8,128)(2,1)S(1)} %get-tuple-element.86.refs_0_), channel_id=1, source_target_pairs={{0,32},{16,112},{32,64},{48,16},{64,96},{80,48},{96,0},{112,80},{1... | collective-permute-start | bytes 1179656 | tf_op jit(solution)/shard_map/ppermute | solution.py:62
  23.9 15.2 %collective-permute-start.9 = (bf16[3,64,1024]{2,1,0:T(8,128)(2,1)S(1)}, bf16[3,64,1024]{2,1,0:T(8,128)(2,1)S(1)}, u32[]{:S(2)}, u32[]{:S(2)}) collective-permute-start(bf16[3,64,1024]{2,1,0:T(8,128)(2,1)S(1)} %collective-permute-done.7.refs_1_), channel_id=1, source_target_pairs={{0,32},{16,112},{32,64},{48,16},{64,96},{80,48},{96,0},{112,80},{1... | collective-permute-start | bytes 1179656 | tf_op jit(solution)/shard_map/ppermute | solution.py:62
  29.0 11.6 %collective-permute-start.12 = (bf16[3,64,1024]{2,1,0:T(8,128)(2,1)S(1)}, bf16[3,64,1024]{2,1,0:T(8,128)(2,1)S(1)}, u32[]{:S(2)}, u32[]{:S(2)}) collective-permute-start(bf16[3,64,1024]{2,1,0:T(8,128)(2,1)S(1)} %collective-permute-done.8.refs_2_), channel_id=1, source_target_pairs={{0,32},{16,112},{32,64},{48,16},{64,96},{80,48},{96,0},{112,80},{1... | collective-permute-start | bytes 1179656 | tf_op jit(solution)/shard_map/ppermute | solution.py:62
  32.4 5.6 %collective-permute-start.13 = (bf16[64,1024]{1,0:T(8,128)(2,1)S(1)}, bf16[64,1024]{1,0:T(8,128)(2,1)S(1)}, u32[]{:S(2)}, u32[]{:S(2)}) collective-permute-start(bf16[64,1024]{1,0:T(8,128)(2,1)S(1)} %join_features.1.refs_0_), channel_id=1, source_target_pairs={{0,1},{1,2},{2,3},{3,0},{4,5},{5,6},{6,7},{7,4},{8,9},{9,10},{10,1... | collective-permute-start | bytes 393224 | tf_op jit(solution)/shard_map/ppermute | solution.py:106
  33.8 6.7 %collective-permute-start.14 = (bf16[64,1024]{1,0:T(8,128)(2,1)S(1)}, bf16[64,1024]{1,0:T(8,128)(2,1)S(1)}, u32[]{:S(2)}, u32[]{:S(2)}) collective-permute-start(bf16[64,1024]{1,0:T(8,128)(2,1)S(1)} %join_features.1.refs_0_), channel_id=1, source_target_pairs={{0,2},{1,3},{2,0},{3,1},{4,6},{5,7},{6,4},{7,5},{8,10},{9,11},{10,... | collective-permute-start | bytes 393224 | tf_op jit(solution)/shard_map/ppermute | solution.py:106
  36.5 4.1 %collective-permute-start.15 = (bf16[64,1024]{1,0:T(8,128)(2,1)S(1)}, bf16[64,1024]{1,0:T(8,128)(2,1)S(1)}, u32[]{:S(2)}, u32[]{:S(2)}) collective-permute-start(bf16[64,1024]{1,0:T(8,128)(2,1)S(1)} %join_features.1.refs_0_), channel_id=1, source_target_pairs={{0,3},{1,0},{2,1},{3,2},{4,7},{5,4},{6,5},{7,6},{8,11},{9,8},{10,9... | collective-permute-start | bytes 393224 | tf_op jit(solution)/shard_map/ppermute | solution.py:106
  37.9 4.7 %collective-permute-start.10 = (bf16[3,64,1024]{2,1,0:T(8,128)(2,1)S(1)}, bf16[3,64,1024]{2,1,0:T(8,128)(2,1)S(1)}, u32[]{:S(2)}, u32[]{:S(2)}) collective-permute-start(bf16[3,64,1024]{2,1,0:T(8,128)(2,1)S(1)} %collective-permute-done.8.refs_2_), channel_id=1, source_target_pairs={{0,16},{16,0},{32,48},{48,32},{64,80},{80,64},{96,112},{112,96},{1... | collective-permute-start | bytes 1179656 | tf_op jit(solution)/shard_map/ppermute | solution.py:50
  39.2 3.5 %collective-permute-start.11 = (bf16[3,64,1024]{2,1,0:T(8,128)(2,1)S(1)}, bf16[3,64,1024]{2,1,0:T(8,128)(2,1)S(1)}, u32[]{:S(2)}, u32[]{:S(2)}) collective-permute-start(bf16[3,64,1024]{2,1,0:T(8,128)(2,1)S(1)} %collective-permute-done.9.refs_3_), channel_id=1, source_target_pairs={{0,16},{16,0},{32,48},{48,32},{64,80},{80,64},{96,112},{112,96},{1... | collective-permute-start | bytes 1179656 | tf_op jit(solution)/shard_map/ppermute | solution.py:50
  40.6 3.4 %collective-permute-start.16 = (bf16[3,64,1024]{2,1,0:T(8,128)(2,1)S(1)}, bf16[3,64,1024]{2,1,0:T(8,128)(2,1)S(1)}, u32[]{:S(2)}, u32[]{:S(2)}) collective-permute-start(bf16[3,64,1024]{2,1,0:T(8,128)(2,1)S(1)} %collective-permute-done.12.refs_2_), channel_id=1, source_target_pairs={{0,16},{16,0},{32,48},{48,32},{64,80},{80,64},{96,112},{112,96},{1... | collective-permute-start | bytes 1179656 | tf_op jit(solution)/shard_map/ppermute | solution.py:50
  47.2 9.6 %collective-permute-start.17 = (bf16[4,64,1024]{2,1,0:T(8,128)(2,1)S(1)}, bf16[4,64,1024]{2,1,0:T(8,128)(2,1)S(1)}, u32[]{:S(2)}, u32[]{:S(2)}) collective-permute-start(bf16[4,64,1024]{2,1,0:T(8,128)(2,1)S(1)} %get-tuple-element.103), channel_id=1, source_target_pairs={{0,4},{1,5},{2,6},{3,7},{4,8},{5,9},{6,10},{7,11},{8,12},{9,13},{1... | collective-permute-start | bytes 1572872 | tf_op jit(solution)/shard_map/ppermute | solution.py:106
  47.9 15.0 %collective-permute-start.18 = (bf16[4,64,1024]{2,1,0:T(8,128)(2,1)S(1)}, bf16[4,64,1024]{2,1,0:T(8,128)(2,1)S(1)}, u32[]{:S(2)}, u32[]{:S(2)}) collective-permute-start(bf16[4,64,1024]{2,1,0:T(8,128)(2,1)S(1)} %get-tuple-element.104), channel_id=1, source_target_pairs={{0,8},{1,9},{2,10},{3,11},{4,12},{5,13},{6,14},{7,15},{8,0},{9,1},... | collective-permute-start | bytes 1572872 | tf_op jit(solution)/shard_map/ppermute | solution.py:106
  50.4 12.6 %collective-permute-start.19 = (bf16[4,64,1024]{2,1,0:T(8,128)(2,1)S(1)}, bf16[4,64,1024]{2,1,0:T(8,128)(2,1)S(1)}, u32[]{:S(2)}, u32[]{:S(2)}) collective-permute-start(bf16[4,64,1024]{2,1,0:T(8,128)(2,1)S(1)} %get-tuple-element.105), channel_id=1, source_target_pairs={{0,12},{1,13},{2,14},{3,15},{4,0},{5,1},{6,2},{7,3},{8,4},{9,5},{1... | collective-permute-start | bytes 1572872 | tf_op jit(solution)/shard_map/ppermute | solution.py:106
  51.6 16.5 %collective-permute-start.20 = (bf16[4,64,1024]{2,1,0:T(8,128)(2,1)S(1)}, bf16[4,64,1024]{2,1,0:T(8,128)(2,1)S(1)}, u32[]{:S(2)}, u32[]{:S(2)}) collective-permute-start(bf16[4,64,1024]{2,1,0:T(8,128)(2,1)S(1)} %stack_features.1.refs_0_), channel_id=1, source_target_pairs={{0,4},{1,5},{2,6},{3,7},{4,8},{5,9},{6,10},{7,11},{8,12},{9,13},{1... | collective-permute-start | bytes 1572872 | tf_op jit(solution)/shard_map/ppermute | solution.py:106
  52.6 16.1 %collective-permute-start.21 = (bf16[4,64,1024]{2,1,0:T(8,128)(2,1)S(1)}, bf16[4,64,1024]{2,1,0:T(8,128)(2,1)S(1)}, u32[]{:S(2)}, u32[]{:S(2)}) collective-permute-start(bf16[4,64,1024]{2,1,0:T(8,128)(2,1)S(1)} %stack_features.1.refs_0_), channel_id=1, source_target_pairs={{0,12},{1,13},{2,14},{3,15},{4,0},{5,1},{6,2},{7,3},{8,4},{9,5},{1... | collective-permute-start | bytes 1572872 | tf_op jit(solution)/shard_map/ppermute | solution.py:106
  54.3 19.3 %copy-start = (bf16[1536,1024]{1,0:T(8,128)(2,1)S(1)}, bf16[1536,1024]{1,0:T(8,128)(2,1)}, u32[]{:S(2)}) copy-start(bf16[1536,1024]{1,0:T(8,128)(2,1)} %get-tuple-element.114.whole) | copy-start | bytes 9437188
  56.8 26.4 %collective-permute-start.28 = (bf16[4,64,1024]{2,1,0:T(8,128)(2,1)S(1)}, bf16[4,64,1024]{2,1,0:T(8,128)(2,1)S(1)}, u32[]{:S(2)}, u32[]{:S(2)}) collective-permute-start(bf16[4,64,1024]{2,1,0:T(8,128)(2,1)S(1)} %stack_features.1.refs_0_), channel_id=1, source_target_pairs={{0,8},{1,9},{2,10},{3,11},{4,12},{5,13},{6,14},{7,15},{8,0},{9,1},... | collective-permute-start | bytes 1572872 | tf_op jit(solution)/shard_map/ppermute | solution.py:106
  68.7 9.1 %collective-permute-start.22 = (bf16[64,1024]{1,0:T(8,128)(2,1)S(1)}, bf16[64,1024]{1,0:T(8,128)(2,1)S(1)}, u32[]{:S(2)}, u32[]{:S(2)}) collective-permute-start(bf16[64,1024]{1,0:T(8,128)(2,1)S(1)} %get-tuple-element.111), channel_id=1, source_target_pairs={{0,1},{1,2},{2,3},{3,0},{4,5},{5,6},{6,7},{7,4},{8,9},{9,10},{10,1... | collective-permute-start | bytes 393224 | tf_op jit(solution)/shard_map/ppermute | solution.py:106
  70.0 8.3 %collective-permute-start.23 = (bf16[64,1024]{1,0:T(8,128)(2,1)S(1)}, bf16[64,1024]{1,0:T(8,128)(2,1)S(1)}, u32[]{:S(2)}, u32[]{:S(2)}) collective-permute-start(bf16[64,1024]{1,0:T(8,128)(2,1)S(1)} %get-tuple-element.112), channel_id=1, source_target_pairs={{0,2},{1,3},{2,0},{3,1},{4,6},{5,7},{6,4},{7,5},{8,10},{9,11},{10,... | collective-permute-start | bytes 393224 | tf_op jit(solution)/shard_map/ppermute | solution.py:106
  72.6 5.7 %collective-permute-start.24 = (bf16[64,1024]{1,0:T(8,128)(2,1)S(1)}, bf16[64,1024]{1,0:T(8,128)(2,1)S(1)}, u32[]{:S(2)}, u32[]{:S(2)}) collective-permute-start(bf16[64,1024]{1,0:T(8,128)(2,1)S(1)} %get-tuple-element.113), channel_id=1, source_target_pairs={{0,3},{1,0},{2,1},{3,2},{4,7},{5,4},{6,5},{7,6},{8,11},{9,8},{10,9... | collective-permute-start | bytes 393224 | tf_op jit(solution)/shard_map/ppermute | solution.py:106
  79.0 6.7 %collective-permute-start.25 = (bf16[2,64,128]{2,1,0:T(8,128)(2,1)S(1)}, bf16[2,64,128]{2,1,0:T(8,128)(2,1)S(1)}, u32[]{:S(2)}, u32[]{:S(2)}) collective-permute-start(bf16[2,64,128]{2,1,0:T(8,128)(2,1)S(1)} %get-tuple-element.123), channel_id=1, source_target_pairs={{0,32},{16,48},{32,64},{48,80},{64,96},{80,112},{96,0},{112,16},{1... | collective-permute-start | bytes 98312 | tf_op jit(solution)/shard_map/ppermute | solution.py:46
  80.1 5.6 %collective-permute-start.26 = (bf16[2,64,128]{2,1,0:T(8,128)(2,1)S(1)}, bf16[2,64,128]{2,1,0:T(8,128)(2,1)S(1)}, u32[]{:S(2)}, u32[]{:S(2)}) collective-permute-start(bf16[2,64,128]{2,1,0:T(8,128)(2,1)S(1)} %get-tuple-element.124), channel_id=1, source_target_pairs={{0,64},{16,80},{32,96},{48,112},{64,0},{80,16},{96,32},{112,48},{1... | collective-permute-start | bytes 98312 | tf_op jit(solution)/shard_map/ppermute | solution.py:46
  83.1 3.0 %collective-permute-start.27 = (bf16[2,64,128]{2,1,0:T(8,128)(2,1)S(1)}, bf16[2,64,128]{2,1,0:T(8,128)(2,1)S(1)}, u32[]{:S(2)}, u32[]{:S(2)}) collective-permute-start(bf16[2,64,128]{2,1,0:T(8,128)(2,1)S(1)} %get-tuple-element.125), channel_id=1, source_target_pairs={{0,96},{16,112},{32,0},{48,16},{64,32},{80,48},{96,64},{112,80},{1... | collective-permute-start | bytes 98312 | tf_op jit(solution)/shard_map/ppermute | solution.py:46
  86.1 2.9 %collective-permute-start.29 = (bf16[64,128]{1,0:T(8,128)(2,1)S(1)}, bf16[64,128]{1,0:T(8,128)(2,1)S(1)}, u32[]{:S(2)}, u32[]{:S(2)}) collective-permute-start(bf16[64,128]{1,0:T(8,128)(2,1)S(1)} %get-tuple-element.147), channel_id=1, source_target_pairs={{0,16},{16,0},{32,48},{48,32},{64,80},{80,64},{96,112},{112,96},{1... | collective-permute-start | bytes 49160 | tf_op jit(solution)/shard_map/ppermute | solution.py:50
  88.2 1.2 %collective-permute-start.30 = (bf16[64,128]{1,0:T(8,128)(2,1)S(1)}, bf16[64,128]{1,0:T(8,128)(2,1)S(1)}, u32[]{:S(2)}, u32[]{:S(2)}) collective-permute-start(bf16[64,128]{1,0:T(8,128)(2,1)S(1)} %get-tuple-element.145), channel_id=1, source_target_pairs={{0,16},{16,0},{32,48},{48,32},{64,80},{80,64},{96,112},{112,96},{1... | collective-permute-start | bytes 49160 | tf_op jit(solution)/shard_map/ppermute | solution.py:50
  88.2 1.3 %collective-permute-start.31 = (bf16[64,128]{1,0:T(8,128)(2,1)S(1)}, bf16[64,128]{1,0:T(8,128)(2,1)S(1)}, u32[]{:S(2)}, u32[]{:S(2)}) collective-permute-start(bf16[64,128]{1,0:T(8,128)(2,1)S(1)} %get-tuple-element.143), channel_id=1, source_target_pairs={{0,16},{16,0},{32,48},{48,32},{64,80},{80,64},{96,112},{112,96},{1... | collective-permute-start | bytes 49160 | tf_op jit(solution)/shard_map/ppermute | solution.py:50
  88.7 1.2 %collective-permute-start.32 = (bf16[64,128]{1,0:T(8,128)(2,1)S(1)}, bf16[64,128]{1,0:T(8,128)(2,1)S(1)}, u32[]{:S(2)}, u32[]{:S(2)}) collective-permute-start(bf16[64,128]{1,0:T(8,128)(2,1)S(1)} %get-tuple-element.141), channel_id=1, source_target_pairs={{0,16},{16,0},{32,48},{48,32},{64,80},{80,64},{96,112},{112,96},{1... | collective-permute-start | bytes 49160 | tf_op jit(solution)/shard_map/ppermute | solution.py:50

commit v5 on v4

--- a/solution.py
+++ b/solution.py
@@ -468,9 +468,10 @@
     grads, grad_taps = convolutions(me, pieces, table, (hr, hi, hn))
     own, sibling, next1, next2 = gather_start(grads)
     sibling, pieces = tie(sibling, pieces)
-    last = spin(next1)
     feats = join_features(me, pieces)
     feats = [feats] + [shift_ring(feats, s, first=False) for s in (1, 2, 3)]
+    next1, feats[1] = tie(next1, feats[1])
+    last = spin(next1)
     last, feats = tie(last, feats)
     pieces = (own, sibling, next1, next2, swap_core(next1), swap_core(next2))
     whole = assemble(me, pieces, (0, 1, 2, 3, 5, 6))

time: 91.3 us -> 89.8 us (0.984)
  waiting for transfers between devices: 22.7 us -> 15.4 us
  starting transfers between devices: 41.8 us -> 47.6 us
    ppermute x12, starting transfers between devices: 17.1 us -> 25.3 us  [shift_ring(): return lax.ppermute(a, ('ctx', 'tp'), pairs)]
    ppermute x12, waiting for transfers between devices: 13.9 us -> 8.56 us  [shift_ring(): return lax.ppermute(a, ('ctx', 'tp'), pairs)]
    ppermute x3, waiting for transfers between devices: 3.48 us -> 1.42 us  [spin(): return lax.ppermute(a, 'ctx', pairs)]
    ppermute x12, starting transfers between devices: 8.53 us -> 7.27 us  [swap_core(): return lax.ppermute(a, 'ctx', [(i, i ^ 1) for i in range(N_CTX)])]
  transfers between devices with their start and end apart: 33 -> 33, of which waited for: 21 -> 18; matrix products, arithmetic and copies ran while one was open for 0% -> 0% of each run, Pallas kernels for 16% -> 16%
where the time goes in v5:
time: 89.8 us; the launch traced here: 89.7 us
  starting transfers between devices  47.6 us (53%)
  Pallas kernels  24.8 us (28%)
  waiting for transfers between devices  15.4 us (17%)
  local copies, waits for them, and re-layouts  0.97 us (1%)
    ppermute x12, starting transfers between devices, shift_ring(): return lax.ppermute(a, ('ctx', 'tp'), pairs)  25.3 us
    ppermute x6, starting transfers between devices, shift_x(): lax.ppermute(a, 'ctx', [(i, (i + 2 * steps) % N_CTX) for i in range(N_CTX)])  9.64 us
    ppermute x12, waiting for transfers between devices, shift_ring(): return lax.ppermute(a, ('ctx', 'tp'), pairs)  8.56 us
    ppermute x12, starting transfers between devices, swap_core(): return lax.ppermute(a, 'ctx', [(i, i ^ 1) for i in range(N_CTX)])  7.27 us
    pallas_call x2, Pallas kernels, weight_grad(): pl.pallas_call(functools.partial(weight_kernel, steps), out_shape=pltpu.H...  6.54 us
    ppermute x3, starting transfers between devices, spin(): return lax.ppermute(a, 'ctx', pairs)  5.42 us
    pallas_call x2, Pallas kernels, value_part(): pl.pallas_call(functools.partial(value_kernel, steps, which), out_shape=s...  4.73 us
    pallas_call x1, Pallas kernels, convolutions(): pl.pallas_call(conv_kernel, out_shape=[like(3, chans, n), like(chans, n)]...  3.81 us
  transfers between devices with their start and end apart: 33, of which 18 were waited for; matrix products, arithmetic and copies ran while one was open for 0% of the time, Pallas kernels for 16%

profile of v5, /device:TPU:1, one launch (start us, length us, event | category | flops | bytes accessed | tf_op | source)
XLA Modules:
  0.0 89.7 jit_solution(1072971061611902465)
XLA Ops:
  0.7 2.0 %prepare.1 = (bf16[2,5,64,128]{3,2,1,0:T(8,128)(2,1)S(1)}, bf16[2,5,64,128]{3,2,1,0:T(8,128)(2,1)S(1)}, bf16[2,5,64,128]{3,2,1,0:T(8,128)(2,1)S(1)}, bf16[2,5,64,128]{3,2,1,0:T(8,128)(2,1)S(1)}) custom-call(s32[2]{0:T(128)S(1)} %pad_add_fusion.me, bf16[128,512]{1,0:T(8,128)(2,1)} %refs_0_.2, bf16[128,512]{1,0:T(8,128)(2,1)} %refs_1_.2, ...), custom_call_target="tpu_custom_call" | custom-call | tf_op jit(solution)/shard_map/prepare/pallas_call | solution.py:134
  2.7 2.1 %collective-permute-start = (bf16[2,5,64,128]{3,2,1,0:T(8,128)(2,1)S(1)}, bf16[2,5,64,128]{3,2,1,0:T(8,128)(2,1)S(1)}, u32[]{:S(2)}, u32[]{:S(2)}) collective-permute-start(bf16[2,5,64,128]{3,2,1,0:T(8,128)(2,1)S(1)} %get-tuple-element.71), channel_id=1, source_target_pairs={{0,32},{16,48},{32,64},{48,80},{64,96},{80,112},{96,0},{112,16},{1... | collective-permute-start | bytes 491528 | tf_op jit(solution)/shard_map/ppermute | solution.py:46
  4.8 2.5 %collective-permute-start.1 = (bf16[2,5,64,128]{3,2,1,0:T(8,128)(2,1)S(1)}, bf16[2,5,64,128]{3,2,1,0:T(8,128)(2,1)S(1)}, u32[]{:S(2)}, u32[]{:S(2)}) collective-permute-start(bf16[2,5,64,128]{3,2,1,0:T(8,128)(2,1)S(1)} %get-tuple-element.72), channel_id=1, source_target_pairs={{0,64},{16,80},{32,96},{48,112},{64,0},{80,16},{96,32},{112,48},{1... | collective-permute-start | bytes 491528 | tf_op jit(solution)/shard_map/ppermute | solution.py:46
  7.3 1.2 %collective-permute-start.2 = (bf16[2,5,64,128]{3,2,1,0:T(8,128)(2,1)S(1)}, bf16[2,5,64,128]{3,2,1,0:T(8,128)(2,1)S(1)}, u32[]{:S(2)}, u32[]{:S(2)}) collective-permute-start(bf16[2,5,64,128]{3,2,1,0:T(8,128)(2,1)S(1)} %get-tuple-element.73), channel_id=1, source_target_pairs={{0,96},{16,112},{32,0},{48,16},{64,32},{80,48},{96,64},{112,80},{1... | collective-permute-start | bytes 491528 | tf_op jit(solution)/shard_map/ppermute | solution.py:46
  8.4 0.9 %copy-done.2 = bf16[1,64,1024]{2,1,0:T(8,128)(2,1)S(1)} copy-done((bf16[1,64,1024]{2,1,0:T(8,128)(2,1)S(1)}, bf16[1,64,1024]{2,1,0:T(8,128)(2,1)}, u32[]{:S(2)}) %copy-start.2) | copy-done | bytes 131096
  9.3 3.1 %taps_spectrum.1 = (bf16[1024,1024]{1,0:T(8,128)(2,1)S(1)}, bf16[1024,1024]{1,0:T(8,128)(2,1)S(1)}, f32[64,1024]{1,0:T(8,128)S(1)}, f32[64,1024]{1,0:T(8,128)S(1)}, f32[64,1]{1,0:T(8,128)S(1)}) custom-call(bf16[1024,1024]{1,0:T(8,128)(2,1)} %constant.13.clone.refs_0_, bf16[1024,1024]{1,0:T(8,128)(2,1)} %constant.14.clone.refs_1_, bf16[64,1024]{1,0:T(8,128)(2,1)S(1)} %bitcast.40), custom_call_target="tpu_custom_call" | custom-call | flops 536870912 | bytes 8388608 | tf_op jit(solution)/shard_map/taps_spectrum/pallas_call | solution.py:224
  12.4 2.0 %collective-permute-done.1 = bf16[2,5,64,128]{3,2,1,0:T(8,128)(2,1)S(1)} collective-permute-done((bf16[2,5,64,128]{3,2,1,0:T(8,128)(2,1)S(1)}, bf16[2,5,64,128]{3,2,1,0:T(8,128)(2,1)S(1)}, u32[]{:S(2)}, u32[]{:S(2)}) %collective-permute-start.1) | collective-permute-done | bytes 163872 | tf_op jit(solution)/shard_map/ppermute | solution.py:46
  14.4 1.6 %collective-permute-start.3 = (bf16[5,64,128]{2,1,0:T(8,128)(2,1)S(1)}, bf16[5,64,128]{2,1,0:T(8,128)(2,1)S(1)}, u32[]{:S(2)}, u32[]{:S(2)}) collective-permute-start(bf16[5,64,128]{2,1,0:T(8,128)(2,1)S(1)} %get-tuple-element.143), channel_id=1, source_target_pairs={{0,16},{16,0},{32,48},{48,32},{64,80},{80,64},{96,112},{112,96},{1... | collective-permute-start | bytes 245768 | tf_op jit(solution)/shard_map/ppermute | solution.py:50
  16.0 0.1 collective-permute-start.4
  16.1 0.6 collective-permute-start.5
  16.7 0.1 collective-permute-start.6
  16.8 0.1 collective-permute-done.3.refs_4_
  16.9 0.4 collective-permute-done.4.refs_5_
  17.4 0.2 collective-permute-done.5.refs_6_
  17.6 0.4 collective-permute-done.6.refs_7_
  18.1 3.8 %convolutions.1 = (bf16[3,64,1024]{2,1,0:T(8,128)(2,1)S(1)}, bf16[64,1024]{1,0:T(8,128)(2,1)}) custom-call(s32[2]{0:T(128)S(1)} %pad_add_fusion.me, bf16[5,64,128]{2,1,0:T(8,128)(2,1)S(1)} %get-tuple-element.90.refs_0_, bf16[5,64,128]{2,1,0:T(8,128)(2,1)S(1)} %get-tuple-element.91.refs_1_, bf16[5,64,128]{2,1,0:T(8,128)(2,1)S(1)} %get-tuple-element.92.refs_2_, ...), custom_call_target="tpu_custom_call" | custom-call | flops 2147483648 | bytes 8388608 | tf_op jit(solution)/shard_map/convolutions/pallas_call | solution.py:263
  21.9 0.1 collective-permute-start.7
  22.0 1.9 %collective-permute-start.8 = (bf16[3,64,1024]{2,1,0:T(8,128)(2,1)S(1)}, bf16[3,64,1024]{2,1,0:T(8,128)(2,1)S(1)}, u32[]{:S(2)}, u32[]{:S(2)}) collective-permute-start(bf16[3,64,1024]{2,1,0:T(8,128)(2,1)S(1)} %get-tuple-element.88.refs_0_), channel_id=1, source_target_pairs={{0,32},{16,112},{32,64},{48,16},{64,96},{80,48},{96,0},{112,80},{1... | collective-permute-start | bytes 1179656 | tf_op jit(solution)/shard_map/ppermute | solution.py:62
  23.9 0.6 join_features.1.refs_0_
  24.5 1.5 %collective-permute-start.9 = (bf16[64,1024]{1,0:T(8,128)(2,1)S(1)}, bf16[64,1024]{1,0:T(8,128)(2,1)S(1)}, u32[]{:S(2)}, u32[]{:S(2)}) collective-permute-start(bf16[64,1024]{1,0:T(8,128)(2,1)S(1)} %join_features.1.refs_0_), channel_id=1, source_target_pairs={{0,1},{1,2},{2,3},{3,0},{4,5},{5,6},{6,7},{7,4},{8,9},{9,10},{10,1... | collective-permute-start | bytes 393224 | tf_op jit(solution)/shard_map/ppermute | solution.py:106
  26.0 1.6 %collective-permute-start.10 = (bf16[3,64,1024]{2,1,0:T(8,128)(2,1)S(1)}, bf16[3,64,1024]{2,1,0:T(8,128)(2,1)S(1)}, u32[]{:S(2)}, u32[]{:S(2)}) collective-permute-start(bf16[3,64,1024]{2,1,0:T(8,128)(2,1)S(1)} %collective-permute-done.7.refs_1_), channel_id=1, source_target_pairs={{0,32},{16,112},{32,64},{48,16},{64,96},{80,48},{96,0},{112,80},{1... | collective-permute-start | bytes 1179656 | tf_op jit(solution)/shard_map/ppermute | solution.py:62
  27.6 1.4 %collective-permute-done.8.refs_2_ = bf16[3,64,1024]{2,1,0:T(8,128)(2,1)S(1)} collective-permute-done((bf16[3,64,1024]{2,1,0:T(8,128)(2,1)S(1)}, bf16[3,64,1024]{2,1,0:T(8,128)(2,1)S(1)}, u32[]{:S(2)}, u32[]{:S(2)}) %collective-permute-start.8) | collective-permute-done | bytes 393248 | tf_op jit(solution)/shard_map/ppermute | solution.py:62
  29.0 1.1 %collective-permute-done.9.refs_1_ = bf16[64,1024]{1,0:T(8,128)(2,1)S(1)} collective-permute-done((bf16[64,1024]{1,0:T(8,128)(2,1)S(1)}, bf16[64,1024]{1,0:T(8,128)(2,1)S(1)}, u32[]{:S(2)}, u32[]{:S(2)}) %collective-permute-start.9) | collective-permute-done | bytes 131104 | tf_op jit(solution)/shard_map/ppermute | solution.py:106
  30.1 2.0 %collective-permute-start.13 = (bf16[3,64,1024]{2,1,0:T(8,128)(2,1)S(1)}, bf16[3,64,1024]{2,1,0:T(8,128)(2,1)S(1)}, u32[]{:S(2)}, u32[]{:S(2)}) collective-permute-start(bf16[3,64,1024]{2,1,0:T(8,128)(2,1)S(1)} %collective-permute-done.8.refs_2_), channel_id=1, source_target_pairs={{0,32},{16,112},{32,64},{48,16},{64,96},{80,48},{96,0},{112,80},{1... | collective-permute-start | bytes 1179656 | tf_op jit(solution)/shard_map/ppermute | solution.py:62
  32.1 3.0 %collective-permute-start.14 = (bf16[64,1024]{1,0:T(8,128)(2,1)S(1)}, bf16[64,1024]{1,0:T(8,128)(2,1)S(1)}, u32[]{:S(2)}, u32[]{:S(2)}) collective-permute-start(bf16[64,1024]{1,0:T(8,128)(2,1)S(1)} %join_features.1.refs_0_), channel_id=1, source_target_pairs={{0,2},{1,3},{2,0},{3,1},{4,6},{5,7},{6,4},{7,5},{8,10},{9,11},{10,... | collective-permute-start | bytes 393224 | tf_op jit(solution)/shard_map/ppermute | solution.py:106
  35.1 0.8 collective-permute-start.15
  35.9 0.3 collective-permute-start.11
  36.1 0.3 collective-permute-start.12
  36.4 1.4 %collective-permute-done.14.refs_2_ = bf16[64,1024]{1,0:T(8,128)(2,1)S(1)} collective-permute-done((bf16[64,1024]{1,0:T(8,128)(2,1)S(1)}, bf16[64,1024]{1,0:T(8,128)(2,1)S(1)}, u32[]{:S(2)}, u32[]{:S(2)}) %collective-permute-start.14) | collective-permute-done | bytes 131104 | tf_op jit(solution)/shard_map/ppermute | solution.py:106
  37.7 1.8 %collective-permute-done.15.refs_3_ = bf16[64,1024]{1,0:T(8,128)(2,1)S(1)} collective-permute-done((bf16[64,1024]{1,0:T(8,128)(2,1)S(1)}, bf16[64,1024]{1,0:T(8,128)(2,1)S(1)}, u32[]{:S(2)}, u32[]{:S(2)}) %collective-permute-start.15) | collective-permute-done | bytes 131104 | tf_op jit(solution)/shard_map/ppermute | solution.py:106
  39.5 1.2 %collective-permute-start.16 = (bf16[3,64,1024]{2,1,0:T(8,128)(2,1)S(1)}, bf16[3,64,1024]{2,1,0:T(8,128)(2,1)S(1)}, u32[]{:S(2)}, u32[]{:S(2)}) collective-permute-start(bf16[3,64,1024]{2,1,0:T(8,128)(2,1)S(1)} %collective-permute-done.13.refs_2_), channel_id=1, source_target_pairs={{0,16},{16,0},{32,48},{48,32},{64,80},{80,64},{96,112},{112,96},{1... | collective-permute-start | bytes 1179656 | tf_op jit(solution)/shard_map/ppermute | solution.py:50
  40.8 0.7 assemble.1.refs_1_
  41.5 0.6 collective-permute-done.16.refs_3_
  42.1 3.2 %value_part.2 = (bf16[4,64,1024]{2,1,0:T(8,128)(2,1)S(1)}, bf16[4,64,1024]{2,1,0:T(8,128)(2,1)S(1)}, bf16[4,64,1024]{2,1,0:T(8,128)(2,1)S(1)}, bf16[1536,1024]{1,0:T(8,128)(2,1)S(1)}, bf16[1536,1024]{1,0:T(8,128)(2,1)}) custom-call(s32[2]{0:T(128)S(1)} %pad_add_fusion.me, bf16[16,3,64,512]{3,2,1,0:T(8,128)(2,1)S(1)} %bitcast.38, ...), custom_call_target="tpu_custom_call", output_to_operand_aliasing={{3}: (2, {})} | custom-call | flops 2415919104 | bytes 2097152 | tf_op jit(solution)/shard_map/value_part/pallas_call | solution.py:332
  45.3 1.3 %collective-permute-start.17 = (bf16[4,64,1024]{2,1,0:T(8,128)(2,1)S(1)}, bf16[4,64,1024]{2,1,0:T(8,128)(2,1)S(1)}, u32[]{:S(2)}, u32[]{:S(2)}) collective-permute-start(bf16[4,64,1024]{2,1,0:T(8,128)(2,1)S(1)} %get-tuple-element.107), channel_id=1, source_target_pairs={{0,4},{1,5},{2,6},{3,7},{4,8},{5,9},{6,10},{7,11},{8,12},{9,13},{1... | collective-permute-start | bytes 1572872 | tf_op jit(solution)/shard_map/ppermute | solution.py:106
  46.7 3.3 %collective-permute-start.18 = (bf16[4,64,1024]{2,1,0:T(8,128)(2,1)S(1)}, bf16[4,64,1024]{2,1,0:T(8,128)(2,1)S(1)}, u32[]{:S(2)}, u32[]{:S(2)}) collective-permute-start(bf16[4,64,1024]{2,1,0:T(8,128)(2,1)S(1)} %get-tuple-element.108), channel_id=1, source_target_pairs={{0,8},{1,9},{2,10},{3,11},{4,12},{5,13},{6,14},{7,15},{8,0},{9,1},... | collective-permute-start | bytes 1572872 | tf_op jit(solution)/shard_map/ppermute | solution.py:106
  50.0 0.7 collective-permute-start.19
  50.7 0.6 stack_features.1.refs_0_
  51.3 0.8 collective-permute-start.20
  52.1 1.9 %collective-permute-start.21 = (bf16[4,64,1024]{2,1,0:T(8,128)(2,1)S(1)}, bf16[4,64,1024]{2,1,0:T(8,128)(2,1)S(1)}, u32[]{:S(2)}, u32[]{:S(2)}) collective-permute-start(bf16[4,64,1024]{2,1,0:T(8,128)(2,1)S(1)} %stack_features.1.refs_0_), channel_id=1, source_target_pairs={{0,12},{1,13},{2,14},{3,15},{4,0},{5,1},{6,2},{7,3},{8,4},{9,5},{1... | collective-permute-start | bytes 1572872 | tf_op jit(solution)/shard_map/ppermute | solution.py:106
  54.1 1.5 %value_part.3.refs_0_ = bf16[4,64,1024]{2,1,0:T(8,128)(2,1)S(1)} custom-call(s32[2]{0:T(128)S(1)} %pad_add_fusion.me, bf16[16,3,64,512]{3,2,1,0:T(8,128)(2,1)S(1)} %bitcast.39, bf16[1536,1024]{1,0:T(8,128)(2,1)S(1)} %get-tuple-element.101.refs_1_), custom_call_target="tpu_custom_call" | custom-call | flops 805306368 | bytes 2097152 | tf_op jit(solution)/shard_map/value_part/pallas_call | solution.py:332
  55.7 6.9 %collective-permute-start.28 = (bf16[4,64,1024]{2,1,0:T(8,128)(2,1)S(1)}, bf16[4,64,1024]{2,1,0:T(8,128)(2,1)S(1)}, u32[]{:S(2)}, u32[]{:S(2)}) collective-permute-start(bf16[4,64,1024]{2,1,0:T(8,128)(2,1)S(1)} %stack_features.1.refs_0_), channel_id=1, source_target_pairs={{0,8},{1,9},{2,10},{3,11},{4,12},{5,13},{6,14},{7,15},{8,0},{9,1},... | collective-permute-start | bytes 1572872 | tf_op jit(solution)/shard_map/ppermute | solution.py:106
  62.6 0.8 first_sum.1
  63.4 3.5 %collective-permute-done.20.refs_1_ = bf16[4,64,1024]{2,1,0:T(8,128)(2,1)S(1)} collective-permute-done((bf16[4,64,1024]{2,1,0:T(8,128)(2,1)S(1)}, bf16[4,64,1024]{2,1,0:T(8,128)(2,1)S(1)}, u32[]{:S(2)}, u32[]{:S(2)}) %collective-permute-start.20) | collective-permute-done | bytes 524320 | tf_op jit(solution)/shard_map/ppermute | solution.py:106
  66.9 0.7 collective-permute-done.21.refs_2_
  67.6 1.3 %collective-permute-start.22 = (bf16[64,1024]{1,0:T(8,128)(2,1)S(1)}, bf16[64,1024]{1,0:T(8,128)(2,1)S(1)}, u32[]{:S(2)}, u32[]{:S(2)}) collective-permute-start(bf16[64,1024]{1,0:T(8,128)(2,1)S(1)} %get-tuple-element.115), channel_id=1, source_target_pairs={{0,1},{1,2},{2,3},{3,0},{4,5},{5,6},{6,7},{7,4},{8,9},{9,10},{10,1... | collective-permute-start | bytes 393224 | tf_op jit(solution)/shard_map/ppermute | solution.py:106
  68.9 2.6 %collective-permute-start.23 = (bf16[64,1024]{1,0:T(8,128)(2,1)S(1)}, bf16[64,1024]{1,0:T(8,128)(2,1)S(1)}, u32[]{:S(2)}, u32[]{:S(2)}) collective-permute-start(bf16[64,1024]{1,0:T(8,128)(2,1)S(1)} %get-tuple-element.116), channel_id=1, source_target_pairs={{0,2},{1,3},{2,0},{3,1},{4,6},{5,7},{6,4},{7,5},{8,10},{9,11},{10,... | collective-permute-start | bytes 393224 | tf_op jit(solution)/shard_map/ppermute | solution.py:106
  71.5 1.1 %collective-permute-start.24 = (bf16[64,1024]{1,0:T(8,128)(2,1)S(1)}, bf16[64,1024]{1,0:T(8,128)(2,1)S(1)}, u32[]{:S(2)}, u32[]{:S(2)}) collective-permute-start(bf16[64,1024]{1,0:T(8,128)(2,1)S(1)} %get-tuple-element.117), channel_id=1, source_target_pairs={{0,3},{1,0},{2,1},{3,2},{4,7},{5,4},{6,5},{7,6},{8,11},{9,8},{10,9... | collective-permute-start | bytes 393224 | tf_op jit(solution)/shard_map/ppermute | solution.py:106
  72.6 4.1 %weight_grad.2.refs_1_ = bf16[16,3,64,512]{3,2,1,0:T(8,128)(2,1)} custom-call(s32[2]{0:T(128)S(1)} %pad_add_fusion.me, bf16[1536,1024]{1,0:T(8,128)(2,1)S(1)} %copy-done, bf16[4,64,1024]{2,1,0:T(8,128)(2,1)S(1)} %stack_features.1.refs_0_, bf16[4,64,1024]{2,1,0:T(8,128)(2,1)S(1)} %collective-permute-done.20.refs_1_, ...), custom_call_target="tpu_custom_call" | custom-call | flops 2415919104 | bytes 2097152 | tf_op jit(solution)/shard_map/weight_grad/pallas_call | solution.py:369
  76.8 0.7 sum_parts.1
  77.4 0.8 collective-permute-start.25
  78.2 3.0 %collective-permute-start.26 = (bf16[2,64,128]{2,1,0:T(8,128)(2,1)S(1)}, bf16[2,64,128]{2,1,0:T(8,128)(2,1)S(1)}, u32[]{:S(2)}, u32[]{:S(2)}) collective-permute-start(bf16[2,64,128]{2,1,0:T(8,128)(2,1)S(1)} %get-tuple-element.128), channel_id=1, source_target_pairs={{0,64},{16,80},{32,96},{48,112},{64,0},{80,16},{96,32},{112,48},{1... | collective-permute-start | bytes 98312 | tf_op jit(solution)/shard_map/ppermute | solution.py:46
  81.2 0.2 collective-permute-start.27
  81.4 2.4 %weight_grad.3 = bf16[16,3,64,512]{3,2,1,0:T(8,128)(2,1)} custom-call(s32[2]{0:T(128)S(1)} %pad_add_fusion.me, bf16[1536,1024]{1,0:T(8,128)(2,1)S(1)} %copy-done, bf16[4,64,1024]{2,1,0:T(8,128)(2,1)S(1)} %collective-permute-done.28.refs_0_, bf16[16,3,64,512]{3,2,1,0:T(8,128)(2,1)} %weight_grad.2.refs_1_), custom_call_target="tpu_custom_call", output_to_operand_aliasing={{}: (3, {})} | custom-call | flops 805306368 | bytes 2097152 | tf_op jit(solution)/shard_map/weight_grad/pallas_call | solution.py:369
  83.8 0.5 collective-permute-done.27
  84.3 2.4 %collective-permute-start.29 = (bf16[64,128]{1,0:T(8,128)(2,1)S(1)}, bf16[64,128]{1,0:T(8,128)(2,1)S(1)}, u32[]{:S(2)}, u32[]{:S(2)}) collective-permute-start(bf16[64,128]{1,0:T(8,128)(2,1)S(1)} %get-tuple-element.151), channel_id=1, source_target_pairs={{0,16},{16,0},{32,48},{48,32},{64,80},{80,64},{96,112},{112,96},{1... | collective-permute-start | bytes 49160 | tf_op jit(solution)/shard_map/ppermute | solution.py:50
  86.7 0.1 collective-permute-start.30
  86.8 0.4 collective-permute-start.31
  87.2 0.1 collective-permute-start.32
  87.3 0.2 collective-permute-done.29.refs_4_
  87.5 0.3 collective-permute-done.30.refs_5_
  87.9 0.2 collective-permute-done.31.refs_6_
  88.0 0.3 collective-permute-done.32.refs_7_
  88.4 1.3 %finish.1 = bf16[128,512]{1,0:T(8,128)(2,1)} custom-call(s32[2]{0:T(128)S(1)} %pad_add_fusion.me, bf16[64,128]{1,0:T(8,128)(2,1)S(1)} %get-tuple-element.152.refs_0_, bf16[64,128]{1,0:T(8,128)(2,1)S(1)} %get-tuple-element.150.refs_1_, bf16[64,128]{1,0:T(8,128)(2,1)S(1)} %get-tuple-element.148.refs_2_, bf16[64,128]{1,0:T(8,128)(2,1)S(1)} %get-tuple-element.146.refs_3_, ...), custom_call_target="tpu_custom_call" | custom-call | tf_op jit(solution)/shard_map/finish/pallas_call | solution.py:444
  (30 shorter events, 0.3 us)
Async XLA Ops:
  2.7 9.7 %collective-permute-start = (bf16[2,5,64,128]{3,2,1,0:T(8,128)(2,1)S(1)}, bf16[2,5,64,128]{3,2,1,0:T(8,128)(2,1)S(1)}, u32[]{:S(2)}, u32[]{:S(2)}) collective-permute-start(bf16[2,5,64,128]{3,2,1,0:T(8,128)(2,1)S(1)} %get-tuple-element.71), channel_id=1, source_target_pairs={{0,32},{16,48},{32,64},{48,80},{64,96},{80,112},{96,0},{112,16},{1... | collective-permute-start | bytes 491528 | tf_op jit(solution)/shard_map/ppermute | solution.py:46
  4.8 9.6 %collective-permute-start.1 = (bf16[2,5,64,128]{3,2,1,0:T(8,128)(2,1)S(1)}, bf16[2,5,64,128]{3,2,1,0:T(8,128)(2,1)S(1)}, u32[]{:S(2)}, u32[]{:S(2)}) collective-permute-start(bf16[2,5,64,128]{3,2,1,0:T(8,128)(2,1)S(1)} %get-tuple-element.72), channel_id=1, source_target_pairs={{0,64},{16,80},{32,96},{48,112},{64,0},{80,16},{96,32},{112,48},{1... | collective-permute-start | bytes 491528 | tf_op jit(solution)/shard_map/ppermute | solution.py:46
  7.3 7.1 %collective-permute-start.2 = (bf16[2,5,64,128]{3,2,1,0:T(8,128)(2,1)S(1)}, bf16[2,5,64,128]{3,2,1,0:T(8,128)(2,1)S(1)}, u32[]{:S(2)}, u32[]{:S(2)}) collective-permute-start(bf16[2,5,64,128]{3,2,1,0:T(8,128)(2,1)S(1)} %get-tuple-element.73), channel_id=1, source_target_pairs={{0,96},{16,112},{32,0},{48,16},{64,32},{80,48},{96,64},{112,80},{1... | collective-permute-start | bytes 491528 | tf_op jit(solution)/shard_map/ppermute | solution.py:46
  8.4 0.9 %copy-start.2 = (bf16[1,64,1024]{2,1,0:T(8,128)(2,1)S(1)}, bf16[1,64,1024]{2,1,0:T(8,128)(2,1)}, u32[]{:S(2)}) copy-start(bf16[1,64,1024]{2,1,0:T(8,128)(2,1)} %param.11) | copy-start | bytes 393220
  14.4 2.5 %collective-permute-start.3 = (bf16[5,64,128]{2,1,0:T(8,128)(2,1)S(1)}, bf16[5,64,128]{2,1,0:T(8,128)(2,1)S(1)}, u32[]{:S(2)}, u32[]{:S(2)}) collective-permute-start(bf16[5,64,128]{2,1,0:T(8,128)(2,1)S(1)} %get-tuple-element.143), channel_id=1, source_target_pairs={{0,16},{16,0},{32,48},{48,32},{64,80},{80,64},{96,112},{112,96},{1... | collective-permute-start | bytes 245768 | tf_op jit(solution)/shard_map/ppermute | solution.py:50
  16.0 1.4 %collective-permute-start.4 = (bf16[5,64,128]{2,1,0:T(8,128)(2,1)S(1)}, bf16[5,64,128]{2,1,0:T(8,128)(2,1)S(1)}, u32[]{:S(2)}, u32[]{:S(2)}) collective-permute-start(bf16[5,64,128]{2,1,0:T(8,128)(2,1)S(1)} %get-tuple-element.141), channel_id=1, source_target_pairs={{0,16},{16,0},{32,48},{48,32},{64,80},{80,64},{96,112},{112,96},{1... | collective-permute-start | bytes 245768 | tf_op jit(solution)/shard_map/ppermute | solution.py:50
  16.1 1.5 %collective-permute-start.5 = (bf16[5,64,128]{2,1,0:T(8,128)(2,1)S(1)}, bf16[5,64,128]{2,1,0:T(8,128)(2,1)S(1)}, u32[]{:S(2)}, u32[]{:S(2)}) collective-permute-start(bf16[5,64,128]{2,1,0:T(8,128)(2,1)S(1)} %get-tuple-element.139), channel_id=1, source_target_pairs={{0,16},{16,0},{32,48},{48,32},{64,80},{80,64},{96,112},{112,96},{1... | collective-permute-start | bytes 245768 | tf_op jit(solution)/shard_map/ppermute | solution.py:50
  16.7 1.4 %collective-permute-start.6 = (bf16[5,64,128]{2,1,0:T(8,128)(2,1)S(1)}, bf16[5,64,128]{2,1,0:T(8,128)(2,1)S(1)}, u32[]{:S(2)}, u32[]{:S(2)}) collective-permute-start(bf16[5,64,128]{2,1,0:T(8,128)(2,1)S(1)} %get-tuple-element.137), channel_id=1, source_target_pairs={{0,16},{16,0},{32,48},{48,32},{64,80},{80,64},{96,112},{112,96},{1... | collective-permute-start | bytes 245768 | tf_op jit(solution)/shard_map/ppermute | solution.py:50
  21.9 20.2 %copy-start.1 = (bf16[16,64,3,512]{3,1,2,0:T(8,128)(2,1)S(1)}, bf16[16,64,3,512]{3,1,2,0:T(8,128)(2,1)}, u32[]{:S(2)}) copy-start(bf16[16,64,3,512]{3,1,2,0:T(8,128)(2,1)} %param.10) | copy-start | bytes 9437188
  21.9 2.0 %collective-permute-start.7 = (bf16[3,64,1024]{2,1,0:T(8,128)(2,1)S(1)}, bf16[3,64,1024]{2,1,0:T(8,128)(2,1)S(1)}, u32[]{:S(2)}, u32[]{:S(2)}) collective-permute-start(bf16[3,64,1024]{2,1,0:T(8,128)(2,1)S(1)} %get-tuple-element.88.refs_0_), channel_id=1, source_target_pairs={{0,16},{16,0},{32,48},{48,32},{64,80},{80,64},{96,112},{112,96},{1... | collective-permute-start | bytes 1179656 | tf_op jit(solution)/shard_map/ppermute | solution.py:50
  22.0 6.9 %collective-permute-start.8 = (bf16[3,64,1024]{2,1,0:T(8,128)(2,1)S(1)}, bf16[3,64,1024]{2,1,0:T(8,128)(2,1)S(1)}, u32[]{:S(2)}, u32[]{:S(2)}) collective-permute-start(bf16[3,64,1024]{2,1,0:T(8,128)(2,1)S(1)} %get-tuple-element.88.refs_0_), channel_id=1, source_target_pairs={{0,32},{16,112},{32,64},{48,16},{64,96},{80,48},{96,0},{112,80},{1... | collective-permute-start | bytes 1179656 | tf_op jit(solution)/shard_map/ppermute | solution.py:62
  24.5 5.6 %collective-permute-start.9 = (bf16[64,1024]{1,0:T(8,128)(2,1)S(1)}, bf16[64,1024]{1,0:T(8,128)(2,1)S(1)}, u32[]{:S(2)}, u32[]{:S(2)}) collective-permute-start(bf16[64,1024]{1,0:T(8,128)(2,1)S(1)} %join_features.1.refs_0_), channel_id=1, source_target_pairs={{0,1},{1,2},{2,3},{3,0},{4,5},{5,6},{6,7},{7,4},{8,9},{9,10},{10,1... | collective-permute-start | bytes 393224 | tf_op jit(solution)/shard_map/ppermute | solution.py:106
  26.0 10.1 %collective-permute-start.10 = (bf16[3,64,1024]{2,1,0:T(8,128)(2,1)S(1)}, bf16[3,64,1024]{2,1,0:T(8,128)(2,1)S(1)}, u32[]{:S(2)}, u32[]{:S(2)}) collective-permute-start(bf16[3,64,1024]{2,1,0:T(8,128)(2,1)S(1)} %collective-permute-done.7.refs_1_), channel_id=1, source_target_pairs={{0,32},{16,112},{32,64},{48,16},{64,96},{80,48},{96,0},{112,80},{1... | collective-permute-start | bytes 1179656 | tf_op jit(solution)/shard_map/ppermute | solution.py:62
  30.1 9.5 %collective-permute-start.13 = (bf16[3,64,1024]{2,1,0:T(8,128)(2,1)S(1)}, bf16[3,64,1024]{2,1,0:T(8,128)(2,1)S(1)}, u32[]{:S(2)}, u32[]{:S(2)}) collective-permute-start(bf16[3,64,1024]{2,1,0:T(8,128)(2,1)S(1)} %collective-permute-done.8.refs_2_), channel_id=1, source_target_pairs={{0,32},{16,112},{32,64},{48,16},{64,96},{80,48},{96,0},{112,80},{1... | collective-permute-start | bytes 1179656 | tf_op jit(solution)/shard_map/ppermute | solution.py:62
  32.1 5.7 %collective-permute-start.14 = (bf16[64,1024]{1,0:T(8,128)(2,1)S(1)}, bf16[64,1024]{1,0:T(8,128)(2,1)S(1)}, u32[]{:S(2)}, u32[]{:S(2)}) collective-permute-start(bf16[64,1024]{1,0:T(8,128)(2,1)S(1)} %join_features.1.refs_0_), channel_id=1, source_target_pairs={{0,2},{1,3},{2,0},{3,1},{4,6},{5,7},{6,4},{7,5},{8,10},{9,11},{10,... | collective-permute-start | bytes 393224 | tf_op jit(solution)/shard_map/ppermute | solution.py:106
  35.1 4.4 %collective-permute-start.15 = (bf16[64,1024]{1,0:T(8,128)(2,1)S(1)}, bf16[64,1024]{1,0:T(8,128)(2,1)S(1)}, u32[]{:S(2)}, u32[]{:S(2)}) collective-permute-start(bf16[64,1024]{1,0:T(8,128)(2,1)S(1)} %join_features.1.refs_0_), channel_id=1, source_target_pairs={{0,3},{1,0},{2,1},{3,2},{4,7},{5,4},{6,5},{7,6},{8,11},{9,8},{10,9... | collective-permute-start | bytes 393224 | tf_op jit(solution)/shard_map/ppermute | solution.py:106
  35.9 4.9 %collective-permute-start.11 = (bf16[3,64,1024]{2,1,0:T(8,128)(2,1)S(1)}, bf16[3,64,1024]{2,1,0:T(8,128)(2,1)S(1)}, u32[]{:S(2)}, u32[]{:S(2)}) collective-permute-start(bf16[3,64,1024]{2,1,0:T(8,128)(2,1)S(1)} %collective-permute-done.8.refs_2_), channel_id=1, source_target_pairs={{0,16},{16,0},{32,48},{48,32},{64,80},{80,64},{96,112},{112,96},{1... | collective-permute-start | bytes 1179656 | tf_op jit(solution)/shard_map/ppermute | solution.py:50
  36.1 4.7 %collective-permute-start.12 = (bf16[3,64,1024]{2,1,0:T(8,128)(2,1)S(1)}, bf16[3,64,1024]{2,1,0:T(8,128)(2,1)S(1)}, u32[]{:S(2)}, u32[]{:S(2)}) collective-permute-start(bf16[3,64,1024]{2,1,0:T(8,128)(2,1)S(1)} %collective-permute-done.10.refs_3_), channel_id=1, source_target_pairs={{0,16},{16,0},{32,48},{48,32},{64,80},{80,64},{96,112},{112,96},{1... | collective-permute-start | bytes 1179656 | tf_op jit(solution)/shard_map/ppermute | solution.py:50
  39.5 2.6 %collective-permute-start.16 = (bf16[3,64,1024]{2,1,0:T(8,128)(2,1)S(1)}, bf16[3,64,1024]{2,1,0:T(8,128)(2,1)S(1)}, u32[]{:S(2)}, u32[]{:S(2)}) collective-permute-start(bf16[3,64,1024]{2,1,0:T(8,128)(2,1)S(1)} %collective-permute-done.13.refs_2_), channel_id=1, source_target_pairs={{0,16},{16,0},{32,48},{48,32},{64,80},{80,64},{96,112},{112,96},{1... | collective-permute-start | bytes 1179656 | tf_op jit(solution)/shard_map/ppermute | solution.py:50
  45.3 10.3 %collective-permute-start.17 = (bf16[4,64,1024]{2,1,0:T(8,128)(2,1)S(1)}, bf16[4,64,1024]{2,1,0:T(8,128)(2,1)S(1)}, u32[]{:S(2)}, u32[]{:S(2)}) collective-permute-start(bf16[4,64,1024]{2,1,0:T(8,128)(2,1)S(1)} %get-tuple-element.107), channel_id=1, source_target_pairs={{0,4},{1,5},{2,6},{3,7},{4,8},{5,9},{6,10},{7,11},{8,12},{9,13},{1... | collective-permute-start | bytes 1572872 | tf_op jit(solution)/shard_map/ppermute | solution.py:106
  46.7 15.9 %collective-permute-start.18 = (bf16[4,64,1024]{2,1,0:T(8,128)(2,1)S(1)}, bf16[4,64,1024]{2,1,0:T(8,128)(2,1)S(1)}, u32[]{:S(2)}, u32[]{:S(2)}) collective-permute-start(bf16[4,64,1024]{2,1,0:T(8,128)(2,1)S(1)} %get-tuple-element.108), channel_id=1, source_target_pairs={{0,8},{1,9},{2,10},{3,11},{4,12},{5,13},{6,14},{7,15},{8,0},{9,1},... | collective-permute-start | bytes 1572872 | tf_op jit(solution)/shard_map/ppermute | solution.py:106
  50.0 12.6 %collective-permute-start.19 = (bf16[4,64,1024]{2,1,0:T(8,128)(2,1)S(1)}, bf16[4,64,1024]{2,1,0:T(8,128)(2,1)S(1)}, u32[]{:S(2)}, u32[]{:S(2)}) collective-permute-start(bf16[4,64,1024]{2,1,0:T(8,128)(2,1)S(1)} %get-tuple-element.109), channel_id=1, source_target_pairs={{0,12},{1,13},{2,14},{3,15},{4,0},{5,1},{6,2},{7,3},{8,4},{9,5},{1... | collective-permute-start | bytes 1572872 | tf_op jit(solution)/shard_map/ppermute | solution.py:106
  51.3 15.6 %collective-permute-start.20 = (bf16[4,64,1024]{2,1,0:T(8,128)(2,1)S(1)}, bf16[4,64,1024]{2,1,0:T(8,128)(2,1)S(1)}, u32[]{:S(2)}, u32[]{:S(2)}) collective-permute-start(bf16[4,64,1024]{2,1,0:T(8,128)(2,1)S(1)} %stack_features.1.refs_0_), channel_id=1, source_target_pairs={{0,4},{1,5},{2,6},{3,7},{4,8},{5,9},{6,10},{7,11},{8,12},{9,13},{1... | collective-permute-start | bytes 1572872 | tf_op jit(solution)/shard_map/ppermute | solution.py:106
  52.1 15.5 %collective-permute-start.21 = (bf16[4,64,1024]{2,1,0:T(8,128)(2,1)S(1)}, bf16[4,64,1024]{2,1,0:T(8,128)(2,1)S(1)}, u32[]{:S(2)}, u32[]{:S(2)}) collective-permute-start(bf16[4,64,1024]{2,1,0:T(8,128)(2,1)S(1)} %stack_features.1.refs_0_), channel_id=1, source_target_pairs={{0,12},{1,13},{2,14},{3,15},{4,0},{5,1},{6,2},{7,3},{8,4},{9,5},{1... | collective-permute-start | bytes 1572872 | tf_op jit(solution)/shard_map/ppermute | solution.py:106
  54.1 18.5 %copy-start = (bf16[1536,1024]{1,0:T(8,128)(2,1)S(1)}, bf16[1536,1024]{1,0:T(8,128)(2,1)}, u32[]{:S(2)}) copy-start(bf16[1536,1024]{1,0:T(8,128)(2,1)} %get-tuple-element.118.whole) | copy-start | bytes 9437188
  55.7 25.7 %collective-permute-start.28 = (bf16[4,64,1024]{2,1,0:T(8,128)(2,1)S(1)}, bf16[4,64,1024]{2,1,0:T(8,128)(2,1)S(1)}, u32[]{:S(2)}, u32[]{:S(2)}) collective-permute-start(bf16[4,64,1024]{2,1,0:T(8,128)(2,1)S(1)} %stack_features.1.refs_0_), channel_id=1, source_target_pairs={{0,8},{1,9},{2,10},{3,11},{4,12},{5,13},{6,14},{7,15},{8,0},{9,1},... | collective-permute-start | bytes 1572872 | tf_op jit(solution)/shard_map/ppermute | solution.py:106
  67.6 9.1 %collective-permute-start.22 = (bf16[64,1024]{1,0:T(8,128)(2,1)S(1)}, bf16[64,1024]{1,0:T(8,128)(2,1)S(1)}, u32[]{:S(2)}, u32[]{:S(2)}) collective-permute-start(bf16[64,1024]{1,0:T(8,128)(2,1)S(1)} %get-tuple-element.115), channel_id=1, source_target_pairs={{0,1},{1,2},{2,3},{3,0},{4,5},{5,6},{6,7},{7,4},{8,9},{9,10},{10,1... | collective-permute-start | bytes 393224 | tf_op jit(solution)/shard_map/ppermute | solution.py:106
  68.9 7.8 %collective-permute-start.23 = (bf16[64,1024]{1,0:T(8,128)(2,1)S(1)}, bf16[64,1024]{1,0:T(8,128)(2,1)S(1)}, u32[]{:S(2)}, u32[]{:S(2)}) collective-permute-start(bf16[64,1024]{1,0:T(8,128)(2,1)S(1)} %get-tuple-element.116), channel_id=1, source_target_pairs={{0,2},{1,3},{2,0},{3,1},{4,6},{5,7},{6,4},{7,5},{8,10},{9,11},{10,... | collective-permute-start | bytes 393224 | tf_op jit(solution)/shard_map/ppermute | solution.py:106
  71.5 5.2 %collective-permute-start.24 = (bf16[64,1024]{1,0:T(8,128)(2,1)S(1)}, bf16[64,1024]{1,0:T(8,128)(2,1)S(1)}, u32[]{:S(2)}, u32[]{:S(2)}) collective-permute-start(bf16[64,1024]{1,0:T(8,128)(2,1)S(1)} %get-tuple-element.117), channel_id=1, source_target_pairs={{0,3},{1,0},{2,1},{3,2},{4,7},{5,4},{6,5},{7,6},{8,11},{9,8},{10,9... | collective-permute-start | bytes 393224 | tf_op jit(solution)/shard_map/ppermute | solution.py:106
  77.4 6.3 %collective-permute-start.25 = (bf16[2,64,128]{2,1,0:T(8,128)(2,1)S(1)}, bf16[2,64,128]{2,1,0:T(8,128)(2,1)S(1)}, u32[]{:S(2)}, u32[]{:S(2)}) collective-permute-start(bf16[2,64,128]{2,1,0:T(8,128)(2,1)S(1)} %get-tuple-element.127), channel_id=1, source_target_pairs={{0,32},{16,48},{32,64},{48,80},{64,96},{80,112},{96,0},{112,16},{1... | collective-permute-start | bytes 98312 | tf_op jit(solution)/shard_map/ppermute | solution.py:46
  78.2 5.6 %collective-permute-start.26 = (bf16[2,64,128]{2,1,0:T(8,128)(2,1)S(1)}, bf16[2,64,128]{2,1,0:T(8,128)(2,1)S(1)}, u32[]{:S(2)}, u32[]{:S(2)}) collective-permute-start(bf16[2,64,128]{2,1,0:T(8,128)(2,1)S(1)} %get-tuple-element.128), channel_id=1, source_target_pairs={{0,64},{16,80},{32,96},{48,112},{64,0},{80,16},{96,32},{112,48},{1... | collective-permute-start | bytes 98312 | tf_op jit(solution)/shard_map/ppermute | solution.py:46
  81.2 3.1 %collective-permute-start.27 = (bf16[2,64,128]{2,1,0:T(8,128)(2,1)S(1)}, bf16[2,64,128]{2,1,0:T(8,128)(2,1)S(1)}, u32[]{:S(2)}, u32[]{:S(2)}) collective-permute-start(bf16[2,64,128]{2,1,0:T(8,128)(2,1)S(1)} %get-tuple-element.129), channel_id=1, source_target_pairs={{0,96},{16,112},{32,0},{48,16},{64,32},{80,48},{96,64},{112,80},{1... | collective-permute-start | bytes 98312 | tf_op jit(solution)/shard_map/ppermute | solution.py:46
  84.3 3.2 %collective-permute-start.29 = (bf16[64,128]{1,0:T(8,128)(2,1)S(1)}, bf16[64,128]{1,0:T(8,128)(2,1)S(1)}, u32[]{:S(2)}, u32[]{:S(2)}) collective-permute-start(bf16[64,128]{1,0:T(8,128)(2,1)S(1)} %get-tuple-element.151), channel_id=1, source_target_pairs={{0,16},{16,0},{32,48},{48,32},{64,80},{80,64},{96,112},{112,96},{1... | collective-permute-start | bytes 49160 | tf_op jit(solution)/shard_map/ppermute | solution.py:50
  86.7 1.2 %collective-permute-start.30 = (bf16[64,128]{1,0:T(8,128)(2,1)S(1)}, bf16[64,128]{1,0:T(8,128)(2,1)S(1)}, u32[]{:S(2)}, u32[]{:S(2)}) collective-permute-start(bf16[64,128]{1,0:T(8,128)(2,1)S(1)} %get-tuple-element.149), channel_id=1, source_target_pairs={{0,16},{16,0},{32,48},{48,32},{64,80},{80,64},{96,112},{112,96},{1... | collective-permute-start | bytes 49160 | tf_op jit(solution)/shard_map/ppermute | solution.py:50
  86.8 1.3 %collective-permute-start.31 = (bf16[64,128]{1,0:T(8,128)(2,1)S(1)}, bf16[64,128]{1,0:T(8,128)(2,1)S(1)}, u32[]{:S(2)}, u32[]{:S(2)}) collective-permute-start(bf16[64,128]{1,0:T(8,128)(2,1)S(1)} %get-tuple-element.147), channel_id=1, source_target_pairs={{0,16},{16,0},{32,48},{48,32},{64,80},{80,64},{96,112},{112,96},{1... | collective-permute-start | bytes 49160 | tf_op jit(solution)/shard_map/ppermute | solution.py:50
  87.2 1.2 %collective-permute-start.32 = (bf16[64,128]{1,0:T(8,128)(2,1)S(1)}, bf16[64,128]{1,0:T(8,128)(2,1)S(1)}, u32[]{:S(2)}, u32[]{:S(2)}) collective-permute-start(bf16[64,128]{1,0:T(8,128)(2,1)S(1)} %get-tuple-element.145), channel_id=1, source_target_pairs={{0,16},{16,0},{32,48},{48,32},{64,80},{80,64},{96,112},{112,96},{1... | collective-permute-start | bytes 49160 | tf_op jit(solution)/shard_map/ppermute | solution.py:50

commit v6 on v5

--- a/solution.py
+++ b/solution.py
@@ -406,49 +406,42 @@
     )(me, *parts)
 
 
-def sum_kernel(me, *refs):
-    parts, outs, whole = refs[:N_RING], refs[N_RING:-1], refs[-1]
+def sum_kernel(*refs):
+    parts, out = refs[:N_RING], refs[N_RING]
     total = parts[0][...].astype(F32)
     for i in range(1, N_RING):
         total = total + parts[i][...].astype(F32)
-    whole[...] = total.astype(BF16)
-    tokens = outs[0].shape[-1]
-    for ahead in range(N_X):
-        for other in range(2):
-            outs[ahead][other] = whole[:, part_of(target(me[0], ahead, other), tokens)]
-
-
-def sum_parts(me, parts):
+    tokens = out.shape[-1]
+    for i in range(N_CTX):
+        out[i] = total[:, i * tokens : (i + 1) * tokens].astype(BF16)
+
+
+def sum_parts(parts):
     rows, n = parts[0].shape
     return pl.pallas_call(
         sum_kernel,
-        out_shape=[like(2, rows, n // N_CTX)] * N_X,
-        in_specs=[SCALAR] + [ON_CHIP] * N_RING,
-        out_specs=[ON_CHIP] * N_X,
-        scratch_shapes=[pltpu.VMEM((rows, n), BF16)],
+        out_shape=like(N_CTX, rows, n // N_CTX),
+        in_specs=[ON_CHIP] * N_RING,
+        out_specs=ON_CHIP,
         compiler_params=vmem(6),
         name="sum_parts",
-    )(me, *parts)
-
-
-def finish_kernel(me, *refs):
-    pieces, out, whole = refs[:N_CTX], refs[N_CTX], refs[N_CTX + 1]
-    sub = pieces[0].shape[0]
-    for p in range(N_CTX):
-        whole[part_of(source(me[0], p), sub), :] = pieces[p][...]
-    out[...] = whole[...].T
-
-
-def finish(me, pieces):
-    rows, tokens = pieces[0].shape
+    )(*parts)
+
+
+def finish_kernel(pieces, out):
+    n_ctx, sub, tokens = pieces.shape
+    out[...] = pieces[...].reshape(n_ctx * sub, tokens).T
+
+
+def finish(pieces):
+    n_ctx, sub, tokens = pieces.shape
     return pl.pallas_call(
         finish_kernel,
-        out_shape=like(tokens, rows * N_CTX),
-        in_specs=[SCALAR] + [ON_CHIP] * N_CTX,
-        scratch_shapes=[pltpu.VMEM((rows * N_CTX, tokens), BF16)],
+        out_shape=like(tokens, n_ctx * sub),
+        in_specs=[ON_CHIP],
         compiler_params=vmem(6),
         name="finish",
-    )(me, *pieces)
+    )(pieces)
 
 
 def tie(a, b):
@@ -488,11 +481,10 @@
     feats = [feats, feats1, shift_ring(feats, 2, first=True), feats3]
     grad_w = weight_grad(me, far_whole, [feats[s] for s in (0, 1, 3)], (0, 1, 3))
     parts, grad_w = tie(parts, grad_w)
-    ready = sum_parts(me, parts)
-    along = [ready[0]] + [shift_x(ready[s], s) for s in (1, 2, 3)]
+    moved = lax.all_to_all(sum_parts(parts), "ctx", 0, 0)
     grad_w = weight_grad(me, far_whole, [feats[2]], (2,), grad_w)
-    along, grad_w = tie(along, grad_w)
-    grad_features = finish(me, [a[0] for a in along] + [swap_core(a[1]) for a in along])
+    moved, grad_w = tie(moved, grad_w)
+    grad_features = finish(moved)
     return grad_features, grad_w.transpose(0, 2, 1, 3), grad_taps.reshape(filter_taps.shape)
 
 

time: 89.8 us -> 89.9 us (level)
  starting transfers between devices: 47.6 us -> 45.5 us
  Pallas kernels: 24.8 us -> 26.2 us
    all_to_all x0 -> x1, starting transfers between devices: none -> 5.38 us  [per_device(): moved = lax.all_to_all(sum_parts(parts), 'ctx', 0, 0)]
    ppermute x6 -> x3, starting transfers between devices: 9.64 us -> 5.71 us  [shift_x(): lax.ppermute(a, 'ctx', [(i, (i + 2 * steps) % N_CTX) for i in range(N_CTX)])]
    ppermute x12 -> x8, starting transfers between devices: 7.27 us -> 4.28 us  [swap_core(): return lax.ppermute(a, 'ctx', [(i, i ^ 1) for i in range(N_CTX)])]
    all_to_all x0 -> x1, waiting for transfers between devices: none -> 2.37 us  [per_device(): moved = lax.all_to_all(sum_parts(parts), 'ctx', 0, 0)]
    ppermute x12 -> x8, waiting for transfers between devices: 2.99 us -> 1.89 us  [swap_core(): return lax.ppermute(a, 'ctx', [(i, i ^ 1) for i in range(N_CTX)])]
    pallas_call x2, Pallas kernels: 6.54 us -> 7.59 us  [weight_grad(): pl.pallas_call(functools.partial(weight_kernel, steps), out_shape=pltpu.H...]
    ppermute x6 -> x3, waiting for transfers between devices: 2.42 us -> 1.96 us  [shift_x(): lax.ppermute(a, 'ctx', [(i, (i + 2 * steps) % N_CTX) for i in range(N_CTX)])]
  transfers between devices with their start and end apart: 33 -> 27, of which waited for: 18 -> 13; matrix products, arithmetic and copies ran while one was open for 0% -> 0% of each run, Pallas kernels for 16% -> 18%
where the time goes in v6:
time: 89.9 us; the launch traced here: 89.6 us
  starting transfers between devices  45.5 us (51%)
  Pallas kernels  26.2 us (29%)
  waiting for transfers between devices  16.1 us (18%)
  local copies, waits for them, and re-layouts  0.96 us (1%)
    ppermute x12, starting transfers between devices, shift_ring(): return lax.ppermute(a, ('ctx', 'tp'), pairs)  24.7 us
    ppermute x12, waiting for transfers between devices, shift_ring(): return lax.ppermute(a, ('ctx', 'tp'), pairs)  8.49 us
    pallas_call x2, Pallas kernels, weight_grad(): pl.pallas_call(functools.partial(weight_kernel, steps), out_shape=pltpu.H...  7.59 us
    ppermute x3, starting transfers between devices, shift_x(): lax.ppermute(a, 'ctx', [(i, (i + 2 * steps) % N_CTX) for i in range(N_CTX)])  5.71 us
    ppermute x3, starting transfers between devices, spin(): return lax.ppermute(a, 'ctx', pairs)  5.42 us
    all_to_all x1, starting transfers between devices, per_device(): moved = lax.all_to_all(sum_parts(parts), 'ctx', 0, 0)  5.38 us
    pallas_call x2, Pallas kernels, value_part(): pl.pallas_call(functools.partial(value_kernel, steps, which), out_shape=s...  4.73 us
    ppermute x8, starting transfers between devices, swap_core(): return lax.ppermute(a, 'ctx', [(i, i ^ 1) for i in range(N_CTX)])  4.28 us
  transfers between devices with their start and end apart: 27, of which 13 were waited for; matrix products, arithmetic and copies ran while one was open for 0% of the time, Pallas kernels for 18%

profile of v6, /device:TPU:1, one launch (start us, length us, event | category | flops | bytes accessed | tf_op | source)
XLA Modules:
  0.0 89.6 jit_solution(7469425738318350854)
XLA Ops:
  0.6 0.1 pad_add_fusion.me
  0.7 2.0 %prepare.1 = (bf16[2,5,64,128]{3,2,1,0:T(8,128)(2,1)S(1)}, bf16[2,5,64,128]{3,2,1,0:T(8,128)(2,1)S(1)}, bf16[2,5,64,128]{3,2,1,0:T(8,128)(2,1)S(1)}, bf16[2,5,64,128]{3,2,1,0:T(8,128)(2,1)S(1)}) custom-call(s32[2]{0:T(128)S(1)} %pad_add_fusion.me, bf16[128,512]{1,0:T(8,128)(2,1)} %refs_0_.2, bf16[128,512]{1,0:T(8,128)(2,1)} %refs_1_.2, ...), custom_call_target="tpu_custom_call" | custom-call | tf_op jit(solution)/shard_map/prepare/pallas_call | solution.py:134
  2.7 2.1 %collective-permute-start = (bf16[2,5,64,128]{3,2,1,0:T(8,128)(2,1)S(1)}, bf16[2,5,64,128]{3,2,1,0:T(8,128)(2,1)S(1)}, u32[]{:S(2)}, u32[]{:S(2)}) collective-permute-start(bf16[2,5,64,128]{3,2,1,0:T(8,128)(2,1)S(1)} %get-tuple-element.64), channel_id=1, source_target_pairs={{0,32},{16,48},{32,64},{48,80},{64,96},{80,112},{96,0},{112,16},{1... | collective-permute-start | bytes 491528 | tf_op jit(solution)/shard_map/ppermute | solution.py:46
  4.8 2.5 %collective-permute-start.1 = (bf16[2,5,64,128]{3,2,1,0:T(8,128)(2,1)S(1)}, bf16[2,5,64,128]{3,2,1,0:T(8,128)(2,1)S(1)}, u32[]{:S(2)}, u32[]{:S(2)}) collective-permute-start(bf16[2,5,64,128]{3,2,1,0:T(8,128)(2,1)S(1)} %get-tuple-element.65), channel_id=1, source_target_pairs={{0,64},{16,80},{32,96},{48,112},{64,0},{80,16},{96,32},{112,48},{1... | collective-permute-start | bytes 491528 | tf_op jit(solution)/shard_map/ppermute | solution.py:46
  7.3 1.2 %collective-permute-start.2 = (bf16[2,5,64,128]{3,2,1,0:T(8,128)(2,1)S(1)}, bf16[2,5,64,128]{3,2,1,0:T(8,128)(2,1)S(1)}, u32[]{:S(2)}, u32[]{:S(2)}) collective-permute-start(bf16[2,5,64,128]{3,2,1,0:T(8,128)(2,1)S(1)} %get-tuple-element.66), channel_id=1, source_target_pairs={{0,96},{16,112},{32,0},{48,16},{64,32},{80,48},{96,64},{112,80},{1... | collective-permute-start | bytes 491528 | tf_op jit(solution)/shard_map/ppermute | solution.py:46
  8.4 0.9 %copy-done.2 = bf16[1,64,1024]{2,1,0:T(8,128)(2,1)S(1)} copy-done((bf16[1,64,1024]{2,1,0:T(8,128)(2,1)S(1)}, bf16[1,64,1024]{2,1,0:T(8,128)(2,1)}, u32[]{:S(2)}) %copy-start.2) | copy-done | bytes 131096
  9.3 3.1 %taps_spectrum.1 = (bf16[1024,1024]{1,0:T(8,128)(2,1)S(1)}, bf16[1024,1024]{1,0:T(8,128)(2,1)S(1)}, f32[64,1024]{1,0:T(8,128)S(1)}, f32[64,1024]{1,0:T(8,128)S(1)}, f32[64,1]{1,0:T(8,128)S(1)}) custom-call(bf16[1024,1024]{1,0:T(8,128)(2,1)} %constant.13.clone.refs_0_, bf16[1024,1024]{1,0:T(8,128)(2,1)} %constant.14.clone.refs_1_, bf16[64,1024]{1,0:T(8,128)(2,1)S(1)} %bitcast.24), custom_call_target="tpu_custom_call" | custom-call | flops 536870912 | bytes 8388608 | tf_op jit(solution)/shard_map/taps_spectrum/pallas_call | solution.py:224
  12.4 0.0 collective-permute-done
  12.4 2.0 %collective-permute-done.1 = bf16[2,5,64,128]{3,2,1,0:T(8,128)(2,1)S(1)} collective-permute-done((bf16[2,5,64,128]{3,2,1,0:T(8,128)(2,1)S(1)}, bf16[2,5,64,128]{3,2,1,0:T(8,128)(2,1)S(1)}, u32[]{:S(2)}, u32[]{:S(2)}) %collective-permute-start.1) | collective-permute-done | bytes 163872 | tf_op jit(solution)/shard_map/ppermute | solution.py:46
  14.4 1.6 %collective-permute-start.3 = (bf16[5,64,128]{2,1,0:T(8,128)(2,1)S(1)}, bf16[5,64,128]{2,1,0:T(8,128)(2,1)S(1)}, u32[]{:S(2)}, u32[]{:S(2)}) collective-permute-start(bf16[5,64,128]{2,1,0:T(8,128)(2,1)S(1)} %get-tuple-element.129), channel_id=1, source_target_pairs={{0,16},{16,0},{32,48},{48,32},{64,80},{80,64},{96,112},{112,96},{1... | collective-permute-start | bytes 245768 | tf_op jit(solution)/shard_map/ppermute | solution.py:50
  16.0 0.1 collective-permute-start.4
  16.1 0.6 collective-permute-start.5
  16.7 0.1 collective-permute-start.6
  16.8 0.1 collective-permute-done.3.refs_4_
  16.9 0.4 collective-permute-done.4.refs_5_
  17.4 0.2 collective-permute-done.5.refs_6_
  17.6 0.4 collective-permute-done.6.refs_7_
  18.1 3.8 %convolutions.1 = (bf16[3,64,1024]{2,1,0:T(8,128)(2,1)S(1)}, bf16[64,1024]{1,0:T(8,128)(2,1)}) custom-call(s32[2]{0:T(128)S(1)} %pad_add_fusion.me, bf16[5,64,128]{2,1,0:T(8,128)(2,1)S(1)} %get-tuple-element.83.refs_0_, bf16[5,64,128]{2,1,0:T(8,128)(2,1)S(1)} %get-tuple-element.84.refs_1_, bf16[5,64,128]{2,1,0:T(8,128)(2,1)S(1)} %get-tuple-element.85.refs_2_, ...), custom_call_target="tpu_custom_call" | custom-call | flops 2147483648 | bytes 8388608 | tf_op jit(solution)/shard_map/convolutions/pallas_call | solution.py:263
  21.9 0.1 collective-permute-start.7
  22.0 1.9 %collective-permute-start.8 = (bf16[3,64,1024]{2,1,0:T(8,128)(2,1)S(1)}, bf16[3,64,1024]{2,1,0:T(8,128)(2,1)S(1)}, u32[]{:S(2)}, u32[]{:S(2)}) collective-permute-start(bf16[3,64,1024]{2,1,0:T(8,128)(2,1)S(1)} %get-tuple-element.81.refs_0_), channel_id=1, source_target_pairs={{0,32},{16,112},{32,64},{48,16},{64,96},{80,48},{96,0},{112,80},{1... | collective-permute-start | bytes 1179656 | tf_op jit(solution)/shard_map/ppermute | solution.py:62
  23.9 0.6 join_features.1.refs_0_
  24.5 1.5 %collective-permute-start.9 = (bf16[64,1024]{1,0:T(8,128)(2,1)S(1)}, bf16[64,1024]{1,0:T(8,128)(2,1)S(1)}, u32[]{:S(2)}, u32[]{:S(2)}) collective-permute-start(bf16[64,1024]{1,0:T(8,128)(2,1)S(1)} %join_features.1.refs_0_), channel_id=1, source_target_pairs={{0,1},{1,2},{2,3},{3,0},{4,5},{5,6},{6,7},{7,4},{8,9},{9,10},{10,1... | collective-permute-start | bytes 393224 | tf_op jit(solution)/shard_map/ppermute | solution.py:106
  26.0 1.6 %collective-permute-start.10 = (bf16[3,64,1024]{2,1,0:T(8,128)(2,1)S(1)}, bf16[3,64,1024]{2,1,0:T(8,128)(2,1)S(1)}, u32[]{:S(2)}, u32[]{:S(2)}) collective-permute-start(bf16[3,64,1024]{2,1,0:T(8,128)(2,1)S(1)} %collective-permute-done.7.refs_1_), channel_id=1, source_target_pairs={{0,32},{16,112},{32,64},{48,16},{64,96},{80,48},{96,0},{112,80},{1... | collective-permute-start | bytes 1179656 | tf_op jit(solution)/shard_map/ppermute | solution.py:62
  27.6 1.4 %collective-permute-done.8.refs_2_ = bf16[3,64,1024]{2,1,0:T(8,128)(2,1)S(1)} collective-permute-done((bf16[3,64,1024]{2,1,0:T(8,128)(2,1)S(1)}, bf16[3,64,1024]{2,1,0:T(8,128)(2,1)S(1)}, u32[]{:S(2)}, u32[]{:S(2)}) %collective-permute-start.8) | collective-permute-done | bytes 393248 | tf_op jit(solution)/shard_map/ppermute | solution.py:62
  29.0 1.1 %collective-permute-done.9.refs_1_ = bf16[64,1024]{1,0:T(8,128)(2,1)S(1)} collective-permute-done((bf16[64,1024]{1,0:T(8,128)(2,1)S(1)}, bf16[64,1024]{1,0:T(8,128)(2,1)S(1)}, u32[]{:S(2)}, u32[]{:S(2)}) %collective-permute-start.9) | collective-permute-done | bytes 131104 | tf_op jit(solution)/shard_map/ppermute | solution.py:106
  30.1 2.0 %collective-permute-start.13 = (bf16[3,64,1024]{2,1,0:T(8,128)(2,1)S(1)}, bf16[3,64,1024]{2,1,0:T(8,128)(2,1)S(1)}, u32[]{:S(2)}, u32[]{:S(2)}) collective-permute-start(bf16[3,64,1024]{2,1,0:T(8,128)(2,1)S(1)} %collective-permute-done.8.refs_2_), channel_id=1, source_target_pairs={{0,32},{16,112},{32,64},{48,16},{64,96},{80,48},{96,0},{112,80},{1... | collective-permute-start | bytes 1179656 | tf_op jit(solution)/shard_map/ppermute | solution.py:62
  32.1 3.0 %collective-permute-start.14 = (bf16[64,1024]{1,0:T(8,128)(2,1)S(1)}, bf16[64,1024]{1,0:T(8,128)(2,1)S(1)}, u32[]{:S(2)}, u32[]{:S(2)}) collective-permute-start(bf16[64,1024]{1,0:T(8,128)(2,1)S(1)} %join_features.1.refs_0_), channel_id=1, source_target_pairs={{0,2},{1,3},{2,0},{3,1},{4,6},{5,7},{6,4},{7,5},{8,10},{9,11},{10,... | collective-permute-start | bytes 393224 | tf_op jit(solution)/shard_map/ppermute | solution.py:106
  35.1 0.8 collective-permute-start.15
  35.9 0.3 collective-permute-start.11
  36.1 0.0 collective-permute-done.10.refs_3_
  36.1 0.3 collective-permute-start.12
  36.4 1.4 %collective-permute-done.14.refs_2_ = bf16[64,1024]{1,0:T(8,128)(2,1)S(1)} collective-permute-done((bf16[64,1024]{1,0:T(8,128)(2,1)S(1)}, bf16[64,1024]{1,0:T(8,128)(2,1)S(1)}, u32[]{:S(2)}, u32[]{:S(2)}) %collective-permute-start.14) | collective-permute-done | bytes 131104 | tf_op jit(solution)/shard_map/ppermute | solution.py:106
  37.7 1.8 %collective-permute-done.15.refs_3_ = bf16[64,1024]{1,0:T(8,128)(2,1)S(1)} collective-permute-done((bf16[64,1024]{1,0:T(8,128)(2,1)S(1)}, bf16[64,1024]{1,0:T(8,128)(2,1)S(1)}, u32[]{:S(2)}, u32[]{:S(2)}) %collective-permute-start.15) | collective-permute-done | bytes 131104 | tf_op jit(solution)/shard_map/ppermute | solution.py:106
  39.5 0.0 collective-permute-done.13.refs_2_
  39.5 1.2 %collective-permute-start.16 = (bf16[3,64,1024]{2,1,0:T(8,128)(2,1)S(1)}, bf16[3,64,1024]{2,1,0:T(8,128)(2,1)S(1)}, u32[]{:S(2)}, u32[]{:S(2)}) collective-permute-start(bf16[3,64,1024]{2,1,0:T(8,128)(2,1)S(1)} %collective-permute-done.13.refs_2_), channel_id=1, source_target_pairs={{0,16},{16,0},{32,48},{48,32},{64,80},{80,64},{96,112},{112,96},{1... | collective-permute-start | bytes 1179656 | tf_op jit(solution)/shard_map/ppermute | solution.py:50
  40.8 0.0 collective-permute-done.12.refs_5_
  40.8 0.7 assemble.1.refs_1_
  41.5 0.6 collective-permute-done.16.refs_3_
  42.1 3.2 %value_part.2 = (bf16[4,64,1024]{2,1,0:T(8,128)(2,1)S(1)}, bf16[4,64,1024]{2,1,0:T(8,128)(2,1)S(1)}, bf16[4,64,1024]{2,1,0:T(8,128)(2,1)S(1)}, bf16[1536,1024]{1,0:T(8,128)(2,1)S(1)}, bf16[1536,1024]{1,0:T(8,128)(2,1)}) custom-call(s32[2]{0:T(128)S(1)} %pad_add_fusion.me, bf16[16,3,64,512]{3,2,1,0:T(8,128)(2,1)S(1)} %bitcast.22, ...), custom_call_target="tpu_custom_call", output_to_operand_aliasing={{3}: (2, {})} | custom-call | flops 2415919104 | bytes 2097152 | tf_op jit(solution)/shard_map/value_part/pallas_call | solution.py:332
  45.3 1.3 %collective-permute-start.17 = (bf16[4,64,1024]{2,1,0:T(8,128)(2,1)S(1)}, bf16[4,64,1024]{2,1,0:T(8,128)(2,1)S(1)}, u32[]{:S(2)}, u32[]{:S(2)}) collective-permute-start(bf16[4,64,1024]{2,1,0:T(8,128)(2,1)S(1)} %get-tuple-element.100), channel_id=1, source_target_pairs={{0,4},{1,5},{2,6},{3,7},{4,8},{5,9},{6,10},{7,11},{8,12},{9,13},{1... | collective-permute-start | bytes 1572872 | tf_op jit(solution)/shard_map/ppermute | solution.py:106
  46.7 3.3 %collective-permute-start.18 = (bf16[4,64,1024]{2,1,0:T(8,128)(2,1)S(1)}, bf16[4,64,1024]{2,1,0:T(8,128)(2,1)S(1)}, u32[]{:S(2)}, u32[]{:S(2)}) collective-permute-start(bf16[4,64,1024]{2,1,0:T(8,128)(2,1)S(1)} %get-tuple-element.101), channel_id=1, source_target_pairs={{0,8},{1,9},{2,10},{3,11},{4,12},{5,13},{6,14},{7,15},{8,0},{9,1},... | collective-permute-start | bytes 1572872 | tf_op jit(solution)/shard_map/ppermute | solution.py:106
  50.0 0.7 collective-permute-start.19
  50.7 1.4 %stack_features.1.refs_0_ = bf16[4,64,1024]{2,1,0:T(8,128)(2,1)} custom-call(s32[2]{0:T(128)S(1)} %pad_add_fusion.me, bf16[64,1024]{1,0:T(8,128)(2,1)S(1)} %join_features.1.refs_0_, bf16[64,1024]{1,0:T(8,128)(2,1)S(1)} %collective-permute-done.9.refs_1_, bf16[64,1024]{1,0:T(8,128)(2,1)S(1)} %collective-permute-done.14.refs_2_, ...), custom_call_target="tpu_custom_call" | custom-call | tf_op jit(solution)/shard_map/stack_features/pallas_call | solution.py:175
  52.1 0.7 collective-permute-start.20
  52.8 1.9 %collective-permute-start.21 = (bf16[4,64,1024]{2,1,0:T(8,128)(2,1)}, bf16[4,64,1024]{2,1,0:T(8,128)(2,1)S(1)}, u32[]{:S(2)}, u32[]{:S(2)}) collective-permute-start(bf16[4,64,1024]{2,1,0:T(8,128)(2,1)} %stack_features.1.refs_0_), channel_id=1, source_target_pairs={{0,12},{1,13},{2,14},{3,15},{4,0},{5,1},{6,2},{7,3},{8,4},{9,5},{1... | collective-permute-start | bytes 1572872 | tf_op jit(solution)/shard_map/ppermute | solution.py:106
  54.8 1.5 %value_part.3.refs_0_ = bf16[4,64,1024]{2,1,0:T(8,128)(2,1)S(1)} custom-call(s32[2]{0:T(128)S(1)} %pad_add_fusion.me, bf16[16,3,64,512]{3,2,1,0:T(8,128)(2,1)S(1)} %bitcast.23, bf16[1536,1024]{1,0:T(8,128)(2,1)S(1)} %get-tuple-element.94.refs_1_), custom_call_target="tpu_custom_call" | custom-call | flops 805306368 | bytes 2097152 | tf_op jit(solution)/shard_map/value_part/pallas_call | solution.py:332
  56.3 0.0 collective-permute-done.17.refs_1_
  56.3 6.3 %collective-permute-start.25 = (bf16[4,64,1024]{2,1,0:T(8,128)(2,1)}, bf16[4,64,1024]{2,1,0:T(8,128)(2,1)}, u32[]{:S(2)}, u32[]{:S(2)}) collective-permute-start(bf16[4,64,1024]{2,1,0:T(8,128)(2,1)} %stack_features.1.refs_0_), channel_id=1, source_target_pairs={{0,8},{1,9},{2,10},{3,11},{4,12},{5,13},{6,14},{7,15},{8,0},{9,1},... | collective-permute-start | bytes 1572872 | tf_op jit(solution)/shard_map/ppermute | solution.py:106
  62.6 0.0 collective-permute-done.18.refs_2_
  62.6 0.0 collective-permute-done.19.refs_3_
  62.6 0.8 first_sum.1
  63.4 4.0 %collective-permute-done.20.refs_1_ = bf16[4,64,1024]{2,1,0:T(8,128)(2,1)S(1)} collective-permute-done((bf16[4,64,1024]{2,1,0:T(8,128)(2,1)}, bf16[4,64,1024]{2,1,0:T(8,128)(2,1)S(1)}, u32[]{:S(2)}, u32[]{:S(2)}) %collective-permute-start.20) | collective-permute-done | bytes 524320 | tf_op jit(solution)/shard_map/ppermute | solution.py:106
  67.5 0.1 collective-permute-done.21.refs_2_
  67.6 1.3 %collective-permute-start.22 = (bf16[64,1024]{1,0:T(8,128)(2,1)S(1)}, bf16[64,1024]{1,0:T(8,128)(2,1)S(1)}, u32[]{:S(2)}, u32[]{:S(2)}) collective-permute-start(bf16[64,1024]{1,0:T(8,128)(2,1)S(1)} %get-tuple-element.108), channel_id=1, source_target_pairs={{0,1},{1,2},{2,3},{3,0},{4,5},{5,6},{6,7},{7,4},{8,9},{9,10},{10,1... | collective-permute-start | bytes 393224 | tf_op jit(solution)/shard_map/ppermute | solution.py:106
  68.9 2.7 %collective-permute-start.23 = (bf16[64,1024]{1,0:T(8,128)(2,1)S(1)}, bf16[64,1024]{1,0:T(8,128)(2,1)S(1)}, u32[]{:S(2)}, u32[]{:S(2)}) collective-permute-start(bf16[64,1024]{1,0:T(8,128)(2,1)S(1)} %get-tuple-element.109), channel_id=1, source_target_pairs={{0,2},{1,3},{2,0},{3,1},{4,6},{5,7},{6,4},{7,5},{8,10},{9,11},{10,... | collective-permute-start | bytes 393224 | tf_op jit(solution)/shard_map/ppermute | solution.py:106
  71.6 1.1 %collective-permute-start.24 = (bf16[64,1024]{1,0:T(8,128)(2,1)S(1)}, bf16[64,1024]{1,0:T(8,128)(2,1)S(1)}, u32[]{:S(2)}, u32[]{:S(2)}) collective-permute-start(bf16[64,1024]{1,0:T(8,128)(2,1)S(1)} %get-tuple-element.110), channel_id=1, source_target_pairs={{0,3},{1,0},{2,1},{3,2},{4,7},{5,4},{6,5},{7,6},{8,11},{9,8},{10,9... | collective-permute-start | bytes 393224 | tf_op jit(solution)/shard_map/ppermute | solution.py:106
  72.7 4.7 %weight_grad.2.refs_1_ = bf16[16,3,64,512]{3,2,1,0:T(8,128)(2,1)} custom-call(s32[2]{0:T(128)S(1)} %pad_add_fusion.me, bf16[1536,1024]{1,0:T(8,128)(2,1)S(1)} %copy-done, bf16[4,64,1024]{2,1,0:T(8,128)(2,1)} %stack_features.1.refs_0_, bf16[4,64,1024]{2,1,0:T(8,128)(2,1)S(1)} %collective-permute-done.20.refs_1_, ...), custom_call_target="tpu_custom_call" | custom-call | flops 2415919104 | bytes 2097152 | tf_op jit(solution)/shard_map/weight_grad/pallas_call | solution.py:369
  77.4 0.0 collective-permute-done.22.refs_1_
  77.4 0.0 collective-permute-done.24.refs_3_
  77.4 0.7 sum_parts.1
  78.1 5.4 %all-to-all-start = ((bf16[8,64,128]{2,1,0:T(8,128)(2,1)}), bf16[8,64,128]{2,1,0:T(8,128)(2,1)S(1)}, u32[]{:S(2)}, u32[]{:S(2)}) async-start(bf16[8,64,128]{2,1,0:T(8,128)(2,1)} %sum_parts.1), calls=%async_computation | async-start | bytes 262144 | tf_op jit(solution)/shard_map/all_to_all | solution.py:484
  83.5 2.9 %weight_grad.3 = bf16[16,3,64,512]{3,2,1,0:T(8,128)(2,1)} custom-call(s32[2]{0:T(128)S(1)} %pad_add_fusion.me, bf16[1536,1024]{1,0:T(8,128)(2,1)S(1)} %copy-done, bf16[4,64,1024]{2,1,0:T(8,128)(2,1)} %collective-permute-done.25.refs_0_, bf16[16,3,64,512]{3,2,1,0:T(8,128)(2,1)} %weight_grad.2.refs_1_), custom_call_target="tpu_custom_call", output_to_operand_aliasing={{}: (3, {})} | custom-call | flops 805306368 | bytes 2097152 | tf_op jit(solution)/shard_map/weight_grad/pallas_call | solution.py:369
  86.5 2.4 %all-to-all-done.pieces = bf16[8,64,128]{2,1,0:T(8,128)(2,1)S(1)} async-done(((bf16[8,64,128]{2,1,0:T(8,128)(2,1)}), bf16[8,64,128]{2,1,0:T(8,128)(2,1)S(1)}, u32[]{:S(2)}, u32[]{:S(2)}) %all-to-all-start) | async-done | bytes 131104 | tf_op jit(solution)/shard_map/all_to_all | solution.py:484
  88.8 0.7 finish.1
  (14 shorter events, 0.1 us)
Async XLA Ops:
  2.7 9.7 %collective-permute-start = (bf16[2,5,64,128]{3,2,1,0:T(8,128)(2,1)S(1)}, bf16[2,5,64,128]{3,2,1,0:T(8,128)(2,1)S(1)}, u32[]{:S(2)}, u32[]{:S(2)}) collective-permute-start(bf16[2,5,64,128]{3,2,1,0:T(8,128)(2,1)S(1)} %get-tuple-element.64), channel_id=1, source_target_pairs={{0,32},{16,48},{32,64},{48,80},{64,96},{80,112},{96,0},{112,16},{1... | collective-permute-start | bytes 491528 | tf_op jit(solution)/shard_map/ppermute | solution.py:46
  4.8 9.6 %collective-permute-start.1 = (bf16[2,5,64,128]{3,2,1,0:T(8,128)(2,1)S(1)}, bf16[2,5,64,128]{3,2,1,0:T(8,128)(2,1)S(1)}, u32[]{:S(2)}, u32[]{:S(2)}) collective-permute-start(bf16[2,5,64,128]{3,2,1,0:T(8,128)(2,1)S(1)} %get-tuple-element.65), channel_id=1, source_target_pairs={{0,64},{16,80},{32,96},{48,112},{64,0},{80,16},{96,32},{112,48},{1... | collective-permute-start | bytes 491528 | tf_op jit(solution)/shard_map/ppermute | solution.py:46
  7.3 7.1 %collective-permute-start.2 = (bf16[2,5,64,128]{3,2,1,0:T(8,128)(2,1)S(1)}, bf16[2,5,64,128]{3,2,1,0:T(8,128)(2,1)S(1)}, u32[]{:S(2)}, u32[]{:S(2)}) collective-permute-start(bf16[2,5,64,128]{3,2,1,0:T(8,128)(2,1)S(1)} %get-tuple-element.66), channel_id=1, source_target_pairs={{0,96},{16,112},{32,0},{48,16},{64,32},{80,48},{96,64},{112,80},{1... | collective-permute-start | bytes 491528 | tf_op jit(solution)/shard_map/ppermute | solution.py:46
  8.4 0.9 %copy-start.2 = (bf16[1,64,1024]{2,1,0:T(8,128)(2,1)S(1)}, bf16[1,64,1024]{2,1,0:T(8,128)(2,1)}, u32[]{:S(2)}) copy-start(bf16[1,64,1024]{2,1,0:T(8,128)(2,1)} %param.11) | copy-start | bytes 393220
  14.4 2.5 %collective-permute-start.3 = (bf16[5,64,128]{2,1,0:T(8,128)(2,1)S(1)}, bf16[5,64,128]{2,1,0:T(8,128)(2,1)S(1)}, u32[]{:S(2)}, u32[]{:S(2)}) collective-permute-start(bf16[5,64,128]{2,1,0:T(8,128)(2,1)S(1)} %get-tuple-element.129), channel_id=1, source_target_pairs={{0,16},{16,0},{32,48},{48,32},{64,80},{80,64},{96,112},{112,96},{1... | collective-permute-start | bytes 245768 | tf_op jit(solution)/shard_map/ppermute | solution.py:50
  16.0 1.4 %collective-permute-start.4 = (bf16[5,64,128]{2,1,0:T(8,128)(2,1)S(1)}, bf16[5,64,128]{2,1,0:T(8,128)(2,1)S(1)}, u32[]{:S(2)}, u32[]{:S(2)}) collective-permute-start(bf16[5,64,128]{2,1,0:T(8,128)(2,1)S(1)} %get-tuple-element.127), channel_id=1, source_target_pairs={{0,16},{16,0},{32,48},{48,32},{64,80},{80,64},{96,112},{112,96},{1... | collective-permute-start | bytes 245768 | tf_op jit(solution)/shard_map/ppermute | solution.py:50
  16.1 1.5 %collective-permute-start.5 = (bf16[5,64,128]{2,1,0:T(8,128)(2,1)S(1)}, bf16[5,64,128]{2,1,0:T(8,128)(2,1)S(1)}, u32[]{:S(2)}, u32[]{:S(2)}) collective-permute-start(bf16[5,64,128]{2,1,0:T(8,128)(2,1)S(1)} %get-tuple-element.125), channel_id=1, source_target_pairs={{0,16},{16,0},{32,48},{48,32},{64,80},{80,64},{96,112},{112,96},{1... | collective-permute-start | bytes 245768 | tf_op jit(solution)/shard_map/ppermute | solution.py:50
  16.7 1.4 %collective-permute-start.6 = (bf16[5,64,128]{2,1,0:T(8,128)(2,1)S(1)}, bf16[5,64,128]{2,1,0:T(8,128)(2,1)S(1)}, u32[]{:S(2)}, u32[]{:S(2)}) collective-permute-start(bf16[5,64,128]{2,1,0:T(8,128)(2,1)S(1)} %get-tuple-element.123), channel_id=1, source_target_pairs={{0,16},{16,0},{32,48},{48,32},{64,80},{80,64},{96,112},{112,96},{1... | collective-permute-start | bytes 245768 | tf_op jit(solution)/shard_map/ppermute | solution.py:50
  21.9 20.2 %copy-start.1 = (bf16[16,64,3,512]{3,1,2,0:T(8,128)(2,1)S(1)}, bf16[16,64,3,512]{3,1,2,0:T(8,128)(2,1)}, u32[]{:S(2)}) copy-start(bf16[16,64,3,512]{3,1,2,0:T(8,128)(2,1)} %param.10) | copy-start | bytes 9437188
  21.9 2.0 %collective-permute-start.7 = (bf16[3,64,1024]{2,1,0:T(8,128)(2,1)S(1)}, bf16[3,64,1024]{2,1,0:T(8,128)(2,1)S(1)}, u32[]{:S(2)}, u32[]{:S(2)}) collective-permute-start(bf16[3,64,1024]{2,1,0:T(8,128)(2,1)S(1)} %get-tuple-element.81.refs_0_), channel_id=1, source_target_pairs={{0,16},{16,0},{32,48},{48,32},{64,80},{80,64},{96,112},{112,96},{1... | collective-permute-start | bytes 1179656 | tf_op jit(solution)/shard_map/ppermute | solution.py:50
  22.0 6.9 %collective-permute-start.8 = (bf16[3,64,1024]{2,1,0:T(8,128)(2,1)S(1)}, bf16[3,64,1024]{2,1,0:T(8,128)(2,1)S(1)}, u32[]{:S(2)}, u32[]{:S(2)}) collective-permute-start(bf16[3,64,1024]{2,1,0:T(8,128)(2,1)S(1)} %get-tuple-element.81.refs_0_), channel_id=1, source_target_pairs={{0,32},{16,112},{32,64},{48,16},{64,96},{80,48},{96,0},{112,80},{1... | collective-permute-start | bytes 1179656 | tf_op jit(solution)/shard_map/ppermute | solution.py:62
  24.5 5.6 %collective-permute-start.9 = (bf16[64,1024]{1,0:T(8,128)(2,1)S(1)}, bf16[64,1024]{1,0:T(8,128)(2,1)S(1)}, u32[]{:S(2)}, u32[]{:S(2)}) collective-permute-start(bf16[64,1024]{1,0:T(8,128)(2,1)S(1)} %join_features.1.refs_0_), channel_id=1, source_target_pairs={{0,1},{1,2},{2,3},{3,0},{4,5},{5,6},{6,7},{7,4},{8,9},{9,10},{10,1... | collective-permute-start | bytes 393224 | tf_op jit(solution)/shard_map/ppermute | solution.py:106
  26.0 10.1 %collective-permute-start.10 = (bf16[3,64,1024]{2,1,0:T(8,128)(2,1)S(1)}, bf16[3,64,1024]{2,1,0:T(8,128)(2,1)S(1)}, u32[]{:S(2)}, u32[]{:S(2)}) collective-permute-start(bf16[3,64,1024]{2,1,0:T(8,128)(2,1)S(1)} %collective-permute-done.7.refs_1_), channel_id=1, source_target_pairs={{0,32},{16,112},{32,64},{48,16},{64,96},{80,48},{96,0},{112,80},{1... | collective-permute-start | bytes 1179656 | tf_op jit(solution)/shard_map/ppermute | solution.py:62
  30.1 9.5 %collective-permute-start.13 = (bf16[3,64,1024]{2,1,0:T(8,128)(2,1)S(1)}, bf16[3,64,1024]{2,1,0:T(8,128)(2,1)S(1)}, u32[]{:S(2)}, u32[]{:S(2)}) collective-permute-start(bf16[3,64,1024]{2,1,0:T(8,128)(2,1)S(1)} %collective-permute-done.8.refs_2_), channel_id=1, source_target_pairs={{0,32},{16,112},{32,64},{48,16},{64,96},{80,48},{96,0},{112,80},{1... | collective-permute-start | bytes 1179656 | tf_op jit(solution)/shard_map/ppermute | solution.py:62
  32.1 5.7 %collective-permute-start.14 = (bf16[64,1024]{1,0:T(8,128)(2,1)S(1)}, bf16[64,1024]{1,0:T(8,128)(2,1)S(1)}, u32[]{:S(2)}, u32[]{:S(2)}) collective-permute-start(bf16[64,1024]{1,0:T(8,128)(2,1)S(1)} %join_features.1.refs_0_), channel_id=1, source_target_pairs={{0,2},{1,3},{2,0},{3,1},{4,6},{5,7},{6,4},{7,5},{8,10},{9,11},{10,... | collective-permute-start | bytes 393224 | tf_op jit(solution)/shard_map/ppermute | solution.py:106
  35.1 4.4 %collective-permute-start.15 = (bf16[64,1024]{1,0:T(8,128)(2,1)S(1)}, bf16[64,1024]{1,0:T(8,128)(2,1)S(1)}, u32[]{:S(2)}, u32[]{:S(2)}) collective-permute-start(bf16[64,1024]{1,0:T(8,128)(2,1)S(1)} %join_features.1.refs_0_), channel_id=1, source_target_pairs={{0,3},{1,0},{2,1},{3,2},{4,7},{5,4},{6,5},{7,6},{8,11},{9,8},{10,9... | collective-permute-start | bytes 393224 | tf_op jit(solution)/shard_map/ppermute | solution.py:106
  35.9 4.9 %collective-permute-start.11 = (bf16[3,64,1024]{2,1,0:T(8,128)(2,1)S(1)}, bf16[3,64,1024]{2,1,0:T(8,128)(2,1)S(1)}, u32[]{:S(2)}, u32[]{:S(2)}) collective-permute-start(bf16[3,64,1024]{2,1,0:T(8,128)(2,1)S(1)} %collective-permute-done.8.refs_2_), channel_id=1, source_target_pairs={{0,16},{16,0},{32,48},{48,32},{64,80},{80,64},{96,112},{112,96},{1... | collective-permute-start | bytes 1179656 | tf_op jit(solution)/shard_map/ppermute | solution.py:50
  36.1 4.7 %collective-permute-start.12 = (bf16[3,64,1024]{2,1,0:T(8,128)(2,1)S(1)}, bf16[3,64,1024]{2,1,0:T(8,128)(2,1)S(1)}, u32[]{:S(2)}, u32[]{:S(2)}) collective-permute-start(bf16[3,64,1024]{2,1,0:T(8,128)(2,1)S(1)} %collective-permute-done.10.refs_3_), channel_id=1, source_target_pairs={{0,16},{16,0},{32,48},{48,32},{64,80},{80,64},{96,112},{112,96},{1... | collective-permute-start | bytes 1179656 | tf_op jit(solution)/shard_map/ppermute | solution.py:50
  39.5 2.6 %collective-permute-start.16 = (bf16[3,64,1024]{2,1,0:T(8,128)(2,1)S(1)}, bf16[3,64,1024]{2,1,0:T(8,128)(2,1)S(1)}, u32[]{:S(2)}, u32[]{:S(2)}) collective-permute-start(bf16[3,64,1024]{2,1,0:T(8,128)(2,1)S(1)} %collective-permute-done.13.refs_2_), channel_id=1, source_target_pairs={{0,16},{16,0},{32,48},{48,32},{64,80},{80,64},{96,112},{112,96},{1... | collective-permute-start | bytes 1179656 | tf_op jit(solution)/shard_map/ppermute | solution.py:50
  45.3 11.0 %collective-permute-start.17 = (bf16[4,64,1024]{2,1,0:T(8,128)(2,1)S(1)}, bf16[4,64,1024]{2,1,0:T(8,128)(2,1)S(1)}, u32[]{:S(2)}, u32[]{:S(2)}) collective-permute-start(bf16[4,64,1024]{2,1,0:T(8,128)(2,1)S(1)} %get-tuple-element.100), channel_id=1, source_target_pairs={{0,4},{1,5},{2,6},{3,7},{4,8},{5,9},{6,10},{7,11},{8,12},{9,13},{1... | collective-permute-start | bytes 1572872 | tf_op jit(solution)/shard_map/ppermute | solution.py:106
  46.7 15.9 %collective-permute-start.18 = (bf16[4,64,1024]{2,1,0:T(8,128)(2,1)S(1)}, bf16[4,64,1024]{2,1,0:T(8,128)(2,1)S(1)}, u32[]{:S(2)}, u32[]{:S(2)}) collective-permute-start(bf16[4,64,1024]{2,1,0:T(8,128)(2,1)S(1)} %get-tuple-element.101), channel_id=1, source_target_pairs={{0,8},{1,9},{2,10},{3,11},{4,12},{5,13},{6,14},{7,15},{8,0},{9,1},... | collective-permute-start | bytes 1572872 | tf_op jit(solution)/shard_map/ppermute | solution.py:106
  50.0 12.6 %collective-permute-start.19 = (bf16[4,64,1024]{2,1,0:T(8,128)(2,1)S(1)}, bf16[4,64,1024]{2,1,0:T(8,128)(2,1)S(1)}, u32[]{:S(2)}, u32[]{:S(2)}) collective-permute-start(bf16[4,64,1024]{2,1,0:T(8,128)(2,1)S(1)} %get-tuple-element.102), channel_id=1, source_target_pairs={{0,12},{1,13},{2,14},{3,15},{4,0},{5,1},{6,2},{7,3},{8,4},{9,5},{1... | collective-permute-start | bytes 1572872 | tf_op jit(solution)/shard_map/ppermute | solution.py:106
  52.1 15.4 %collective-permute-start.20 = (bf16[4,64,1024]{2,1,0:T(8,128)(2,1)}, bf16[4,64,1024]{2,1,0:T(8,128)(2,1)S(1)}, u32[]{:S(2)}, u32[]{:S(2)}) collective-permute-start(bf16[4,64,1024]{2,1,0:T(8,128)(2,1)} %stack_features.1.refs_0_), channel_id=1, source_target_pairs={{0,4},{1,5},{2,6},{3,7},{4,8},{5,9},{6,10},{7,11},{8,12},{9,13},{1... | collective-permute-start | bytes 1572872 | tf_op jit(solution)/shard_map/ppermute | solution.py:106
  52.8 14.8 %collective-permute-start.21 = (bf16[4,64,1024]{2,1,0:T(8,128)(2,1)}, bf16[4,64,1024]{2,1,0:T(8,128)(2,1)S(1)}, u32[]{:S(2)}, u32[]{:S(2)}) collective-permute-start(bf16[4,64,1024]{2,1,0:T(8,128)(2,1)} %stack_features.1.refs_0_), channel_id=1, source_target_pairs={{0,12},{1,13},{2,14},{3,15},{4,0},{5,1},{6,2},{7,3},{8,4},{9,5},{1... | collective-permute-start | bytes 1572872 | tf_op jit(solution)/shard_map/ppermute | solution.py:106
  54.8 17.9 %copy-start = (bf16[1536,1024]{1,0:T(8,128)(2,1)S(1)}, bf16[1536,1024]{1,0:T(8,128)(2,1)}, u32[]{:S(2)}) copy-start(bf16[1536,1024]{1,0:T(8,128)(2,1)} %get-tuple-element.111.whole) | copy-start | bytes 9437188
  56.3 27.2 %collective-permute-start.25 = (bf16[4,64,1024]{2,1,0:T(8,128)(2,1)}, bf16[4,64,1024]{2,1,0:T(8,128)(2,1)}, u32[]{:S(2)}, u32[]{:S(2)}) collective-permute-start(bf16[4,64,1024]{2,1,0:T(8,128)(2,1)} %stack_features.1.refs_0_), channel_id=1, source_target_pairs={{0,8},{1,9},{2,10},{3,11},{4,12},{5,13},{6,14},{7,15},{8,0},{9,1},... | collective-permute-start | bytes 1572872 | tf_op jit(solution)/shard_map/ppermute | solution.py:106
  67.6 9.8 %collective-permute-start.22 = (bf16[64,1024]{1,0:T(8,128)(2,1)S(1)}, bf16[64,1024]{1,0:T(8,128)(2,1)S(1)}, u32[]{:S(2)}, u32[]{:S(2)}) collective-permute-start(bf16[64,1024]{1,0:T(8,128)(2,1)S(1)} %get-tuple-element.108), channel_id=1, source_target_pairs={{0,1},{1,2},{2,3},{3,0},{4,5},{5,6},{6,7},{7,4},{8,9},{9,10},{10,1... | collective-permute-start | bytes 393224 | tf_op jit(solution)/shard_map/ppermute | solution.py:106
  68.9 8.5 %collective-permute-start.23 = (bf16[64,1024]{1,0:T(8,128)(2,1)S(1)}, bf16[64,1024]{1,0:T(8,128)(2,1)S(1)}, u32[]{:S(2)}, u32[]{:S(2)}) collective-permute-start(bf16[64,1024]{1,0:T(8,128)(2,1)S(1)} %get-tuple-element.109), channel_id=1, source_target_pairs={{0,2},{1,3},{2,0},{3,1},{4,6},{5,7},{6,4},{7,5},{8,10},{9,11},{10,... | collective-permute-start | bytes 393224 | tf_op jit(solution)/shard_map/ppermute | solution.py:106
  71.6 5.8 %collective-permute-start.24 = (bf16[64,1024]{1,0:T(8,128)(2,1)S(1)}, bf16[64,1024]{1,0:T(8,128)(2,1)S(1)}, u32[]{:S(2)}, u32[]{:S(2)}) collective-permute-start(bf16[64,1024]{1,0:T(8,128)(2,1)S(1)} %get-tuple-element.110), channel_id=1, source_target_pairs={{0,3},{1,0},{2,1},{3,2},{4,7},{5,4},{6,5},{7,6},{8,11},{9,8},{10,9... | collective-permute-start | bytes 393224 | tf_op jit(solution)/shard_map/ppermute | solution.py:106
  78.1 10.7 %all-to-all-start = ((bf16[8,64,128]{2,1,0:T(8,128)(2,1)}), bf16[8,64,128]{2,1,0:T(8,128)(2,1)S(1)}, u32[]{:S(2)}, u32[]{:S(2)}) async-start(bf16[8,64,128]{2,1,0:T(8,128)(2,1)} %sum_parts.1), calls=%async_computation | async-start | bytes 262144 | tf_op jit(solution)/shard_map/all_to_all | solution.py:484
